TPU v7x, 128 devices: a whole 4x4x4 slice. The times are simulated.
128 devices in a mesh: wav: 8 (over x, core), slab: 16 (over y, z).
Axes of the slice: x: 4, y: 4, z: 4, core: 2. Of those that a mesh axis runs over, the one named last changes fastest.
Arguments:
- amplitude: float32 [512, 512], P('slab'), may hold values from 0.5 to 1
- seg_map: int32 [512, 512], P('slab'), may hold values from 0 to 797, as said below
- seg_table: int32 [798, 3], replicated, may hold values from -3000 to 3000
- focal_mask: float32 [1024, 1024], P('slab'), may hold values from 0.1 to 1
- trace_row: int32 [128, 128], P('slab', 'wav'), may hold values from 0 to 31
- trace_col: int32 [128, 128], P('slab', 'wav'), may hold values from 0 to 31
- block_count: int32 [128, 128], P('slab', 'wav'), may hold values from 1 to 16
- crosstalk: float32 [5, 5], replicated, may hold values from 0.01 to 0.1
Outputs:
- detector: float32 [4096, 4096], P('slab', 'wav')
Inputs may be any that keep to these rules, and one draw needn't show every extreme that they name: seg_map is constant over aligned square blocks of 16 samples.
All inputs are finite; a program needn't handle non-finite values.
Results may differ from a plain program's by a relative error of at most 0.0001.
Values sent between devices are 32-bit elements; how exact they have to be, the bound alone decides.
No kernel may reach another device: no remote copies, remote signals or barrier semaphores. Data moves between devices by JAX's collectives and lax.ppermute only.
A program may use at most 128 MiB of HBM per device.

v0:
```python
import functools

import jax
import jax.numpy as jnp
import numpy as np
from jax import lax
from jax.experimental import pallas as pl
from jax.experimental.pallas import tpu as pltpu
from jax.sharding import PartitionSpec as P

F32, BF16, I32 = jnp.float32, jnp.bfloat16, jnp.int32

NP, NF, NL, DPIX, SEGMENTS, WAVES = 512, 1024, 128, 32, 798, 16
NWAV, NSLAB = 8, 16
ROWS = NP // NSLAB
FROWS = NF // NSLAB
UROWS = FROWS + 16
GROUP = 128
MROWS = GROUP + 8
HALF, FHALF = NP // 2, NF // 2

SIN = (6.283185302511503, -41.34170040531721, 81.6051313857832, -76.70301535364747,
       42.02592698447418, -14.899846663536497, 3.2381375046186873)
COS = (0.9999999890590228, -19.73920449945383, 64.93911745989081, -85.45013953079767,
       60.167630950263465, -25.967599245923743, 6.52865815775625)


def scalars():
    wavelength = 1000.0 + np.arange(WAVES, dtype=np.float64)
    whole = 250.0 / wavelength
    short = np.round(whole * 2.0**14) / 2.0**14
    return np.stack([short, whole - short, whole / 1024.0, 1.0 / wavelength], 1).astype(np.float32).reshape(-1)


def iota(shape, dim):
    return lax.broadcasted_iota(I32, shape, dim)


def dot(a, b):
    return jnp.dot(a, b, preferred_element_type=F32)


def split2(x):
    high = x.astype(BF16)
    return high, (x - high.astype(F32)).astype(BF16)


def split3(x):
    high = x.astype(BF16)
    rest = x - high.astype(F32)
    middle = rest.astype(BF16)
    return high, middle, (rest - middle.astype(F32)).astype(BF16)


def sincos(turns):
    t = turns - jnp.round(turns)
    z = t * t
    s, c = SIN[-1], COS[-1]
    for a, b in zip(SIN[-2::-1], COS[-2::-1]):
        s, c = s * z + a, c * z + b
    return s * t, c


def reversal(n):
    return (iota((n, n), 0) + iota((n, n), 1) == n - 1).astype(BF16)


def prepare_kernel(info, amp, seg, tab, out):
    lower = info[2] >= 2
    rows, cols = iota((ROWS, ROWS), 0), iota((ROWS, ROWS), 1)
    order = (cols == jnp.where(lower, ROWS - 1 - rows, rows)).astype(BF16)
    rev = reversal(HALF)
    left = right = 0.0
    for part in split3(amp[...]):
        left = left + dot(order, part[:, :HALF])
        right = right + dot(order, dot(part[:, HALF:], rev).astype(BF16))
    out[0:ROWS, 0:HALF] = left
    out[0:ROWS, HALF:NP] = right
    lane = iota((NP, 128), 1)
    pick = ((iota((NP, 128), 0) == 16 * (lane & 31)) & (lane < 96)).astype(BF16)

    def ids(first):
        return sum(dot(part, pick) for part in split2(seg[first:first + 8, :].astype(F32)))[0:1]

    upper_ids, lower_ids = ids(0), ids(16)
    lane = iota((SEGMENTS, 128), 1)
    table = tab[...].astype(F32)
    wide = jnp.where(lane < 32, table[:, 0:1], jnp.where(lane < 64, table[:, 1:2], table[:, 2:3]))
    which = iota((SEGMENTS, 128), 0).astype(F32)
    out[ROWS:ROWS + 8, :] = jnp.zeros((8, NP), F32)
    for k in range(2):
        own = jnp.where(lower, lower_ids if k == 0 else upper_ids, upper_ids if k == 0 else lower_ids)
        out[ROWS + k:ROWS + k + 1, 0:128] = jnp.sum(jnp.where(which == own, wide, 0.0), axis=0, keepdims=True)


def merge_kernel(info, p0, p1, p2, p3, out):
    z = info[3]
    out[:, GROUP:MROWS, :] = jnp.zeros((4, 8, 128), F32)
    for k, piece in enumerate((p0, p1, p2, p3)):
        source = lax.rem(z - k + 4, 4)
        place = jnp.where(info[2] >= 2, 3 - source, source)
        for at in range(4):

            @pl.when(place == at)
            def _(at=at, piece=piece):
                for t in range(4):
                    lanes = slice(128 * t, 128 * t + 128)
                    for b in range(2):
                        out[t, pl.ds(2 * at + b, 16, stride=8), :] = piece[16 * b:16 * b + 16, lanes]
                out[0, GROUP + 2 * at:GROUP + 2 * at + 2, :] = piece[ROWS:ROWS + 2, 0:128]


def angle(m, n, finfo, w):
    product = m * n
    a, b = (product >> 10).astype(F32), (product & 1023).astype(F32)
    t = a * finfo[4 * w]
    t = t - jnp.round(t)
    return sincos(t + a * finfo[4 * w + 1] + b * finfo[4 * w + 2])


def table_kernel(info, finfo, mask, above, below, utab, vtab, weight, smat):
    s, sign, g0 = info[1], info[4].astype(F32), info[5]
    for m in range(2):
        w = 2 * info[0] + m
        for p in range(2):
            g = g0 if p == 0 else 1 - g0
            u = 64 * s - 8 + iota((UROWS, GROUP), 0)
            rho = iota((UROWS, GROUP), 1)
            i = 128 * g + 16 * (rho & 7) + (rho >> 3)
            sin, cos = angle(2 * u + 1 - NF, 2 * i + 1 - NP, finfo, w)
            for at, part in ((0, cos), (GROUP, sin * sign)):
                high, low = split2(part)
                utab[p, m, 0:UROWS, at:at + GROUP] = high
                utab[p, m, UROWS:2 * UROWS, at:at + GROUP] = low

        def chunk(c, carry, m=m, w=w):
            j0 = pl.multiple_of(16 * c, 16)
            j = j0 + iota((16, FHALF), 0)
            v = iota((16, FHALF), 1)
            sin, cos = angle(2 * v + 1 - NF, 2 * j + 1 - NP, finfo, w)
            for q, part in ((0, cos), (1, sin)):
                high, low = split2(part)
                vtab[m, q, 0, pl.ds(j0, 16), :] = high
                vtab[m, q, 1, pl.ds(j0, 16), :] = low
            return carry

        lax.fori_loop(0, HALF // 16, chunk, 0)
    u = 64 * s - 8 + iota((UROWS, FHALF), 0)
    v = iota((UROWS, FHALF), 1)
    down, across = (2 * u + 1 - NF).astype(F32) * 0.5, (2 * v + 1 - NF).astype(F32) * 0.5
    fade = 1.0 - jnp.exp((down * down + across * across) * (-1.0 / 1024.0))
    rev = reversal(256)
    full = jnp.concatenate([above[0:8, :], mask[...], below[0:8, :]], axis=0)
    t = full[:, :FHALF] * fade
    weight[:, :FHALF] = t * t * 2.0**-24
    for q in range(2):
        flipped = sum(dot(part, rev) for part in split3(full[:, NF - 256 * (q + 1):NF - 256 * q]))
        t = flipped * fade[:, 256 * q:256 * (q + 1)]
        weight[:, FHALF + 256 * q:FHALF + 256 * (q + 1)] = t * t * 2.0**-24
    row, lane = iota((FHALF, 256), 0), iota((FHALF, 256), 1)
    lens = jnp.where((lane & 31) < 18, 16 * (lane >> 5) - 1 + (lane & 31), -1)
    smat[0:FHALF, :] = (lens == row >> 3).astype(BF16)
    smat[FHALF:NF, :] = (lens == NL - 1 - (row >> 3)).astype(BF16)


def pair_fields(info, finfo, first, second, utab, p, whi, wlo):
    sign = info[4].astype(F32)
    g = info[5] if p == 0 else 1 - info[5]
    coef = jnp.concatenate([first[0, GROUP:MROWS, :], second[0, GROUP:MROWS, :]], axis=0)
    high, low = split2(coef)
    coef = jnp.concatenate([high, low], axis=0)
    row, lane = iota((128, HALF), 0), iota((128, HALF), 1)
    place = iota((16, HALF), 0)
    y = (32 * (8 * g + (place & 7)) + 1 - NP).astype(F32) * (1.0 / 1024.0)
    toward = jnp.where(place < 8, sign, -sign)
    x = (2 * iota((16, HALF), 1) + 1 - NP).astype(F32) * (1.0 / 1024.0)
    paths, steps = [], []
    for side in range(2):
        block = lane >> 4 if side == 0 else 31 - (lane >> 4)
        pqr = []
        for c in range(3):
            both = dot(coef, (row == 32 * c + block).astype(BF16))
            pqr.append(both[0:16] + both[16:32])
        slope = toward * pqr[2]
        paths.append(pqr[0] + (x if side == 0 else -x) * pqr[1] + slope * y)
        steps.append(slope * (1.0 / 512.0))
    fields = []
    for m in range(2):
        inverse = finfo[4 * (2 * info[0] + m) + 3]
        start = [sincos(path * inverse) for path in paths]
        turn = [sincos(step * inverse) for step in steps]
        for lt in range(2):
            at = slice(128 * lt, 128 * lt + 128)

            def four(values, n):
                return [values[side][n][8 * t:8 * t + 8, at] for t in range(2) for side in range(2)]

            step_im, step_re = four(turn, 0), four(turn, 1)

            def rows(r2, carry, lt=lt, step_im=step_im, step_re=step_re):
                re, im = carry
                found = [[] for _ in range(8)]
                for h in range(2):
                    r0 = pl.multiple_of(16 * r2 + 8 * h, 8)
                    qre, qim = [], []
                    for t, ref in enumerate((first, second)):
                        for side in range(2):
                            a = ref[2 * side + lt, pl.ds(r0, 8), :]
                            qre.append(a * re[2 * t + side])
                            qim.append(a * im[2 * t + side])
                    (fl, fr, sl, sr), (gl, gr, hl, hr) = qre, qim
                    a, b, c, d = fl + sl, sl - fl, fr + sr, sr - fr
                    e, f, k, n = gl + hl, gl - hl, gr + hr, gr - hr
                    for q, value in enumerate((a + c, e + k, e - k, c - a, f + n, b + d, b - d, n - f)):
                        found[q].append(value)
                    re, im = (
                        [x * p - y * q for x, y, p, q in zip(re, im, step_re, step_im)],
                        [x * q + y * p for x, y, p, q in zip(re, im, step_re, step_im)],
                    )
                for q, values in enumerate(found):
                    high, low = split2(jnp.concatenate(values, axis=0))
                    r0 = pl.multiple_of(16 * r2 + (GROUP if q >= 4 else 0), 16)
                    c0 = HALF * (q & 3) + 128 * lt
                    whi[pl.ds(r0, 16), c0:c0 + 128] = high
                    wlo[pl.ds(r0, 16), c0:c0 + 128] = low
                return re, im

            lax.fori_loop(0, 8, rows, (four(start, 1), four(start, 0)))
        table = utab[p, m]
        both = dot(table, whi[...])
        fields.append(both[:UROWS] + both[UROWS:] + dot(table[:UROWS], wlo[...]))
    return fields


def first_kernel(info, finfo, first, second, utab, out, whi, wlo):
    for m, field in enumerate(pair_fields(info, finfo, first, second, utab, 0, whi, wlo)):
        out[m] = field


def second_kernel(info, finfo, first, second, utab, before, vtab, weight, smat, trow, tcol, count, above, below, out, whi, wlo):
    fields = pair_fields(info, finfo, first, second, utab, 1, whi, wlo)
    out[...] = jnp.zeros(out.shape, F32)
    for m, field in enumerate(fields):
        field = field + before[m]
        terms = []
        for q in range(2):
            side = jnp.concatenate([field[:, 512 * q:512 * q + 256], field[:, 512 * q + 256:512 * q + 512]], axis=0)
            high, low = split2(side)
            both = dot(jnp.concatenate([high, low], axis=0), vtab[m, q, 0])
            terms.append(both[:2 * UROWS] + both[2 * UROWS:] + dot(high, vtab[m, q, 1]))
        lens = 0.0
        for q, value in enumerate((terms[0] + terms[1], terms[0] - terms[1])):
            re, im = value[:UROWS], value[UROWS:]
            power = (re * re + im * im) * weight[:, FHALF * q:FHALF * (q + 1)]
            summed = jnp.sum(power.reshape(UROWS // 8, 8, FHALF), axis=1)
            for part in split3(summed):
                lens = lens + dot(part, smat[FHALF * q:FHALF * (q + 1), :])
        for d in range(NWAV):
            out[d, 10 * m:10 * m + 10, 0:32] = lens[:, 32 * d:32 * d + 32]
    for c, table in enumerate((trow, tcol, count)):
        own = table[...].astype(F32)
        for d in range(NWAV):
            out[d, 0:8, 32 + 16 * c:48 + 16 * c] = own
    for d in range(NWAV):
        out[d, 8:9, 32:80] = above[8:9, 0:48]
        out[d, 9:10, 32:80] = below[8:9, 0:48]


TILES = 4 * 8 + 2


def order(a):
    return a - 1 if 0 < a < 9 else 8 + a // 9


def detector_kernel(info, kernel, arrived, out, spec, trace, sums, aq, bq, hp):
    w = info[0]
    lane = iota((24, 128), 1)
    prev, own, nxt = arrived[jnp.maximum(w - 1, 0)], arrived[w], arrived[jnp.minimum(w + 1, NWAV - 1)]
    spot = (iota((128, 640), 0) == iota((128, 640), 1) >> 5).astype(BF16)
    rows = arrived[...].reshape(NWAV * 24, 128)
    wide = sum(dot(part, spot) for part in split3(rows))
    for t in range(5):
        spec[t] = wide[:, 128 * t:128 * t + 128]
    tables = []
    for c in range(3):
        tables.append(
            jnp.where(
                lane == 0,
                pltpu.roll(prev, 128 - (47 + 16 * c), 1),
                jnp.where(
                    lane < 17,
                    pltpu.roll(own, 128 - (31 + 16 * c), 1),
                    jnp.where(lane == 17, pltpu.roll(nxt, 128 - (15 + 16 * c), 1), 0.0),
                ),
            )
        )
    trace[...] = dot(jnp.concatenate(tables, axis=0).astype(BF16), spot)
    place = (iota((8, 640), 1) & 31).astype(F32)
    wave = 2.0 * iota((8, 640), 0).astype(F32)
    sums[...] = jnp.zeros(sums.shape, F32)
    for a in range(10):
        at = order(a)
        offset = place - trace[24 + at:25 + at, :]
        count = trace[48 + at:49 + at, :]
        spread = 0.0
        for m in range(2):
            value = jnp.concatenate([spec[t, pl.ds(10 * m + a, NWAV, stride=24), :] for t in range(5)], axis=1)
            along = jnp.exp(-0.5 * jnp.abs(offset - (wave + m)))
            spread = spread + jnp.where(wave + m < count, value, 0.0) * along
        sums[at:at + 1, :] = jnp.sum(spread, axis=0, keepdims=True)
    row = trace[0:16, :] * 0.25
    total = sums[...]
    falling, rising = total * jnp.exp(row), total * jnp.exp(-row)
    for q in range(5):
        aq[q] = pltpu.roll(falling, 640 - (30 + q), 1)[:, 0:512]
        bq[q] = pltpu.roll(rising, 640 - (30 + q), 1)[:, 0:512]
    weights = [[kernel[p, q] + (1.0 if p == q == 2 else 0.0) for q in range(5)] for p in range(5)]
    depth = iota((8, 128), 0).astype(F32) * 0.25

    def cell(a, tiles):
        for lt in range(4):
            at = slice(128 * lt, 128 * lt + 128)
            if isinstance(a, int):
                fall, rise = ([ref[q, order(a):order(a) + 1, at] for q in range(5)] for ref in (aq, bq))
            else:
                fall, rise = ([pltpu.roll(ref[q, 0:8, at], 9 - a, 0)[0:1] for q in range(5)] for ref in (aq, bq))
            for rt in tiles:
                down, up = jnp.exp(-(depth + 2.0 * rt)), jnp.exp(depth + 2.0 * rt)
                raw = [jnp.minimum(down * f, up * r) for f, r in zip(fall, rise)]
                r0 = pl.multiple_of(8 * (4 * a + rt - 3), 8)
                for p in range(5):
                    h = raw[0] * weights[p][0]
                    for q in range(1, 5):
                        h = h + raw[q] * weights[p][q]
                    hp[p, pl.ds(r0, 8), at] = h

    cell(0, (3,))
    cell(9, (0,))

    def middle(a, carry):
        cell(a, range(4))
        return carry

    lax.fori_loop(1, 9, middle, 0)
    for r in range(0, 256, 8):
        out[r:r + 8, :] = sum(hp[p, r + 6 + p:r + 14 + p, :] for p in range(5))


def call(kernel, outs, in_smem, n_in, scratch=()):
    specs = [pl.BlockSpec(memory_space=pltpu.SMEM)] * in_smem
    specs += [pl.BlockSpec(memory_space=pltpu.VMEM)] * (n_in - in_smem)
    single = not isinstance(outs, (list, tuple))
    vmem = pl.BlockSpec(memory_space=pltpu.VMEM)
    return pl.pallas_call(
        kernel,
        out_shape=outs,
        in_specs=specs,
        out_specs=vmem if single else [vmem] * len(outs),
        scratch_shapes=list(scratch),
        compiler_params=pltpu.CompilerParams(vmem_limit_bytes=40 * 2**20),
        name=kernel.__name__,
    )


def shape(*dims, dtype=F32):
    return jax.ShapeDtypeStruct(dims, dtype)


def along_z(k):
    return [(4 * y + z, 4 * y + (z + k) % 4) for y in range(4) for z in range(4)]


def along_y(other):
    return [(4 * y + z, 4 * other[y] + z) for y in range(4) for z in range(4)]


def body(amplitude, seg_map, seg_table, focal_mask, trace_row, trace_col, block_count, crosstalk):
    w, s = lax.axis_index("wav").astype(I32), lax.axis_index("slab").astype(I32)
    y, z = s // 4, s % 4
    info = jnp.stack([w, s, y, z, jnp.where(y < 2, 1, -1), jnp.where((y == 0) | (y == 3), 0, 1), w, w]).astype(I32)
    finfo = jnp.asarray(scalars())

    piece = call(prepare_kernel, shape(ROWS + 8, NP), 1, 4)(info, amplitude, seg_map, seg_table)
    pieces = [piece] + [lax.ppermute(piece, "slab", along_z(k)) for k in (1, 3, 2)]
    pieces = [pieces[0], pieces[1], pieces[3], pieces[2]]
    own = call(merge_kernel, shape(4, MROWS, 128), 1, 5)(info, *pieces)
    partner = lax.ppermute(own, "slab", along_y((3, 2, 1, 0)))
    beside = lax.ppermute(own, "slab", along_y((1, 0, 3, 2)))
    last = lax.ppermute(own, "slab", along_y((2, 3, 0, 1)))

    def edge(row, rows):
        traces = jnp.concatenate([trace_row[row], trace_col[row], block_count[row]]).astype(F32)
        return jnp.concatenate([focal_mask[rows], jnp.pad(traces, (0, NF - 48))[None]], axis=0)

    above = lax.ppermute(edge(7, slice(56, 64)), "slab", [(i, i + 1) for i in range(NSLAB - 1)])
    below = lax.ppermute(edge(0, slice(0, 8)), "slab", [(i + 1, i) for i in range(NSLAB - 1)])

    utab, vtab, weight, smat = call(
        table_kernel,
        [
            shape(2, 2, 2 * UROWS, 256, dtype=BF16),
            shape(2, 2, 2, HALF, FHALF, dtype=BF16),
            shape(UROWS, NF),
            shape(NF, 256, dtype=BF16),
        ],
        2,
        5,
    )(info, finfo, focal_mask, above, below)
    scratch = [pltpu.VMEM((256, 1024), BF16), pltpu.VMEM((256, 1024), BF16)]
    before = call(first_kernel, shape(2, UROWS, 1024), 2, 5, scratch)(info, finfo, own, partner, utab)
    sent = call(second_kernel, shape(NWAV, 24, 128), 2, 14, scratch)(
        info, finfo, beside, last, utab, before, vtab, weight, smat, trace_row, trace_col, block_count, above, below
    )
    arrived = lax.all_to_all(sent, "wav", split_axis=0, concat_axis=0, tiled=True)
    return call(
        detector_kernel,
        shape(256, 512),
        2,
        3,
        [
            pltpu.VMEM((5, NWAV * 24, 128), F32),
            pltpu.VMEM((72, 640), F32),
            pltpu.VMEM((16, 640), F32),
            pltpu.VMEM((5, 16, 512), F32),
            pltpu.VMEM((5, 16, 512), F32),
            pltpu.VMEM((5, 8 * TILES, 512), F32),
        ],
    )(info, crosstalk, arrived)


def solution(mesh):
    return jax.shard_map(
        body,
        mesh=mesh,
        in_specs=(
            P("slab", None),
            P("slab", None),
            P(),
            P("slab", None),
            P("slab", "wav"),
            P("slab", "wav"),
            P("slab", "wav"),
            P(),
        ),
        out_specs=P("slab", "wav"),
        check_vma=False,
    )
```

profile of v0, /device:TPU:8, one launch (start us, length us, event | category | flops | bytes accessed | tf_op | source)
XLA Modules:
  0.0 55.9 jit_solution(3851003960189075256)
XLA Ops:
  0.0 0.0 copy-start.6
  0.0 0.0 copy-start.5
  0.0 0.0 copy-start.4
  0.0 0.0 copy-start
  0.0 0.0 copy-start.3
  0.1 0.9 %copy.10.tab = s32[798,3]{1,0:T(8,128)S(1)} copy(s32[798,3]{0,1:T(4,128)} %param.11) | data formatting | bytes 19152 | tf_op args[2]
  1.0 0.1 stack.29.info
  1.1 0.0 copy-start.1
  1.1 0.8 %copy-done.1 = f32[32,512]{1,0:T(8,128)S(1)} copy-done((f32[32,512]{1,0:T(8,128)S(1)}, f32[32,512]{1,0:T(8,128)}, u32[]{:S(2)}) %copy-start.1) | copy-done | bytes 65560
  2.0 0.0 copy-start.2
  2.0 0.8 %copy-done.2 = s32[32,512]{1,0:T(8,128)S(1)} copy-done((s32[32,512]{1,0:T(8,128)S(1)}, s32[32,512]{1,0:T(8,128)}, u32[]{:S(2)}) %copy-start.2) | copy-done | bytes 65560
  2.8 1.2 %prepare_kernel.1.p0 = f32[40,512]{1,0:T(8,128)S(1)} custom-call(s32[8]{0:T(128)S(1)} %stack.29.info, f32[32,512]{1,0:T(8,128)S(1)} %copy-done.1, s32[32,512]{1,0:T(8,128)S(1)} %copy-done.2, s32[798,3]{1,0:T(8,128)S(1)} %copy.10.tab), custom_call_target="tpu_custom_call" | custom-call | tf_op jit(solution)/shard_map/prepare_kernel/pallas_call | solution.py:384
  4.0 2.0 %collective-permute-start = (f32[40,512]{1,0:T(8,128)S(1)}, f32[40,512]{1,0:T(8,128)S(1)}, u32[]{:S(2)}, u32[]{:S(2)}) collective-permute-start(f32[40,512]{1,0:T(8,128)S(1)} %prepare_kernel.1.p0), channel_id=1, source_target_pairs={{0,1},{1,2},{2,3},{3,0},{4,5},{5,6},{6,7},{7,4},{8,9},{9,10},{10,1... | collective-permute-start | bytes 245768 | tf_op jit(solution)/shard_map/ppermute | solution.py:385
  6.0 3.6 %collective-permute-start.1 = (f32[40,512]{1,0:T(8,128)S(1)}, f32[40,512]{1,0:T(8,128)S(1)}, u32[]{:S(2)}, u32[]{:S(2)}) collective-permute-start(f32[40,512]{1,0:T(8,128)S(1)} %prepare_kernel.1.p0), channel_id=1, source_target_pairs={{0,2},{1,3},{2,0},{3,1},{4,6},{5,7},{6,4},{7,5},{8,10},{9,11},{10,... | collective-permute-start | bytes 245768 | tf_op jit(solution)/shard_map/ppermute | solution.py:385
  9.6 1.0 %collective-permute-start.2 = (f32[40,512]{1,0:T(8,128)S(1)}, f32[40,512]{1,0:T(8,128)S(1)}, u32[]{:S(2)}, u32[]{:S(2)}) collective-permute-start(f32[40,512]{1,0:T(8,128)S(1)} %prepare_kernel.1.p0), channel_id=1, source_target_pairs={{0,3},{1,0},{2,1},{3,2},{4,7},{5,4},{6,5},{7,6},{8,11},{9,8},{10,9... | collective-permute-start | bytes 245768 | tf_op jit(solution)/shard_map/ppermute | solution.py:385
  10.6 0.8 %slice_bitcast_fusion.2 = (s32[16]{0:T(128)S(1)}, s32[16]{0:T(128)S(1)}) fusion(s32[8,16]{1,0:T(8,128)} %trow.1), kind=kLoop, calls=%fused_computation.6 | loop fusion | bytes 256 | tf_op jit(solution)/shard_map/squeeze | solution.py:393
  11.4 0.8 %slice_bitcast_fusion.1 = (s32[16]{0:T(128)S(1)}, s32[16]{0:T(128)S(1)}) fusion(s32[8,16]{1,0:T(8,128)} %tcol.1), kind=kLoop, calls=%fused_computation.5 | loop fusion | bytes 256 | tf_op jit(solution)/shard_map/squeeze | solution.py:393
  12.1 0.8 %fusion = (f32[8,1024]{1,0:T(8,128)S(1)}, f32[8,1024]{1,0:T(8,128)S(1)}) fusion(f32[64,1024]{1,0:T(8,128)} %mask.1), kind=kLoop, calls=%fused_computation.10 | loop fusion | bytes 131072 | tf_op jit(solution)/shard_map/slice | solution.py:394
  12.9 0.8 %slice_bitcast_fusion = (s32[16]{0:T(128)S(1)}, s32[16]{0:T(128)S(1)}) fusion(s32[8,16]{1,0:T(8,128)} %count.1), kind=kLoop, calls=%fused_computation.4 | loop fusion | bytes 256 | tf_op jit(solution)/shard_map/squeeze | solution.py:393
  13.7 0.0 collective-permute-done.p1
  13.7 0.0 collective-permute-done.1.p2
  13.7 0.3 collective-permute-done.2.p3
  14.0 0.7 %merge_kernel.1.first = f32[4,136,128]{2,1,0:T(8,128)S(1)} custom-call(s32[8]{0:T(128)S(1)} %stack.29.info, f32[40,512]{1,0:T(8,128)S(1)} %prepare_kernel.1.p0, f32[40,512]{1,0:T(8,128)S(1)} %collective-permute-done.p1, f32[40,512]{1,0:T(8,128)S(1)} %collective-permute-done.1.p2, f32[40,512]{1,0:T(8,128)S(1)} %collective-permute-done.2.p3), custom_call_target="tpu_custom_call" | custom-call | tf_op jit(solution)/shard_map/merge_kernel/pallas_call | solution.py:387
  14.7 1.7 %collective-permute-start.7 = (f32[4,136,128]{2,1,0:T(8,128)S(1)}, f32[4,136,128]{2,1,0:T(8,128)S(1)}, u32[]{:S(2)}, u32[]{:S(2)}) collective-permute-start(f32[4,136,128]{2,1,0:T(8,128)S(1)} %merge_kernel.1.first), channel_id=1, source_target_pairs={{0,12},{1,13},{2,14},{3,15},{4,8},{5,9},{6,10},{7,11},{8,4},{9,5},... | collective-permute-start | bytes 835592 | tf_op jit(solution)/shard_map/ppermute | solution.py:388
  16.4 1.9 %collective-permute-start.3 = (f32[4,136,128]{2,1,0:T(8,128)S(1)}, f32[4,136,128]{2,1,0:T(8,128)S(1)}, u32[]{:S(2)}, u32[]{:S(2)}) collective-permute-start(f32[4,136,128]{2,1,0:T(8,128)S(1)} %merge_kernel.1.first), channel_id=1, source_target_pairs={{0,4},{1,5},{2,6},{3,7},{4,0},{5,1},{6,2},{7,3},{8,12},{9,13},{10,... | collective-permute-start | bytes 835592 | tf_op jit(solution)/shard_map/ppermute | solution.py:389
  18.3 0.0 collective-permute-start.4
  18.3 0.1 add_convert_fusion
  18.4 2.6 %collective-permute-start.5 = (f32[9,1024]{1,0:T(8,128)S(1)}, f32[9,1024]{1,0:T(8,128)S(1)}, u32[]{:S(2)}, u32[]{:S(2)}) collective-permute-start(f32[9,1024]{1,0:T(8,128)S(1)} %pad_maximum_fusion), channel_id=1, source_target_pairs={{0,1},{1,2},{2,3},{3,4},{4,5},{5,6},{6,7},{7,8},{8,9},{9,10},{10,1... | collective-permute-start | bytes 110600 | tf_op jit(solution)/shard_map/ppermute | solution.py:396
  21.0 5.3 %collective-permute-start.6 = (f32[9,1024]{1,0:T(8,128)S(1)}, f32[9,1024]{1,0:T(8,128)S(1)}, u32[]{:S(2)}, u32[]{:S(2)}) collective-permute-start(f32[9,1024]{1,0:T(8,128)S(1)} %pad_maximum_fusion.1), channel_id=1, source_target_pairs={{1,0},{2,1},{3,2},{4,3},{5,4},{6,5},{7,6},{8,7},{9,8},{10,9},{11,1... | collective-permute-start | bytes 110600 | tf_op jit(solution)/shard_map/ppermute | solution.py:397
  26.4 6.1 %collective-permute-done.5.above = f32[9,1024]{1,0:T(8,128)S(1)} collective-permute-done((f32[9,1024]{1,0:T(8,128)S(1)}, f32[9,1024]{1,0:T(8,128)S(1)}, u32[]{:S(2)}, u32[]{:S(2)}) %collective-permute-start.5) | collective-permute-done | bytes 36896 | tf_op jit(solution)/shard_map/ppermute | solution.py:396
  32.4 0.0 collective-permute-done.6.below
  32.4 0.0 copy-done.6
  32.4 0.0 copy-done
  32.5 3.2 %table_kernel.1 = (bf16[2,2,160,256]{3,2,1,0:T(8,128)(2,1)S(1)}, bf16[2,2,2,256,512]{4,3,2,1,0:T(8,128)(2,1)S(1)}, f32[80,1024]{1,0:T(8,128)S(1)}, bf16[1024,256]{1,0:T(8,128)(2,1)S(1)}) custom-call(s32[8]{0:T(128)S(1)} %stack.29.info, f32[64]{0:T(128)S(1)} %copy-done.6, f32[64,1024]{1,0:T(8,128)S(1)} %copy-done, ...), custom_call_target="tpu_custom_call" | custom-call | tf_op jit(solution)/shard_map/table_kernel/pallas_call | solution.py:399
  35.7 0.0 collective-permute-done.7.second
  35.7 2.3 %first_kernel.1.before = f32[2,80,1024]{2,1,0:T(8,128)S(1)} custom-call(s32[8]{0:T(128)S(1)} %stack.29.info, f32[64]{0:T(128)S(1)} %copy-done.6, f32[4,136,128]{2,1,0:T(8,128)S(1)} %merge_kernel.1.first, f32[4,136,128]{2,1,0:T(8,128)S(1)} %collective-permute-done.7.second, bf16[2,2,160,256]{3,2,1,0:T(8,128)(2,1)S(1)} %get-tuple-element.9.utab), custom_call_target="tpu_custom_call" | custom-call | tf_op jit(solution)/shard_map/first_kernel/pallas_call | solution.py:411
  38.0 0.0 collective-permute-done.3.first
  38.0 0.0 collective-permute-done.4.second
  38.0 0.0 copy-done.5
  38.0 0.0 copy-done.4
  38.0 0.0 copy-done.3
  38.0 0.0 copy-start.7
  38.1 4.1 %second_kernel.1 = f32[8,24,128]{2,1,0:T(8,128)S(1)} custom-call(s32[8]{0:T(128)S(1)} %stack.29.info, f32[64]{0:T(128)S(1)} %copy-done.6, f32[4,136,128]{2,1,0:T(8,128)S(1)} %collective-permute-done.3.first, f32[4,136,128]{2,1,0:T(8,128)S(1)} %collective-permute-done.4.second, bf16[2,2,160,256]{3,2,1,0:T(8,128)(2,1)S(1)} %get-tuple-element.9.utab, ...), custom_call_target="tpu_custom_call" | custom-call | tf_op jit(solution)/shard_map/second_kernel/pallas_call | solution.py:412
  42.1 9.9 %all_to_all.5.arrived = f32[8,24,128]{2,1,0:T(8,128)S(1)} all-to-all(f32[8,24,128]{2,1,0:T(8,128)S(1)} %second_kernel.1), channel_id=1, replica_groups=mesh['wav'=8,'slab'=16] {'wav'}, dimensions={0} | all-to-all | bytes 196608 | tf_op jit(solution)/shard_map/all_to_all | solution.py:415
  52.1 0.0 copy-done.7
  52.1 3.9 %detector_kernel.1 = f32[256,512]{1,0:T(8,128)} custom-call(s32[8]{0:T(128)S(1)} %stack.29.info, f32[5,5]{1,0:T(8,128)S(1)} %copy-done.7, f32[8,24,128]{2,1,0:T(8,128)S(1)} %all_to_all.5.arrived), custom_call_target="tpu_custom_call" | custom-call | tf_op jit(solution)/shard_map/detector_kernel/pallas_call | solution.py:416
  (4 shorter events, 0.0 us)
Async XLA Ops:
  0.0 32.4 %copy-start.6 = (f32[64]{0:T(128)S(1)}, f32[64]{0:T(128)}, u32[]{:S(2)}) copy-start(f32[64]{0:T(128)} %constant.44.clone.finfo) | copy-start | bytes 772
  0.0 38.0 %copy-start.5 = (s32[8,16]{1,0:T(8,128)S(1)}, s32[8,16]{1,0:T(8,128)}, u32[]{:S(2)}) copy-start(s32[8,16]{1,0:T(8,128)} %trow.1) | copy-start | bytes 1540
  0.0 38.0 %copy-start.4 = (s32[8,16]{1,0:T(8,128)S(1)}, s32[8,16]{1,0:T(8,128)}, u32[]{:S(2)}) copy-start(s32[8,16]{1,0:T(8,128)} %tcol.1) | copy-start | bytes 1540
  0.0 32.4 %copy-start = (f32[64,1024]{1,0:T(8,128)S(1)}, f32[64,1024]{1,0:T(8,128)}, u32[]{:S(2)}) copy-start(f32[64,1024]{1,0:T(8,128)} %mask.1) | copy-start | bytes 786436
  0.0 38.0 %copy-start.3 = (s32[8,16]{1,0:T(8,128)S(1)}, s32[8,16]{1,0:T(8,128)}, u32[]{:S(2)}) copy-start(s32[8,16]{1,0:T(8,128)} %count.1) | copy-start | bytes 1540
  1.1 0.8 %copy-start.1 = (f32[32,512]{1,0:T(8,128)S(1)}, f32[32,512]{1,0:T(8,128)}, u32[]{:S(2)}) copy-start(f32[32,512]{1,0:T(8,128)} %amp.1) | copy-start | bytes 196612
  2.0 0.8 %copy-start.2 = (s32[32,512]{1,0:T(8,128)S(1)}, s32[32,512]{1,0:T(8,128)}, u32[]{:S(2)}) copy-start(s32[32,512]{1,0:T(8,128)} %seg.1) | copy-start | bytes 196612
  4.0 9.7 %collective-permute-start = (f32[40,512]{1,0:T(8,128)S(1)}, f32[40,512]{1,0:T(8,128)S(1)}, u32[]{:S(2)}, u32[]{:S(2)}) collective-permute-start(f32[40,512]{1,0:T(8,128)S(1)} %prepare_kernel.1.p0), channel_id=1, source_target_pairs={{0,1},{1,2},{2,3},{3,0},{4,5},{5,6},{6,7},{7,4},{8,9},{9,10},{10,1... | collective-permute-start | bytes 245768 | tf_op jit(solution)/shard_map/ppermute | solution.py:385
  6.0 7.7 %collective-permute-start.1 = (f32[40,512]{1,0:T(8,128)S(1)}, f32[40,512]{1,0:T(8,128)S(1)}, u32[]{:S(2)}, u32[]{:S(2)}) collective-permute-start(f32[40,512]{1,0:T(8,128)S(1)} %prepare_kernel.1.p0), channel_id=1, source_target_pairs={{0,2},{1,3},{2,0},{3,1},{4,6},{5,7},{6,4},{7,5},{8,10},{9,11},{10,... | collective-permute-start | bytes 245768 | tf_op jit(solution)/shard_map/ppermute | solution.py:385
  9.6 4.4 %collective-permute-start.2 = (f32[40,512]{1,0:T(8,128)S(1)}, f32[40,512]{1,0:T(8,128)S(1)}, u32[]{:S(2)}, u32[]{:S(2)}) collective-permute-start(f32[40,512]{1,0:T(8,128)S(1)} %prepare_kernel.1.p0), channel_id=1, source_target_pairs={{0,3},{1,0},{2,1},{3,2},{4,7},{5,4},{6,5},{7,6},{8,11},{9,8},{10,9... | collective-permute-start | bytes 245768 | tf_op jit(solution)/shard_map/ppermute | solution.py:385
  14.7 21.0 %collective-permute-start.7 = (f32[4,136,128]{2,1,0:T(8,128)S(1)}, f32[4,136,128]{2,1,0:T(8,128)S(1)}, u32[]{:S(2)}, u32[]{:S(2)}) collective-permute-start(f32[4,136,128]{2,1,0:T(8,128)S(1)} %merge_kernel.1.first), channel_id=1, source_target_pairs={{0,12},{1,13},{2,14},{3,15},{4,8},{5,9},{6,10},{7,11},{8,4},{9,5},... | collective-permute-start | bytes 835592 | tf_op jit(solution)/shard_map/ppermute | solution.py:388
  16.4 21.6 %collective-permute-start.3 = (f32[4,136,128]{2,1,0:T(8,128)S(1)}, f32[4,136,128]{2,1,0:T(8,128)S(1)}, u32[]{:S(2)}, u32[]{:S(2)}) collective-permute-start(f32[4,136,128]{2,1,0:T(8,128)S(1)} %merge_kernel.1.first), channel_id=1, source_target_pairs={{0,4},{1,5},{2,6},{3,7},{4,0},{5,1},{6,2},{7,3},{8,12},{9,13},{10,... | collective-permute-start | bytes 835592 | tf_op jit(solution)/shard_map/ppermute | solution.py:389
  18.3 19.8 %collective-permute-start.4 = (f32[4,136,128]{2,1,0:T(8,128)S(1)}, f32[4,136,128]{2,1,0:T(8,128)S(1)}, u32[]{:S(2)}, u32[]{:S(2)}) collective-permute-start(f32[4,136,128]{2,1,0:T(8,128)S(1)} %merge_kernel.1.first), channel_id=1, source_target_pairs={{0,8},{1,9},{2,10},{3,11},{4,12},{5,13},{6,14},{7,15},{8,0},{9,1},... | collective-permute-start | bytes 835592 | tf_op jit(solution)/shard_map/ppermute | solution.py:390
  18.4 14.1 %collective-permute-start.5 = (f32[9,1024]{1,0:T(8,128)S(1)}, f32[9,1024]{1,0:T(8,128)S(1)}, u32[]{:S(2)}, u32[]{:S(2)}) collective-permute-start(f32[9,1024]{1,0:T(8,128)S(1)} %pad_maximum_fusion), channel_id=1, source_target_pairs={{0,1},{1,2},{2,3},{3,4},{4,5},{5,6},{6,7},{7,8},{8,9},{9,10},{10,1... | collective-permute-start | bytes 110600 | tf_op jit(solution)/shard_map/ppermute | solution.py:396
  21.0 11.4 %collective-permute-start.6 = (f32[9,1024]{1,0:T(8,128)S(1)}, f32[9,1024]{1,0:T(8,128)S(1)}, u32[]{:S(2)}, u32[]{:S(2)}) collective-permute-start(f32[9,1024]{1,0:T(8,128)S(1)} %pad_maximum_fusion.1), channel_id=1, source_target_pairs={{1,0},{2,1},{3,2},{4,3},{5,4},{6,5},{7,6},{8,7},{9,8},{10,9},{11,1... | collective-permute-start | bytes 110600 | tf_op jit(solution)/shard_map/ppermute | solution.py:397
  38.0 14.0 %copy-start.7 = (f32[5,5]{1,0:T(8,128)S(1)}, f32[5,5]{1,0:T(8,128)}, u32[]{:S(2)}) copy-start(f32[5,5]{1,0:T(8,128)} %kernel.1) | copy-start | bytes 304
where the time goes:
time: 56.4 us; the launch traced here: 55.9 us
  starting transfers between devices  18.1 us (32%)
  Pallas kernels  15.4 us (27%)
  blocking collectives  9.92 us (18%)
  waiting for transfers between devices  6.43 us (11%)
  local copies, waits for them, and re-layouts  5.83 us (10%)
    all_to_all x1, blocking collectives, body(): lax.all_to_all(sent, 'wav', split_axis=0, concat_axis=0, tiled=True)  9.92 us
    ppermute x3, starting transfers between devices, body(): lax.ppermute(piece, 'slab', along_z(k))  6.57 us
    ppermute x1, waiting for transfers between devices, body(): lax.ppermute(edge(7, slice(56, 64)), 'slab', [(i, i + 1) for i in range(N...  6.07 us
    ppermute x1, starting transfers between devices, body(): lax.ppermute(edge(0, slice(0, 8)), 'slab', [(i + 1, i) for i in range(NSL...  5.34 us
    pallas_call x1, Pallas kernels, body(): call(second_kernel, shape(NWAV, 24, 128), 2, 14, scratch)  4.06 us
    pallas_call x1, Pallas kernels, body(): call(detector_kernel, shape(256, 512), 2, 3, [pltpu.VMEM((5, NWAV * 24, 1...  3.89 us
    pallas_call x1, Pallas kernels, body(): call(table_kernel, [shape(2, 2, 2 * UROWS, 256, dtype=BF16), shape(2, 2,...  3.2 us
    unnamed x17, local copies, waits for them, and re-layouts  2.66 us
  transfers between devices with their start and end apart: 8, of which 2 were waited for; matrix products, arithmetic and copies ran while one was open for 6% of the time, Pallas kernels for 10%

commit v1 on v0

v1 whole, which is shorter than its diff:
```python
import functools

import jax
import jax.numpy as jnp
import numpy as np
from jax import lax
from jax.experimental import pallas as pl
from jax.experimental.pallas import tpu as pltpu
from jax.sharding import PartitionSpec as P

F32, BF16, I32 = jnp.float32, jnp.bfloat16, jnp.int32

NP, NF, NL, DPIX, SEGMENTS, WAVES = 512, 1024, 128, 32, 798, 16
NWAV, NSLAB = 8, 16
ROWS = NP // NSLAB
FROWS = NF // NSLAB
UROWS = FROWS + 16
GROUP = 128
PIECE, EDGE = 2 * (ROWS + 8), 72
MROWS = GROUP + 8
HALF, FHALF = NP // 2, NF // 2

SIN = (6.283185302511503, -41.34170040531721, 81.6051313857832, -76.70301535364747,
       42.02592698447418, -14.899846663536497, 3.2381375046186873)
COS = (0.9999999890590228, -19.73920449945383, 64.93911745989081, -85.45013953079767,
       60.167630950263465, -25.967599245923743, 6.52865815775625)


def place_of():
    w, s = lax.axis_index("wav").astype(I32), lax.axis_index("slab").astype(I32)
    y = s >> 2
    return w, s, y, s & 3, w >> 1, w & 1, jnp.where(y < 2, 1.0, -1.0), jnp.where((y == 0) | (y == 3), 0, 1)


def iota(shape, dim):
    return lax.broadcasted_iota(I32, shape, dim)


def dot(a, b):
    return jnp.dot(a, b, preferred_element_type=F32)


def split2(x):
    high = x.astype(BF16)
    return high, (x - high.astype(F32)).astype(BF16)


def split3(x):
    high = x.astype(BF16)
    rest = x - high.astype(F32)
    middle = rest.astype(BF16)
    return high, middle, (rest - middle.astype(F32)).astype(BF16)


def sincos(turns):
    t = turns - jnp.round(turns)
    z = t * t
    s, c = SIN[-1], COS[-1]
    for a, b in zip(SIN[-2::-1], COS[-2::-1]):
        s, c = s * z + a, c * z + b
    return s * t, c


def reversal(n):
    return (iota((n, n), 0) + iota((n, n), 1) == n - 1).astype(BF16)


def prepare_kernel(amp_in, seg_in, tab_in, mask, trow, tcol, count, out, up, down, trace, amp, seg, tab, tables, edges, sems):
    w, s, y, z, x, core, sign, pair = place_of()
    copies = [
        pltpu.make_async_copy(a, b, sems.at[k])
        for k, (a, b) in enumerate(
            (
                (tab_in, tab),
                (seg_in.at[0:8, :], seg.at[0:8, :]),
                (seg_in.at[16:24, :], seg.at[8:16, :]),
                (amp_in, amp),
                (trow, tables.at[0]),
                (tcol, tables.at[1]),
                (count, tables.at[2]),
                (mask.at[FROWS - 8:FROWS, :], edges.at[0]),
                (mask.at[0:8, :], edges.at[1]),
            )
        )
    ]
    for copy in copies:
        copy.start()
    lower = y >= 2
    rows, cols = iota((ROWS, ROWS), 0), iota((ROWS, ROWS), 1)
    turned = (cols == jnp.where(lower, ROWS - 1 - rows, rows)).astype(BF16)
    rev = reversal(128)
    lane = iota((NP, 128), 1)
    pick = ((iota((NP, 128), 0) == 16 * (lane & 31)) & (lane < 96)).astype(BF16)
    out[...] = jnp.zeros((PIECE, 128), F32)
    for ref in (up, down):
        ref[PIECE + 64:PIECE + EDGE, :] = jnp.zeros((8, 128), F32)
    trace[...] = jnp.zeros((8, 128), F32)
    for copy in copies:
        copy.wait()
    for c in range(3):
        table = tables[c].astype(F32)
        trace[:, 16 * c:16 * c + 16] = table
        up[PIECE + 64:PIECE + 65, 16 * c:16 * c + 16] = table[7:8]
        down[PIECE + 64:PIECE + 65, 16 * c:16 * c + 16] = table[0:1]
    ids = sum(dot(part, pick) for part in split2(seg[...].astype(F32)))
    upper_ids, lower_ids = ids[0:1], ids[8:9]
    ids = jnp.concatenate(
        [jnp.where(lower, lower_ids, upper_ids), jnp.where(lower, upper_ids, lower_ids)], axis=1
    )
    which = iota((SEGMENTS, 256), 0).astype(F32)
    found = sum(dot(part, (which == ids).astype(BF16)) for part in split2(tab[...].astype(F32)))
    found = jnp.sum(jnp.where(iota((3, 256), 0) == (iota((3, 256), 1) & 127) >> 5, found, 0.0), axis=0, keepdims=True)
    for k in range(2):
        out[ROWS + k:ROWS + k + 1, :] = found[:, 128 * k:128 * k + 128]
    first = core == 0
    left = jnp.where(first, amp[:, 0:128], amp[:, 128:256])
    right = jnp.where(first, amp[:, 384:512], amp[:, 256:384])
    out[0:ROWS, :] = sum(dot(turned, part) for part in split3(left))
    out[ROWS + 8:2 * ROWS + 8, :] = sum(dot(turned, dot(part, rev).astype(BF16)) for part in split3(right))
    for k, ref in enumerate((up, down)):
        ref[0:PIECE, :] = out[...]
        for q in range(8):
            ref[PIECE + 8 * q:PIECE + 8 * q + 8, :] = edges[k, :, 128 * q:128 * q + 128]


def merge_kernel(p0, p1, p2, p3, after, out, wrap):
    del after
    w, s, y, z, x, core, sign, pair = place_of()
    wrap[...] = jnp.where(z == 0, p1[PIECE:PIECE + EDGE, :], p3[PIECE:PIECE + EDGE, :])
    out[:, GROUP:MROWS, :] = jnp.zeros((2, 8, 128), F32)
    for k, piece in enumerate((p0, p1, p2, p3)):
        source = lax.rem(z - k + 4, 4)
        place = jnp.where(y >= 2, 3 - source, source)
        for at in range(4):

            @pl.when(place == at)
            def _(at=at, piece=piece):
                for t in range(2):
                    for b in range(2):
                        r0 = (ROWS + 8) * t + 16 * b
                        out[t, pl.ds(2 * at + b, 16, stride=8), :] = piece[r0:r0 + 16, :]
                out[0, GROUP + 2 * at:GROUP + 2 * at + 2, :] = piece[ROWS:ROWS + 2, :]


def wavelength(w):
    return jnp.full((1, 1), 1000 + w, I32).astype(F32)


def angle(m, n, w):
    lam = wavelength(w)
    short = jnp.round(250.0 / lam * 2.0**14) * 2.0**-14
    rest = (250.0 - short * lam) / lam
    product = m * n
    a, b = (product >> 10).astype(F32), (product & 1023).astype(F32)
    t = a * short
    t = t - jnp.round(t)
    return sincos(t + a * rest + b * (250.0 / 1024.0 / lam))


def table_kernel(after, utab, vtab, smat):
    del after
    w, s, y, z, x, core, sign, pair = place_of()
    for m in range(4):
        wave = 2 * (w if m < 2 else w ^ 1) + (m & 1)
        for p in range(2):
            g = pair if p == 0 else 1 - pair
            u = 64 * s - 8 + iota((UROWS, GROUP), 0)
            rho = iota((UROWS, GROUP), 1)
            i = 128 * g + 16 * (rho & 7) + (rho >> 3)
            sin, cos = angle(2 * u + 1 - NF, 2 * i + 1 - NP, wave)
            for at, part in ((0, cos), (GROUP, sin * sign)):
                high, low = split2(part)
                utab[p, m, 0:UROWS, at:at + GROUP] = high
                utab[p, m, UROWS:2 * UROWS, at:at + GROUP] = low

        if m >= 2:
            continue

        def chunk(c, carry, m=m, wave=wave):
            j0 = pl.multiple_of(16 * c, 16)
            j = ((j0 + 128 * core) & 255) + iota((16, FHALF), 0)
            v = iota((16, FHALF), 1)
            sin, cos = angle(2 * v + 1 - NF, 2 * j + 1 - NP, wave)
            for q, part in ((0, cos), (1, sin)):
                high, low = split2(part)
                vtab[m, q, 0, pl.ds(j0, 16), :] = high
                vtab[m, q, 1, pl.ds(j0, 16), :] = low
            return carry

        lax.fori_loop(0, HALF // 16, chunk, 0)
    row, lane = iota((FHALF, 256), 0), iota((FHALF, 256), 1)
    column = 2 * ((x + (lane >> 5)) & 3) + jnp.where(lane < 128, core, 1 - core)
    lens = jnp.where((lane & 31) < 18, 16 * column - 1 + (lane & 31), -1)
    smat[0:FHALF, :] = (lens == row >> 3).astype(BF16)
    smat[FHALF:NF, :] = (lens == NL - 1 - (row >> 3)).astype(BF16)


def weight_kernel(mask, p1, p3, edge, trace, after, weight, lenses):
    del after
    w, s, y, z, x, core, sign, pair = place_of()
    above = jnp.where(z == 0, edge[...], p1[PIECE:PIECE + EDGE, :])
    below = jnp.where(z == 3, edge[...], p3[PIECE:PIECE + EDGE, :])
    lenses[0:8, :] = trace[...]
    lenses[8:9, :] = above[64:65]
    lenses[9:10, :] = below[64:65]
    lenses[10:16, :] = jnp.zeros((6, 128), F32)
    u = 64 * s - 8 + iota((UROWS, FHALF), 0)
    v = iota((UROWS, FHALF), 1)
    down, across = (2 * u + 1 - NF).astype(F32) * 0.5, (2 * v + 1 - NF).astype(F32) * 0.5
    fade = 1.0 - jnp.exp((down * down + across * across) * (-1.0 / 1024.0))
    rev = reversal(256)
    above, below = (jnp.concatenate([ref[8 * q:8 * q + 8] for q in range(8)], axis=1) for ref in (above, below))
    full = jnp.concatenate([above, mask[...], below], axis=0)
    t = full[:, :FHALF] * fade
    weight[:, :FHALF] = t * t * 2.0**-24
    for q in range(2):
        flipped = sum(dot(part, rev) for part in split3(full[:, NF - 256 * (q + 1):NF - 256 * q]))
        t = flipped * fade[:, 256 * q:256 * (q + 1)]
        weight[:, FHALF + 256 * q:FHALF + 256 * (q + 1)] = t * t * 2.0**-24


def pair_fields(first, second, utab, p, whi, wlo):
    w, s, y, z, x, core, sign, pair = place_of()
    g = pair if p == 0 else 1 - pair
    coef = jnp.concatenate([first[0, GROUP:MROWS, :], second[0, GROUP:MROWS, :]], axis=0)
    high, low = split2(coef)
    coef = jnp.concatenate([high, low], axis=0)
    row, lane = iota((128, 128), 0), iota((128, 128), 1)
    place = iota((16, 128), 0)
    down = (32 * (8 * g + (place & 7)) + 1 - NP).astype(F32) * (1.0 / 1024.0)
    toward = jnp.where(place < 8, sign, -sign)
    across = (2 * (128 * core + iota((16, 128), 1)) + 1 - NP).astype(F32) * (1.0 / 1024.0)
    paths, steps = [], []
    for side in range(2):
        block = 8 * core + (lane >> 4)
        block = block if side == 0 else 31 - block
        pqr = []
        for c in range(3):
            both = dot(coef, (row == 32 * c + block).astype(BF16))
            pqr.append(both[0:16] + both[16:32])
        slope = toward * pqr[2]
        paths.append(pqr[0] + (across if side == 0 else -across) * pqr[1] + slope * down)
        steps.append(slope * (1.0 / 512.0))
    fields = []
    for m in range(4):
        inverse = 1.0 / wavelength(2 * (w if m < 2 else w ^ 1) + (m & 1))
        start = [sincos(path * inverse) for path in paths]
        turn = [sincos(step * inverse) for step in steps]

        def four(values, n):
            return [values[side][n][8 * t:8 * t + 8] for t in range(2) for side in range(2)]

        step_im, step_re = four(turn, 0), four(turn, 1)

        def rows(r2, carry, step_im=step_im, step_re=step_re):
            re, im = carry
            found = [[] for _ in range(8)]
            for h in range(2):
                r0 = pl.multiple_of(16 * r2 + 8 * h, 8)
                qre, qim = [], []
                for t, ref in enumerate((first, second)):
                    for side in range(2):
                        a = ref[side, pl.ds(r0, 8), :]
                        qre.append(a * re[2 * t + side])
                        qim.append(a * im[2 * t + side])
                (fl, fr, sl, sr), (gl, gr, hl, hr) = qre, qim
                a, b, c, d = fl + sl, sl - fl, fr + sr, sr - fr
                e, f, k, n = gl + hl, gl - hl, gr + hr, gr - hr
                for q, value in enumerate((a + c, e + k, e - k, c - a, f + n, b + d, b - d, n - f)):
                    found[q].append(value)
                re, im = (
                    [x * p - y * q for x, y, p, q in zip(re, im, step_re, step_im)],
                    [x * q + y * p for x, y, p, q in zip(re, im, step_re, step_im)],
                )
            for q, values in enumerate(found):
                high, low = split2(jnp.concatenate(values, axis=0))
                r0 = pl.multiple_of(16 * r2 + (GROUP if q >= 4 else 0), 16)
                c0 = 128 * (q & 3)
                whi[pl.ds(r0, 16), c0:c0 + 128] = high
                wlo[pl.ds(r0, 16), c0:c0 + 128] = low
            return re, im

        lax.fori_loop(0, 8, rows, (four(start, 1), four(start, 0)))
        table = utab[p, m]
        both = dot(table, whi[...])
        fields.append(both[:UROWS] + both[UROWS:] + dot(table[:UROWS], wlo[...]))
    return fields


def first_kernel(first, second, utab, out, whi, wlo):
    for m, field in enumerate(pair_fields(first, second, utab, 0, whi, wlo)):
        out[m] = field


def second_kernel(first, second, utab, before, after, keep, give, whi, wlo):
    del after
    for m, field in enumerate(pair_fields(first, second, utab, 1, whi, wlo)):
        (keep if m < 2 else give)[m & 1] = field + before[m]


def lens_kernel(keep, got, vtab, weight, smat, lenses, mine, other):
    mine[...] = jnp.zeros(mine.shape, F32)
    other[...] = jnp.zeros(other.shape, F32)
    outs = [ref.at[k] for ref in (mine, other) for k in range(4)]
    for m in range(2):
        parts = [
            jnp.concatenate([ref[m, :, 128 * q:128 * q + 128] for ref in (keep, got)], axis=1) for q in range(4)
        ]
        terms = []
        for q in range(2):
            side = jnp.concatenate(parts[2 * q:2 * q + 2], axis=0)
            high, low = split2(side)
            both = dot(jnp.concatenate([high, low], axis=0), vtab[m, q, 0])
            terms.append(both[:2 * UROWS] + both[2 * UROWS:] + dot(high, vtab[m, q, 1]))
        lens = 0.0
        for q, value in enumerate((terms[0] + terms[1], terms[0] - terms[1])):
            re, im = value[:UROWS], value[UROWS:]
            power = (re * re + im * im) * weight[:, FHALF * q:FHALF * (q + 1)]
            summed = jnp.sum(power.reshape(UROWS // 8, 8, FHALF), axis=1)
            for part in split3(summed):
                lens = lens + dot(part, smat[FHALF * q:FHALF * (q + 1), :])
        for d in range(NWAV):
            outs[d][10 * m:10 * m + 10, 0:32] = lens[:, 32 * d:32 * d + 32]
    tables = lenses[0:10, 0:48]
    for out in outs:
        out[0:10, 32:80] = tables


def pack_kernel(mine, got, *outs):
    for k, out in enumerate(outs):
        out[0] = mine[k]
        out[1] = got[k]


TILES = 4 * 8 + 2


def order(a):
    return a - 1 if 0 < a < 9 else 8 + a // 9


def detector_kernel(kernel, a0, a1, a2, a3, out, arrived, spec, trace, sums, aq, bq, hp):
    w, s, y, z, x, core, sign, pair = place_of()
    for k, ref in enumerate((a0, a1, a2, a3)):
        source = 2 * ((x - k + 4) & 3)
        arrived[source + core] = ref[0]
        arrived[source + 1 - core] = ref[1]
    lane = iota((24, 128), 1)
    prev, own, nxt = arrived[jnp.maximum(w - 1, 0)], arrived[w], arrived[jnp.minimum(w + 1, NWAV - 1)]
    spot = (iota((128, 640), 0) == iota((128, 640), 1) >> 5).astype(BF16)
    rows = arrived[...].reshape(NWAV * 24, 128)
    wide = sum(dot(part, spot) for part in split3(rows))
    for t in range(5):
        spec[t] = wide[:, 128 * t:128 * t + 128]
    tables = []
    for c in range(3):
        tables.append(
            jnp.where(
                lane == 0,
                pltpu.roll(prev, 128 - (47 + 16 * c), 1),
                jnp.where(
                    lane < 17,
                    pltpu.roll(own, 128 - (31 + 16 * c), 1),
                    jnp.where(lane == 17, pltpu.roll(nxt, 128 - (15 + 16 * c), 1), 0.0),
                ),
            )
        )
    trace[...] = dot(jnp.concatenate(tables, axis=0).astype(BF16), spot)
    place = (iota((8, 640), 1) & 31).astype(F32)
    wave = 2.0 * iota((8, 640), 0).astype(F32)
    sums[...] = jnp.zeros(sums.shape, F32)
    for a in range(10):
        at = order(a)
        offset = place - trace[24 + at:25 + at, :]
        count = trace[48 + at:49 + at, :]
        spread = 0.0
        for m in range(2):
            value = jnp.concatenate([spec[t, pl.ds(10 * m + a, NWAV, stride=24), :] for t in range(5)], axis=1)
            along = jnp.exp(-0.5 * jnp.abs(offset - (wave + m)))
            spread = spread + jnp.where(wave + m < count, value, 0.0) * along
        sums[at:at + 1, :] = jnp.sum(spread, axis=0, keepdims=True)
    row = trace[0:16, :] * 0.25
    total = sums[...]
    falling, rising = total * jnp.exp(row), total * jnp.exp(-row)
    for q in range(5):
        aq[q] = pltpu.roll(falling, 640 - (30 + q), 1)[:, 0:512]
        bq[q] = pltpu.roll(rising, 640 - (30 + q), 1)[:, 0:512]
    weights = [[kernel[p, q] + (1.0 if p == q == 2 else 0.0) for q in range(5)] for p in range(5)]
    depth = iota((8, 128), 0).astype(F32) * 0.25

    def cell(a, tiles):
        for lt in range(4):
            at = slice(128 * lt, 128 * lt + 128)
            if isinstance(a, int):
                fall, rise = ([ref[q, order(a):order(a) + 1, at] for q in range(5)] for ref in (aq, bq))
            else:
                fall, rise = ([pltpu.roll(ref[q, 0:8, at], 9 - a, 0)[0:1] for q in range(5)] for ref in (aq, bq))
            for rt in tiles:
                down, up = jnp.exp(-(depth + 2.0 * rt)), jnp.exp(depth + 2.0 * rt)
                raw = [jnp.minimum(down * f, up * r) for f, r in zip(fall, rise)]
                r0 = pl.multiple_of(8 * (4 * a + rt - 3), 8)
                for p in range(5):
                    h = raw[0] * weights[p][0]
                    for q in range(1, 5):
                        h = h + raw[q] * weights[p][q]
                    hp[p, pl.ds(r0, 8), at] = h

    cell(0, (3,))
    cell(9, (0,))

    def middle(a, carry):
        cell(a, range(4))
        return carry

    lax.fori_loop(1, 9, middle, 0)
    for r in range(0, 256, 8):
        out[r:r + 8, :] = sum(hp[p, r + 6 + p:r + 14 + p, :] for p in range(5))


def call(kernel, outs, in_smem, n_in, scratch=(), tail=(), limit=40):
    specs = [pl.BlockSpec(memory_space=pltpu.SMEM)] * in_smem
    specs += [pl.BlockSpec(memory_space=pltpu.VMEM)] * (n_in - in_smem)
    specs[n_in - len(tail):] = tail
    single = not isinstance(outs, (list, tuple))
    vmem = pl.BlockSpec(memory_space=pltpu.VMEM)
    return pl.pallas_call(
        kernel,
        out_shape=outs,
        in_specs=specs,
        out_specs=vmem if single else [vmem] * len(outs),
        scratch_shapes=list(scratch),
        compiler_params=pltpu.CompilerParams(vmem_limit_bytes=limit * 2**20),
        name=kernel.__name__,
    )


def shape(*dims, dtype=F32):
    return jax.ShapeDtypeStruct(dims, dtype)


def along_z(k):
    return [(4 * y + z, 4 * y + (z + k) % 4) for y in range(4) for z in range(4)]


def along_y(other):
    return [(4 * y + z, 4 * other[y] + z) for y in range(4) for z in range(4)]


def body(amplitude, seg_map, seg_table, focal_mask, trace_row, trace_col, block_count, crosstalk):
    anywhere = [pl.BlockSpec(memory_space=pl.ANY)]
    piece, up, down, trace = call(
        prepare_kernel,
        [shape(PIECE, 128), shape(PIECE + EDGE, 128), shape(PIECE + EDGE, 128), shape(8, 128)],
        0,
        7,
        [
            pltpu.VMEM((ROWS, NP), F32),
            pltpu.VMEM((16, NP), I32),
            pltpu.VMEM((3, SEGMENTS), I32),
            pltpu.VMEM((3, 8, 16), I32),
            pltpu.VMEM((2, 8, NF), F32),
            pltpu.SemaphoreType.DMA((9,)),
        ],
        tail=anywhere * 7,
        limit=54,
    )(amplitude, seg_map, seg_table.T, focal_mask, trace_row, trace_col, block_count)
    utab, vtab, smat = call(
        table_kernel,
        [
            shape(2, 4, 2 * UROWS, 256, dtype=BF16),
            shape(2, 2, 2, HALF, FHALF, dtype=BF16),
            shape(NF, 256, dtype=BF16),
        ],
        0,
        1,
        tail=anywhere,
    )(piece)
    p1 = lax.ppermute(up, "slab", along_z(1))
    p3 = lax.ppermute(down, "slab", along_z(3))
    p2 = lax.ppermute(piece, "slab", along_z(2))
    own, wrap = call(merge_kernel, [shape(2, MROWS, 128), shape(EDGE, 128)], 0, 5, tail=anywhere)(
        piece, p1, p2, p3, smat
    )
    partner = lax.ppermute(own, "slab", along_y((3, 2, 1, 0)))
    beside = lax.ppermute(own, "slab", along_y((1, 0, 3, 2)))
    last = lax.ppermute(own, "slab", along_y((2, 3, 0, 1)))
    edge = lax.ppermute(
        wrap, "slab", [(4 * y, 4 * y + 4) for y in range(3)] + [(4 * y + 7, 4 * y + 3) for y in range(3)]
    )
    scratch = [pltpu.VMEM((256, 512), BF16)] * 2
    before = call(first_kernel, shape(4, UROWS, 512), 0, 3, scratch)(own, partner, utab)
    keep, give = call(second_kernel, [shape(2, UROWS, 512)] * 2, 0, 5, scratch, tail=anywhere)(
        beside, last, utab, before, edge
    )
    weight, lenses = call(weight_kernel, [shape(UROWS, NF), shape(16, 128)], 0, 6, tail=anywhere)(
        focal_mask, p1, p3, edge, trace, give
    )
    sibling = [(i, i ^ 1) for i in range(NWAV)]
    crossed = lax.ppermute(give, "wav", sibling)
    mine, other = call(lens_kernel, [shape(4, 24, 128)] * 2, 0, 6)(
        keep, crossed, vtab, weight, smat, lenses
    )
    got = lax.ppermute(other, "wav", sibling)
    sent = call(pack_kernel, [shape(2, 24, 128)] * 4, 0, 2)(mine, got)
    arrived = [sent[0]] + [
        lax.ppermute(sent[k], "wav", [(i, (i + 2 * k) % NWAV) for i in range(NWAV)]) for k in (1, 2, 3)
    ]
    return call(
        detector_kernel,
        shape(256, 512),
        1,
        5,
        [
            pltpu.VMEM((NWAV, 24, 128), F32),
            pltpu.VMEM((5, NWAV * 24, 128), F32),
            pltpu.VMEM((72, 640), F32),
            pltpu.VMEM((16, 640), F32),
            pltpu.VMEM((5, 16, 512), F32),
            pltpu.VMEM((5, 16, 512), F32),
            pltpu.VMEM((5, 8 * TILES, 512), F32),
        ],
    )(crosstalk, *arrived)


def solution(mesh):
    return jax.shard_map(
        body,
        mesh=mesh,
        in_specs=(
            P("slab", None),
            P("slab", None),
            P(),
            P("slab", None),
            P("slab", "wav"),
            P("slab", "wav"),
            P("slab", "wav"),
            P(),
        ),
        out_specs=P("slab", "wav"),
        check_vma=False,
    )
```

time: 56.4 us -> 42.1 us (0.75)
  the two profiles are of different devices: /device:TPU:8 before, /device:TPU:0 now
where the time goes in v1:
time: 42.1 us; the launch traced here: 41.9 us
  starting transfers between devices  19.7 us (47%)
  Pallas kernels  15.3 us (36%)
  waiting for transfers between devices  5.97 us (14%)
  local copies, waits for them, and re-layouts  0.83 us (2%)
    ppermute x3, starting transfers between devices, body(): lax.ppermute(sent[k], 'wav', [(i, (i + 2 * k) % NWAV) for i in range(NWAV)])  5.73 us
    pallas_call x1, Pallas kernels, body(): call(detector_kernel, shape(256, 512), 1, 5, [pltpu.VMEM((NWAV, 24, 128),...  3.9 us
    ppermute x1, starting transfers between devices, body(): lax.ppermute(wrap, 'slab', [(4 * y, 4 * y + 4) for y in range(3)] + [(4 *...  3.47 us
    ppermute x1, starting transfers between devices, body(): partner = lax.ppermute(own, 'slab', along_y((3, 2, 1, 0)))  3.09 us
    pallas_call x1, Pallas kernels, body(): call(table_kernel, [shape(2, 4, 2 * UROWS, 256, dtype=BF16), shape(2, 2,...  2.76 us
    ppermute x3, waiting for transfers between devices, body(): lax.ppermute(sent[k], 'wav', [(i, (i + 2 * k) % NWAV) for i in range(NWAV)])  2.39 us
    pallas_call x1, Pallas kernels, body(): call(prepare_kernel, [shape(PIECE, 128), shape(PIECE + EDGE, 128), shape(...  2.31 us
    ppermute x1, starting transfers between devices, body(): p3 = lax.ppermute(down, 'slab', along_z(3))  2.2 us
  transfers between devices with their start and end apart: 12, of which 7 were waited for; matrix products, arithmetic and copies ran while one was open for 0% of the time, Pallas kernels for 12%

profile of v1, /device:TPU:0, one launch (start us, length us, event | category | flops | bytes accessed | tf_op | source)
XLA Modules:
  0.0 41.9 jit_solution(4625364818968215169)
XLA Ops:
  0.0 2.3 %prepare_kernel.1 = (f32[80,128]{1,0:T(8,128)}, f32[152,128]{1,0:T(8,128)}, f32[152,128]{1,0:T(8,128)}, f32[8,128]{1,0:T(8,128)}) custom-call(f32[32,512]{1,0:T(8,128)} %amp_in.1, s32[32,512]{1,0:T(8,128)} %seg_in.1, s32[3,798]{1,0:T(4,128)} %bitcast.1, f32[64,1024]{1,0:T(8,128)} %mask.3, s32[8,16]{1,0:T(8,128)} %trow.1, s32[8,16]{1,0:T(8,128)} %tcol.1, ...), custom_call_target="tpu_custom_call" | custom-call | tf_op jit(solution)/shard_map/prepare_kernel/pallas_call | solution.py:451
  2.3 0.0 copy-start
  2.3 2.1 %collective-permute-start = (f32[152,128]{1,0:T(8,128)}, f32[152,128]{1,0:T(8,128)S(1)}, u32[]{:S(2)}, u32[]{:S(2)}) collective-permute-start(f32[152,128]{1,0:T(8,128)} %get-tuple-element.25), channel_id=1, source_target_pairs={{0,1},{1,2},{2,3},{3,0},{4,5},{5,6},{6,7},{7,4},{8,9},{9,10},{10,1... | collective-permute-start | bytes 233480 | tf_op jit(solution)/shard_map/ppermute | solution.py:478
  4.4 2.2 %collective-permute-start.2 = (f32[152,128]{1,0:T(8,128)}, f32[152,128]{1,0:T(8,128)S(1)}, u32[]{:S(2)}, u32[]{:S(2)}) collective-permute-start(f32[152,128]{1,0:T(8,128)} %get-tuple-element.26), channel_id=1, source_target_pairs={{0,3},{1,0},{2,1},{3,2},{4,7},{5,4},{6,5},{7,6},{8,11},{9,8},{10,9... | collective-permute-start | bytes 233480 | tf_op jit(solution)/shard_map/ppermute | solution.py:479
  6.6 1.8 %collective-permute-start.1 = (f32[80,128]{1,0:T(8,128)}, f32[80,128]{1,0:T(8,128)S(1)}, u32[]{:S(2)}, u32[]{:S(2)}) collective-permute-start(f32[80,128]{1,0:T(8,128)} %get-tuple-element.24.after.p0), channel_id=1, source_target_pairs={{0,2},{1,3},{2,0},{3,1},{4,6},{5,7},{6,4},{7,5},{8,10},{9,11},{10,... | collective-permute-start | bytes 122888 | tf_op jit(solution)/shard_map/ppermute | solution.py:480
  8.4 0.0 copy-start.1
  8.4 0.8 %copy-done.1 = f32[80,128]{1,0:T(8,128)S(1)} copy-done((f32[80,128]{1,0:T(8,128)S(1)}, f32[80,128]{1,0:T(8,128)}, u32[]{:S(2)}) %copy-start.1) | copy-done | bytes 40984
  9.2 0.0 copy-start.3
  9.2 2.8 %table_kernel.1 = (bf16[2,4,160,256]{3,2,1,0:T(8,128)(2,1)S(1)}, bf16[2,2,2,256,512]{4,3,2,1,0:T(8,128)(2,1)S(1)}, bf16[1024,256]{1,0:T(8,128)(2,1)S(1)}) custom-call(f32[80,128]{1,0:T(8,128)S(1)} %copy-done.1), custom_call_target="tpu_custom_call" | custom-call | tf_op jit(solution)/shard_map/table_kernel/pallas_call | solution.py:467
  12.0 0.4 collective-permute-done.1.p2
  12.3 0.0 collective-permute-done.p1
  12.3 0.0 collective-permute-done.2.p3
  12.3 0.1 merge_kernel.1
  12.4 3.1 %collective-permute-start.5 = (f32[2,136,128]{2,1,0:T(8,128)S(1)}, f32[2,136,128]{2,1,0:T(8,128)S(1)}, u32[]{:S(2)}, u32[]{:S(2)}) collective-permute-start(f32[2,136,128]{2,1,0:T(8,128)S(1)} %get-tuple-element.28.first), channel_id=1, source_target_pairs={{0,12},{1,13},{2,14},{3,15},{4,8},{5,9},{6,10},{7,11},{8,4},{9,5},... | collective-permute-start | bytes 417800 | tf_op jit(solution)/shard_map/ppermute | solution.py:484
  15.5 0.6 %collective-permute-start.4 = (f32[2,136,128]{2,1,0:T(8,128)S(1)}, f32[2,136,128]{2,1,0:T(8,128)S(1)}, u32[]{:S(2)}, u32[]{:S(2)}) collective-permute-start(f32[2,136,128]{2,1,0:T(8,128)S(1)} %get-tuple-element.28.first), channel_id=1, source_target_pairs={{0,8},{1,9},{2,10},{3,11},{4,12},{5,13},{6,14},{7,15},{8,0},{9,1},... | collective-permute-start | bytes 417800 | tf_op jit(solution)/shard_map/ppermute | solution.py:486
  16.2 0.5 %collective-permute-start.3 = (f32[2,136,128]{2,1,0:T(8,128)S(1)}, f32[2,136,128]{2,1,0:T(8,128)S(1)}, u32[]{:S(2)}, u32[]{:S(2)}) collective-permute-start(f32[2,136,128]{2,1,0:T(8,128)S(1)} %get-tuple-element.28.first), channel_id=1, source_target_pairs={{0,4},{1,5},{2,6},{3,7},{4,0},{5,1},{6,2},{7,3},{8,12},{9,13},{10,... | collective-permute-start | bytes 417800 | tf_op jit(solution)/shard_map/ppermute | solution.py:485
  16.6 3.5 %collective-permute-start.6 = (f32[72,128]{1,0:T(8,128)S(1)}, f32[72,128]{1,0:T(8,128)S(1)}, u32[]{:S(2)}, u32[]{:S(2)}) collective-permute-start(f32[72,128]{1,0:T(8,128)S(1)} %get-tuple-element.30), channel_id=1, source_target_pairs={{0,4},{4,8},{8,12},{7,3},{11,7},{15,11},{16,20},{20,24},{24,28},{2... | collective-permute-start | bytes 110600 | tf_op jit(solution)/shard_map/ppermute | solution.py:487
  20.1 0.2 collective-permute-done.5.second
  20.3 2.0 %first_kernel.1.before = f32[4,80,512]{2,1,0:T(8,128)S(1)} custom-call(f32[2,136,128]{2,1,0:T(8,128)S(1)} %get-tuple-element.28.first, f32[2,136,128]{2,1,0:T(8,128)S(1)} %collective-permute-done.5.second, bf16[2,4,160,256]{3,2,1,0:T(8,128)(2,1)S(1)} %get-tuple-element.29.utab), custom_call_target="tpu_custom_call" | custom-call | tf_op jit(solution)/shard_map/first_kernel/pallas_call | solution.py:491
  22.3 0.0 collective-permute-done.6.after.edge
  22.3 0.6 %collective-permute-done.4.second = f32[2,136,128]{2,1,0:T(8,128)S(1)} collective-permute-done((f32[2,136,128]{2,1,0:T(8,128)S(1)}, f32[2,136,128]{2,1,0:T(8,128)S(1)}, u32[]{:S(2)}, u32[]{:S(2)}) %collective-permute-start.4) | collective-permute-done | bytes 139296 | tf_op jit(solution)/shard_map/ppermute | solution.py:486
  22.9 0.0 collective-permute-done.3.first
  22.9 2.0 %second_kernel.1 = (f32[2,80,512]{2,1,0:T(8,128)S(1)}, f32[2,80,512]{2,1,0:T(8,128)S(1)}) custom-call(f32[2,136,128]{2,1,0:T(8,128)S(1)} %collective-permute-done.3.first, f32[2,136,128]{2,1,0:T(8,128)S(1)} %collective-permute-done.4.second, bf16[2,4,160,256]{3,2,1,0:T(8,128)(2,1)S(1)} %get-tuple-element.29.utab, f32[4,80,512]{2,1,0:T(8,128)S(1)} %first_kernel.1.before, ...), custom_call_target="tpu_custom_call" | custom-call | tf_op jit(solution)/shard_map/second_kernel/pallas_call | solution.py:492
  25.0 0.1 collective-permute-start.7
  25.0 0.0 copy-done
  25.1 0.0 copy-done.3
  25.1 0.0 copy-start.2
  25.1 0.3 weight_kernel.1
  25.4 1.3 %collective-permute-done.7.got = f32[2,80,512]{2,1,0:T(8,128)S(1)} collective-permute-done((f32[2,80,512]{2,1,0:T(8,128)S(1)}, f32[2,80,512]{2,1,0:T(8,128)S(1)}, u32[]{:S(2)}, u32[]{:S(2)}) %collective-permute-start.7) | collective-permute-done | bytes 327712 | tf_op jit(solution)/shard_map/ppermute | solution.py:499
  26.7 1.9 %lens_kernel.1 = (f32[4,24,128]{2,1,0:T(8,128)S(1)}, f32[4,24,128]{2,1,0:T(8,128)S(1)}) custom-call(f32[2,80,512]{2,1,0:T(8,128)S(1)} %get-tuple-element.31.keep, f32[2,80,512]{2,1,0:T(8,128)S(1)} %collective-permute-done.7.got, bf16[2,2,2,256,512]{4,3,2,1,0:T(8,128)(2,1)S(1)} %get-tuple-element.33.vtab, f32[80,1024]{1,0:T(8,128)S(1)} %get-tuple-element.35.weight, ...), custom_call_target="tpu_custom_call" | custom-call | tf_op jit(solution)/shard_map/lens_kernel/pallas_call | solution.py:500
  28.5 0.2 collective-permute-start.8
  28.8 1.1 %collective-permute-done.8.got = f32[4,24,128]{2,1,0:T(8,128)S(1)} collective-permute-done((f32[4,24,128]{2,1,0:T(8,128)S(1)}, f32[4,24,128]{2,1,0:T(8,128)S(1)}, u32[]{:S(2)}, u32[]{:S(2)}) %collective-permute-start.8) | collective-permute-done | bytes 49184 | tf_op jit(solution)/shard_map/ppermute | solution.py:503
  29.9 1.6 %collective-permute-start.9 = (f32[2,24,128]{2,1,0:T(8,128)S(1)}, f32[2,24,128]{2,1,0:T(8,128)S(1)}, u32[]{:S(2)}, u32[]{:S(2)}) collective-permute-start(f32[2,24,128]{2,1,0:T(8,128)S(1)} %get-tuple-element.40), channel_id=1, source_target_pairs={{0,32},{16,48},{32,64},{48,80},{64,96},{80,112},{96,0},{112,16},{1... | collective-permute-start | bytes 73736 | tf_op jit(solution)/shard_map/ppermute | solution.py:506
  31.4 2.7 %collective-permute-start.10 = (f32[2,24,128]{2,1,0:T(8,128)S(1)}, f32[2,24,128]{2,1,0:T(8,128)S(1)}, u32[]{:S(2)}, u32[]{:S(2)}) collective-permute-start(f32[2,24,128]{2,1,0:T(8,128)S(1)} %get-tuple-element.41), channel_id=1, source_target_pairs={{0,64},{16,80},{32,96},{48,112},{64,0},{80,16},{96,32},{112,48},{1... | collective-permute-start | bytes 73736 | tf_op jit(solution)/shard_map/ppermute | solution.py:506
  34.2 1.4 %collective-permute-start.11 = (f32[2,24,128]{2,1,0:T(8,128)S(1)}, f32[2,24,128]{2,1,0:T(8,128)S(1)}, u32[]{:S(2)}, u32[]{:S(2)}) collective-permute-start(f32[2,24,128]{2,1,0:T(8,128)S(1)} %get-tuple-element.42), channel_id=1, source_target_pairs={{0,96},{16,112},{32,0},{48,16},{64,32},{80,48},{96,64},{112,80},{1... | collective-permute-start | bytes 73736 | tf_op jit(solution)/shard_map/ppermute | solution.py:506
  35.6 0.0 collective-permute-done.9.a1
  35.6 1.2 %collective-permute-done.10.a2 = f32[2,24,128]{2,1,0:T(8,128)S(1)} collective-permute-done((f32[2,24,128]{2,1,0:T(8,128)S(1)}, f32[2,24,128]{2,1,0:T(8,128)S(1)}, u32[]{:S(2)}, u32[]{:S(2)}) %collective-permute-start.10) | collective-permute-done | bytes 24608 | tf_op jit(solution)/shard_map/ppermute | solution.py:506
  36.8 1.2 %collective-permute-done.11.a3 = f32[2,24,128]{2,1,0:T(8,128)S(1)} collective-permute-done((f32[2,24,128]{2,1,0:T(8,128)S(1)}, f32[2,24,128]{2,1,0:T(8,128)S(1)}, u32[]{:S(2)}, u32[]{:S(2)}) %collective-permute-start.11) | collective-permute-done | bytes 24608 | tf_op jit(solution)/shard_map/ppermute | solution.py:506
  38.0 0.0 copy-done.2
  38.0 3.9 %detector_kernel.1 = f32[256,512]{1,0:T(8,128)} custom-call(f32[5,5]{1,0:T(8,128)S(1)} %copy-done.2, f32[2,24,128]{2,1,0:T(8,128)S(1)} %get-tuple-element.39.a0, f32[2,24,128]{2,1,0:T(8,128)S(1)} %collective-permute-done.9.a1, f32[2,24,128]{2,1,0:T(8,128)S(1)} %collective-permute-done.10.a2, f32[2,24,128]{2,1,0:T(8,128)S(1)} %collective-permute-done.11.a3), custom_call_target="tpu_custom_call" | custom-call | tf_op jit(solution)/shard_map/detector_kernel/pallas_call | solution.py:508
  (1 shorter events, 0.0 us)
Async XLA Ops:
  2.3 22.7 %copy-start = (f32[64,1024]{1,0:T(8,128)S(1)}, f32[64,1024]{1,0:T(8,128)}, u32[]{:S(2)}) copy-start(f32[64,1024]{1,0:T(8,128)} %mask.3) | copy-start | bytes 786436
  2.3 10.0 %collective-permute-start = (f32[152,128]{1,0:T(8,128)}, f32[152,128]{1,0:T(8,128)S(1)}, u32[]{:S(2)}, u32[]{:S(2)}) collective-permute-start(f32[152,128]{1,0:T(8,128)} %get-tuple-element.25), channel_id=1, source_target_pairs={{0,1},{1,2},{2,3},{3,0},{4,5},{5,6},{6,7},{7,4},{8,9},{9,10},{10,1... | collective-permute-start | bytes 233480 | tf_op jit(solution)/shard_map/ppermute | solution.py:478
  4.4 7.9 %collective-permute-start.2 = (f32[152,128]{1,0:T(8,128)}, f32[152,128]{1,0:T(8,128)S(1)}, u32[]{:S(2)}, u32[]{:S(2)}) collective-permute-start(f32[152,128]{1,0:T(8,128)} %get-tuple-element.26), channel_id=1, source_target_pairs={{0,3},{1,0},{2,1},{3,2},{4,7},{5,4},{6,5},{7,6},{8,11},{9,8},{10,9... | collective-permute-start | bytes 233480 | tf_op jit(solution)/shard_map/ppermute | solution.py:479
  6.6 5.7 %collective-permute-start.1 = (f32[80,128]{1,0:T(8,128)}, f32[80,128]{1,0:T(8,128)S(1)}, u32[]{:S(2)}, u32[]{:S(2)}) collective-permute-start(f32[80,128]{1,0:T(8,128)} %get-tuple-element.24.after.p0), channel_id=1, source_target_pairs={{0,2},{1,3},{2,0},{3,1},{4,6},{5,7},{6,4},{7,5},{8,10},{9,11},{10,... | collective-permute-start | bytes 122888 | tf_op jit(solution)/shard_map/ppermute | solution.py:480
  8.4 0.8 %copy-start.1 = (f32[80,128]{1,0:T(8,128)S(1)}, f32[80,128]{1,0:T(8,128)}, u32[]{:S(2)}) copy-start(f32[80,128]{1,0:T(8,128)} %get-tuple-element.24.after.p0) | copy-start | bytes 122884
  9.2 15.9 %copy-start.3 = (f32[8,128]{1,0:T(8,128)S(1)}, f32[8,128]{1,0:T(8,128)}, u32[]{:S(2)}) copy-start(f32[8,128]{1,0:T(8,128)} %get-tuple-element.34.trace) | copy-start | bytes 12292
  12.4 7.9 %collective-permute-start.5 = (f32[2,136,128]{2,1,0:T(8,128)S(1)}, f32[2,136,128]{2,1,0:T(8,128)S(1)}, u32[]{:S(2)}, u32[]{:S(2)}) collective-permute-start(f32[2,136,128]{2,1,0:T(8,128)S(1)} %get-tuple-element.28.first), channel_id=1, source_target_pairs={{0,12},{1,13},{2,14},{3,15},{4,8},{5,9},{6,10},{7,11},{8,4},{9,5},... | collective-permute-start | bytes 417800 | tf_op jit(solution)/shard_map/ppermute | solution.py:484
  15.5 7.4 %collective-permute-start.4 = (f32[2,136,128]{2,1,0:T(8,128)S(1)}, f32[2,136,128]{2,1,0:T(8,128)S(1)}, u32[]{:S(2)}, u32[]{:S(2)}) collective-permute-start(f32[2,136,128]{2,1,0:T(8,128)S(1)} %get-tuple-element.28.first), channel_id=1, source_target_pairs={{0,8},{1,9},{2,10},{3,11},{4,12},{5,13},{6,14},{7,15},{8,0},{9,1},... | collective-permute-start | bytes 417800 | tf_op jit(solution)/shard_map/ppermute | solution.py:486
  16.2 6.8 %collective-permute-start.3 = (f32[2,136,128]{2,1,0:T(8,128)S(1)}, f32[2,136,128]{2,1,0:T(8,128)S(1)}, u32[]{:S(2)}, u32[]{:S(2)}) collective-permute-start(f32[2,136,128]{2,1,0:T(8,128)S(1)} %get-tuple-element.28.first), channel_id=1, source_target_pairs={{0,4},{1,5},{2,6},{3,7},{4,0},{5,1},{6,2},{7,3},{8,12},{9,13},{10,... | collective-permute-start | bytes 417800 | tf_op jit(solution)/shard_map/ppermute | solution.py:485
  16.6 5.7 %collective-permute-start.6 = (f32[72,128]{1,0:T(8,128)S(1)}, f32[72,128]{1,0:T(8,128)S(1)}, u32[]{:S(2)}, u32[]{:S(2)}) collective-permute-start(f32[72,128]{1,0:T(8,128)S(1)} %get-tuple-element.30), channel_id=1, source_target_pairs={{0,4},{4,8},{8,12},{7,3},{11,7},{15,11},{16,20},{20,24},{24,28},{2... | collective-permute-start | bytes 110600 | tf_op jit(solution)/shard_map/ppermute | solution.py:487
  25.0 1.7 %collective-permute-start.7 = (f32[2,80,512]{2,1,0:T(8,128)S(1)}, f32[2,80,512]{2,1,0:T(8,128)S(1)}, u32[]{:S(2)}, u32[]{:S(2)}) collective-permute-start(f32[2,80,512]{2,1,0:T(8,128)S(1)} %get-tuple-element.32.after), channel_id=1, source_target_pairs={{0,16},{16,0},{32,48},{48,32},{64,80},{80,64},{96,112},{112,96},{1... | collective-permute-start | bytes 983048 | tf_op jit(solution)/shard_map/ppermute | solution.py:499
  25.1 12.9 %copy-start.2 = (f32[5,5]{1,0:T(8,128)S(1)}, f32[5,5]{1,0:T(8,128)}, u32[]{:S(2)}) copy-start(f32[5,5]{1,0:T(8,128)} %kernel.1) | copy-start | bytes 304
  28.5 1.3 %collective-permute-start.8 = (f32[4,24,128]{2,1,0:T(8,128)S(1)}, f32[4,24,128]{2,1,0:T(8,128)S(1)}, u32[]{:S(2)}, u32[]{:S(2)}) collective-permute-start(f32[4,24,128]{2,1,0:T(8,128)S(1)} %get-tuple-element.38), channel_id=1, source_target_pairs={{0,16},{16,0},{32,48},{48,32},{64,80},{80,64},{96,112},{112,96},{1... | collective-permute-start | bytes 147464 | tf_op jit(solution)/shard_map/ppermute | solution.py:503
  29.9 5.7 %collective-permute-start.9 = (f32[2,24,128]{2,1,0:T(8,128)S(1)}, f32[2,24,128]{2,1,0:T(8,128)S(1)}, u32[]{:S(2)}, u32[]{:S(2)}) collective-permute-start(f32[2,24,128]{2,1,0:T(8,128)S(1)} %get-tuple-element.40), channel_id=1, source_target_pairs={{0,32},{16,48},{32,64},{48,80},{64,96},{80,112},{96,0},{112,16},{1... | collective-permute-start | bytes 73736 | tf_op jit(solution)/shard_map/ppermute | solution.py:506
  31.4 5.3 %collective-permute-start.10 = (f32[2,24,128]{2,1,0:T(8,128)S(1)}, f32[2,24,128]{2,1,0:T(8,128)S(1)}, u32[]{:S(2)}, u32[]{:S(2)}) collective-permute-start(f32[2,24,128]{2,1,0:T(8,128)S(1)} %get-tuple-element.41), channel_id=1, source_target_pairs={{0,64},{16,80},{32,96},{48,112},{64,0},{80,16},{96,32},{112,48},{1... | collective-permute-start | bytes 73736 | tf_op jit(solution)/shard_map/ppermute | solution.py:506
  34.2 3.8 %collective-permute-start.11 = (f32[2,24,128]{2,1,0:T(8,128)S(1)}, f32[2,24,128]{2,1,0:T(8,128)S(1)}, u32[]{:S(2)}, u32[]{:S(2)}) collective-permute-start(f32[2,24,128]{2,1,0:T(8,128)S(1)} %get-tuple-element.42), channel_id=1, source_target_pairs={{0,96},{16,112},{32,0},{48,16},{64,32},{80,48},{96,64},{112,80},{1... | collective-permute-start | bytes 73736 | tf_op jit(solution)/shard_map/ppermute | solution.py:506

commit v2 on v1

--- a/solution.py
+++ b/solution.py
@@ -1,4 +1,5 @@
 import functools
+import math
 
 import jax
 import jax.numpy as jnp
@@ -20,8 +21,7 @@
 MROWS = GROUP + 8
 HALF, FHALF = NP // 2, NF // 2
 
-SIN = (6.283185302511503, -41.34170040531721, 81.6051313857832, -76.70301535364747,
-       42.02592698447418, -14.899846663536497, 3.2381375046186873)
+SIN = (6.283184916495428, -41.34158923268831, 81.59994332977429, -76.61447253115396, 41.34288235413569, -12.471243534350362)
 COS = (0.9999999890590228, -19.73920449945383, 64.93911745989081, -85.45013953079767,
        60.167630950263465, -25.967599245923743, 6.52865815775625)
 
@@ -56,9 +56,16 @@
     t = turns - jnp.round(turns)
     z = t * t
     s, c = SIN[-1], COS[-1]
-    for a, b in zip(SIN[-2::-1], COS[-2::-1]):
-        s, c = s * z + a, c * z + b
+    for a in SIN[-2::-1]:
+        s = s * z + a
+    for b in COS[-2::-1]:
+        c = c * z + b
     return s * t, c
+
+
+def focal_row(s, shape):
+    a = iota(shape, 0)
+    return FROWS * s + jnp.where(a < FROWS, a, jnp.where(a < FROWS + 8, a - FROWS - 8, a - 8))
 
 
 def reversal(n):
@@ -146,50 +153,63 @@
     return jnp.full((1, 1), 1000 + w, I32).astype(F32)
 
 
-def angle(m, n, w):
+def slope(n, w):
     lam = wavelength(w)
     short = jnp.round(250.0 / lam * 2.0**14) * 2.0**-14
     rest = (250.0 - short * lam) / lam
-    product = m * n
-    a, b = (product >> 10).astype(F32), (product & 1023).astype(F32)
-    t = a * short
+    whole = n * (short * 2.0**-10)
+    high = jnp.round(whole * 2.0**13) * 2.0**-13
+    return high, (whole - high) + n * (rest * 2.0**-10)
+
+
+def angle(m, step):
+    t = m * step[0]
     t = t - jnp.round(t)
-    return sincos(t + a * rest + b * (250.0 / 1024.0 / lam))
-
-
-def table_kernel(after, utab, vtab, smat):
+    return sincos(t + m * step[1])
+
+
+def odd(index, count):
+    return (2 * index + 1 - count).astype(F32)
+
+
+def focal_table_kernel(after, utab):
     del after
     w, s, y, z, x, core, sign, pair = place_of()
-    for m in range(4):
-        wave = 2 * (w if m < 2 else w ^ 1) + (m & 1)
+    m = odd(focal_row(s, (UROWS, GROUP)), NF)
+    rho = iota((1, GROUP), 1)
+    for k in range(4):
+        wave = 2 * (w if k < 2 else w ^ 1) + (k & 1)
         for p in range(2):
             g = pair if p == 0 else 1 - pair
-            u = 64 * s - 8 + iota((UROWS, GROUP), 0)
-            rho = iota((UROWS, GROUP), 1)
-            i = 128 * g + 16 * (rho & 7) + (rho >> 3)
-            sin, cos = angle(2 * u + 1 - NF, 2 * i + 1 - NP, wave)
+            sin, cos = angle(m, slope(odd(128 * g + 16 * (rho & 7) + (rho >> 3), NP), wave))
             for at, part in ((0, cos), (GROUP, sin * sign)):
                 high, low = split2(part)
-                utab[p, m, 0:UROWS, at:at + GROUP] = high
-                utab[p, m, UROWS:2 * UROWS, at:at + GROUP] = low
-
-        if m >= 2:
-            continue
-
-        def chunk(c, carry, m=m, wave=wave):
+                utab[p, k, 0:UROWS, at:at + GROUP] = high
+                utab[p, k, UROWS:2 * UROWS, at:at + GROUP] = low
+
+
+def lens_table_kernel(after, vtab, smat):
+    del after
+    w, s, y, z, x, core, sign, pair = place_of()
+    m = odd(iota((16, 128), 1), NF)
+    for k in range(2):
+
+        def chunk(c, carry, k=k):
             j0 = pl.multiple_of(16 * c, 16)
-            j = ((j0 + 128 * core) & 255) + iota((16, FHALF), 0)
-            v = iota((16, FHALF), 1)
-            sin, cos = angle(2 * v + 1 - NF, 2 * j + 1 - NP, wave)
-            for q, part in ((0, cos), (1, sin)):
-                high, low = split2(part)
-                vtab[m, q, 0, pl.ds(j0, 16), :] = high
-                vtab[m, q, 1, pl.ds(j0, 16), :] = low
+            step = slope(odd(((j0 + 128 * core) & 255) + iota((16, 128), 0), NP), 2 * w + k)
+            sin, cos = angle(m, step)
+            turn_im, turn_re = angle(jnp.full((16, 128), 256.0, F32), step)
+            for t in range(4):
+                for q, part in ((0, cos), (1, sin)):
+                    high, low = split2(part)
+                    vtab[k, q, 0, pl.ds(j0, 16), 128 * t:128 * t + 128] = high
+                    vtab[k, q, 1, pl.ds(j0, 16), 128 * t:128 * t + 128] = low
+                cos, sin = cos * turn_re - sin * turn_im, cos * turn_im + sin * turn_re
             return carry
 
         lax.fori_loop(0, HALF // 16, chunk, 0)
     row, lane = iota((FHALF, 256), 0), iota((FHALF, 256), 1)
-    column = 2 * ((x + (lane >> 5)) & 3) + jnp.where(lane < 128, core, 1 - core)
+    column = 2 * ((lane >> 5) & 3) + jnp.where(lane < 128, core, 1 - core)
     lens = jnp.where((lane & 31) < 18, 16 * column - 1 + (lane & 31), -1)
     smat[0:FHALF, :] = (lens == row >> 3).astype(BF16)
     smat[FHALF:NF, :] = (lens == NL - 1 - (row >> 3)).astype(BF16)
@@ -204,13 +224,13 @@
     lenses[8:9, :] = above[64:65]
     lenses[9:10, :] = below[64:65]
     lenses[10:16, :] = jnp.zeros((6, 128), F32)
-    u = 64 * s - 8 + iota((UROWS, FHALF), 0)
+    u = focal_row(s, (UROWS, FHALF))
     v = iota((UROWS, FHALF), 1)
     down, across = (2 * u + 1 - NF).astype(F32) * 0.5, (2 * v + 1 - NF).astype(F32) * 0.5
     fade = 1.0 - jnp.exp((down * down + across * across) * (-1.0 / 1024.0))
     rev = reversal(256)
     above, below = (jnp.concatenate([ref[8 * q:8 * q + 8] for q in range(8)], axis=1) for ref in (above, below))
-    full = jnp.concatenate([above, mask[...], below], axis=0)
+    full = jnp.concatenate([mask[...], above, below], axis=0)
     t = full[:, :FHALF] * fade
     weight[:, :FHALF] = t * t * 2.0**-24
     for q in range(2):
@@ -252,7 +272,7 @@
 
         step_im, step_re = four(turn, 0), four(turn, 1)
 
-        def rows(r2, carry, step_im=step_im, step_re=step_re):
+        def rows(r2, carry, m=m, step_im=step_im, step_re=step_re):
             re, im = carry
             found = [[] for _ in range(8)]
             for h in range(2):
@@ -263,11 +283,11 @@
                         a = ref[side, pl.ds(r0, 8), :]
                         qre.append(a * re[2 * t + side])
                         qim.append(a * im[2 * t + side])
-                (fl, fr, sl, sr), (gl, gr, hl, hr) = qre, qim
-                a, b, c, d = fl + sl, sl - fl, fr + sr, sr - fr
-                e, f, k, n = gl + hl, gl - hl, gr + hr, gr - hr
-                for q, value in enumerate((a + c, e + k, e - k, c - a, f + n, b + d, b - d, n - f)):
-                    found[q].append(value)
+                for side in range(2):
+                    found[2 * side].append(qre[side] + qre[2 + side])
+                    found[2 * side + 1].append(qim[side] + qim[2 + side])
+                    found[4 + 2 * side].append(qim[side] - qim[2 + side])
+                    found[5 + 2 * side].append(qre[2 + side] - qre[side])
                 re, im = (
                     [x * p - y * q for x, y, p, q in zip(re, im, step_re, step_im)],
                     [x * q + y * p for x, y, p, q in zip(re, im, step_re, step_im)],
@@ -276,18 +296,19 @@
                 high, low = split2(jnp.concatenate(values, axis=0))
                 r0 = pl.multiple_of(16 * r2 + (GROUP if q >= 4 else 0), 16)
                 c0 = 128 * (q & 3)
-                whi[pl.ds(r0, 16), c0:c0 + 128] = high
-                wlo[pl.ds(r0, 16), c0:c0 + 128] = low
+                whi[m, pl.ds(r0, 16), c0:c0 + 128] = high
+                wlo[m, pl.ds(r0, 16), c0:c0 + 128] = low
             return re, im
 
-        lax.fori_loop(0, 8, rows, (four(start, 1), four(start, 0)))
+        lax.fori_loop(0, 8, rows, (four(start, 1), four(start, 0)), unroll=True)
         table = utab[p, m]
-        both = dot(table, whi[...])
-        fields.append(both[:UROWS] + both[UROWS:] + dot(table[:UROWS], wlo[...]))
+        both = dot(table, whi[m])
+        fields.append(both[:UROWS] + both[UROWS:] + dot(table[:UROWS], wlo[m]))
     return fields
 
 
-def first_kernel(first, second, utab, out, whi, wlo):
+def first_kernel(first, second, utab, after, out, whi, wlo):
+    del after
     for m, field in enumerate(pair_fields(first, second, utab, 0, whi, wlo)):
         out[m] = field
 
@@ -299,13 +320,11 @@
 
 
 def lens_kernel(keep, got, vtab, weight, smat, lenses, mine, other):
-    mine[...] = jnp.zeros(mine.shape, F32)
-    other[...] = jnp.zeros(other.shape, F32)
-    outs = [ref.at[k] for ref in (mine, other) for k in range(4)]
     for m in range(2):
-        parts = [
+        lre, lim, rre, rim = (
             jnp.concatenate([ref[m, :, 128 * q:128 * q + 128] for ref in (keep, got)], axis=1) for q in range(4)
-        ]
+        )
+        parts = [lre + rre, lim + rim, lim - rim, rre - lre]
         terms = []
         for q in range(2):
             side = jnp.concatenate(parts[2 * q:2 * q + 2], axis=0)
@@ -317,107 +336,110 @@
             re, im = value[:UROWS], value[UROWS:]
             power = (re * re + im * im) * weight[:, FHALF * q:FHALF * (q + 1)]
             summed = jnp.sum(power.reshape(UROWS // 8, 8, FHALF), axis=1)
-            for part in split3(summed):
+            for part in split2(summed):
                 lens = lens + dot(part, smat[FHALF * q:FHALF * (q + 1), :])
-        for d in range(NWAV):
-            outs[d][10 * m:10 * m + 10, 0:32] = lens[:, 32 * d:32 * d + 32]
-    tables = lenses[0:10, 0:48]
-    for out in outs:
-        out[0:10, 32:80] = tables
-
-
-def pack_kernel(mine, got, *outs):
-    for k, out in enumerate(outs):
-        out[0] = mine[k]
-        out[1] = got[k]
-
-
-TILES = 4 * 8 + 2
+        for k, out in enumerate((mine, other)):
+            out[16 * m:16 * m + 10, :] = lens[:, 128 * k:128 * k + 128]
+            out[16 * m + 10:16 * m + 16, :] = jnp.zeros((6, 128), F32)
+    row, lane = iota((128, 128), 0), iota((128, 128), 1) & 31
+    spot = ((lane >= 18) & (lane < 21) & (row == 16 * (lane - 18) + 15)) | ((lane >= 21) & (lane < 24) & (row == 16 * (lane - 21)))
+    sides = dot(lenses[...].astype(BF16), spot.astype(BF16))
+    for out in (mine, other):
+        out[0:16, :] += sides
+
+
+def pack_kernel(mine, got, after, *outs, shifts):
+    w, s, y, z, x, core, sign, pair = place_of()
+    lane = iota((16, 128), 1) >> 5
+    for out, k in zip(outs, shifts):
+        at = (x + k) & 3
+        packed = 0.0
+        for c in range(2):
+            rows = jnp.where(core == c, mine[...], got[...])
+            for m in range(2):
+                moved = pltpu.roll(rows[16 * m:16 * m + 16], (32 * (2 * c + m - at)) & 127, 1)
+                packed = jnp.where(lane == 2 * c + m, moved, packed)
+        out[...] = packed
 
 
 def order(a):
     return a - 1 if 0 < a < 9 else 8 + a // 9
 
 
-def detector_kernel(kernel, a0, a1, a2, a3, out, arrived, spec, trace, sums, aq, bq, hp):
+def detector_kernel(kernel, a0, a1, a2, a3, lenses, out, arrived, base, across, image, sems):
     w, s, y, z, x, core, sign, pair = place_of()
     for k, ref in enumerate((a0, a1, a2, a3)):
-        source = 2 * ((x - k + 4) & 3)
-        arrived[source + core] = ref[0]
-        arrived[source + 1 - core] = ref[1]
-    lane = iota((24, 128), 1)
-    prev, own, nxt = arrived[jnp.maximum(w - 1, 0)], arrived[w], arrived[jnp.minimum(w + 1, NWAV - 1)]
-    spot = (iota((128, 640), 0) == iota((128, 640), 1) >> 5).astype(BF16)
-    rows = arrived[...].reshape(NWAV * 24, 128)
-    wide = sum(dot(part, spot) for part in split3(rows))
-    for t in range(5):
-        spec[t] = wide[:, 128 * t:128 * t + 128]
+        for c in range(4):
+            arrived[4 * ((x - k + 4) & 3) + c] = ref[...] if c == 0 else pltpu.roll(ref[...], 128 - 32 * c, 1)
+    spot = (iota((128, 640), 0) == (iota((128, 640), 1) >> 5)) & (iota((128, 640), 1) < 18 * DPIX)
+    spot = spot.astype(BF16)
+    left, own, right = arrived[jnp.maximum(2 * w - 2, 0)], lenses[...], arrived[jnp.minimum(2 * w + 2, WAVES - 1)]
+    lane = iota((16, 128), 1)
     tables = []
     for c in range(3):
         tables.append(
             jnp.where(
                 lane == 0,
-                pltpu.roll(prev, 128 - (47 + 16 * c), 1),
-                jnp.where(
-                    lane < 17,
-                    pltpu.roll(own, 128 - (31 + 16 * c), 1),
-                    jnp.where(lane == 17, pltpu.roll(nxt, 128 - (15 + 16 * c), 1), 0.0),
-                ),
+                pltpu.roll(left, 128 - 18 - c, 1),
+                jnp.where(lane == 17, pltpu.roll(right, 128 - 4 - c, 1), pltpu.roll(own, 129 - 16 * c if c else 1, 1)),
             )
         )
-    trace[...] = dot(jnp.concatenate(tables, axis=0).astype(BF16), spot)
-    place = (iota((8, 640), 1) & 31).astype(F32)
-    wave = 2.0 * iota((8, 640), 0).astype(F32)
-    sums[...] = jnp.zeros(sums.shape, F32)
-    for a in range(10):
-        at = order(a)
-        offset = place - trace[24 + at:25 + at, :]
-        count = trace[48 + at:49 + at, :]
-        spread = 0.0
-        for m in range(2):
-            value = jnp.concatenate([spec[t, pl.ds(10 * m + a, NWAV, stride=24), :] for t in range(5)], axis=1)
-            along = jnp.exp(-0.5 * jnp.abs(offset - (wave + m)))
-            spread = spread + jnp.where(wave + m < count, value, 0.0) * along
-        sums[at:at + 1, :] = jnp.sum(spread, axis=0, keepdims=True)
-    row = trace[0:16, :] * 0.25
-    total = sums[...]
-    falling, rising = total * jnp.exp(row), total * jnp.exp(-row)
-    for q in range(5):
-        aq[q] = pltpu.roll(falling, 640 - (30 + q), 1)[:, 0:512]
-        bq[q] = pltpu.roll(rising, 640 - (30 + q), 1)[:, 0:512]
-    weights = [[kernel[p, q] + (1.0 if p == q == 2 else 0.0) for q in range(5)] for p in range(5)]
-    depth = iota((8, 128), 0).astype(F32) * 0.25
-
-    def cell(a, tiles):
-        for lt in range(4):
-            at = slice(128 * lt, 128 * lt + 128)
-            if isinstance(a, int):
-                fall, rise = ([ref[q, order(a):order(a) + 1, at] for q in range(5)] for ref in (aq, bq))
-            else:
-                fall, rise = ([pltpu.roll(ref[q, 0:8, at], 9 - a, 0)[0:1] for q in range(5)] for ref in (aq, bq))
-            for rt in tiles:
-                down, up = jnp.exp(-(depth + 2.0 * rt)), jnp.exp(depth + 2.0 * rt)
-                raw = [jnp.minimum(down * f, up * r) for f, r in zip(fall, rise)]
-                r0 = pl.multiple_of(8 * (4 * a + rt - 3), 8)
-                for p in range(5):
-                    h = raw[0] * weights[p][0]
-                    for q in range(1, 5):
-                        h = h + raw[q] * weights[p][q]
-                    hp[p, pl.ds(r0, 8), at] = h
-
-    cell(0, (3,))
-    cell(9, (0,))
-
-    def middle(a, carry):
-        cell(a, range(4))
-        return carry
-
-    lax.fori_loop(1, 9, middle, 0)
-    for r in range(0, 256, 8):
-        out[r:r + 8, :] = sum(hp[p, r + 6 + p:r + 14 + p, :] for p in range(5))
-
-
-def call(kernel, outs, in_smem, n_in, scratch=(), tail=(), limit=40):
+    wide = dot(jnp.concatenate(tables, axis=0).astype(BF16), spot)
+    row, column, count = wide[0:16] * 0.25, wide[16:32], wide[32:48]
+    values = sum(dot(part, spot) for part in split2(arrived[...].reshape(WAVES * 16, 128)))
+    offset = 0.5 * ((iota((16, 640), 1) & 31).astype(F32) - column)
+    falling, rising = jnp.exp(-offset), jnp.exp(offset)
+    spread = 0.0
+    for wave in range(WAVES):
+        value = values[16 * wave:16 * wave + 16]
+        along = jnp.minimum(falling * math.exp(0.5 * wave), rising * math.exp(-0.5 * wave))
+        spread = spread + jnp.where(count > wave, value, 0.0) * along
+    within = iota((16, 512), 1) & 31
+    moved = [pltpu.roll(spread, 640 - (30 + q), 1)[:, 0:512] for q in range(5)]
+    inside = [(within + q - 2 >= 0) & (within + q - 2 < DPIX) for q in range(5)]
+    own = [jnp.where(i, v, 0.0) for i, v in zip(inside, moved)]
+    beside = [jnp.where(i, 0.0, v) for i, v in zip(inside, moved)]
+    for p in range(5):
+        weights = [kernel[p:p + 1, q:q + 1] + (1.0 if p == q == 2 else 0.0) for q in range(5)]
+        base[p] = sum(v * k for v, k in zip(own, weights))
+        base[5 + p] = sum(v * k for q, (v, k) in enumerate(zip(beside, weights)) if q != 2)
+    near = row[:, DPIX:DPIX + 512]
+    far = jnp.where(within < 2, pltpu.roll(row, 640 - 30, 1)[:, 0:512], pltpu.roll(row, 640 - 34, 1)[:, 0:512])
+    for k, value in enumerate((near, -near, far, -far)):
+        across[k] = jnp.exp(value)
+    sub = iota((8, 128), 0)
+    depth = sub.astype(F32) * 0.25
+    downs = [jnp.exp(-(depth + 2.0 * t)) for t in range(4)]
+    ups = [jnp.exp(depth + 2.0 * t) for t in range(4)]
+    copies = []
+    for lt in range(4):
+        at = slice(128 * lt, 128 * lt + 128)
+        state = None
+        for a in range(10):
+            r = order(a)
+            scale = [base[p, r:r + 1, at] for p in range(10)]
+            fall, rise, fall_far, rise_far = (across[k, r:r + 1, at] for k in range(4))
+            for t in (3,) if a == 0 else (0,) if a == 9 else range(4):
+                one = jnp.minimum(downs[t] * fall, ups[t] * rise)
+                two = jnp.minimum(downs[t] * fall_far, ups[t] * rise_far)
+                h = [one * scale[p] + two * scale[5 + p] for p in range(5)]
+                if state is not None:
+                    part, h0, h1, h3, h4 = state
+                    done = part + pltpu.roll(jnp.where(sub == 0, h[3], h3), 7, 0)
+                    done = done + pltpu.roll(jnp.where(sub < 2, h[4], h4), 6, 0)
+                    image[lt, 8 * (4 * a + t - 4):8 * (4 * a + t - 4) + 8, :] = done
+                    part = h[2] + pltpu.roll(jnp.where(sub >= 6, h0, h[0]), 2, 0)
+                    part = part + pltpu.roll(jnp.where(sub == 7, h1, h[1]), 1, 0)
+                else:
+                    part = h[2]
+                state = part, h[0], h[1], h[3], h[4]
+        copies.append(pltpu.make_async_copy(image.at[lt, 8:264, :], out.at[:, at], sems.at[lt]))
+        copies[-1].start()
+    for copy in copies:
+        copy.wait()
+
+
+def call(kernel, outs, in_smem, n_in, scratch=(), tail=(), limit=40, outside=False):
     specs = [pl.BlockSpec(memory_space=pltpu.SMEM)] * in_smem
     specs += [pl.BlockSpec(memory_space=pltpu.VMEM)] * (n_in - in_smem)
     specs[n_in - len(tail):] = tail
@@ -427,10 +449,10 @@
         kernel,
         out_shape=outs,
         in_specs=specs,
-        out_specs=vmem if single else [vmem] * len(outs),
+        out_specs=pl.BlockSpec(memory_space=pl.ANY) if outside else vmem if single else [vmem] * len(outs),
         scratch_shapes=list(scratch),
         compiler_params=pltpu.CompilerParams(vmem_limit_bytes=limit * 2**20),
-        name=kernel.__name__,
+        name=getattr(kernel, "func", kernel).__name__,
     )
 
 
@@ -464,31 +486,24 @@
         tail=anywhere * 7,
         limit=54,
     )(amplitude, seg_map, seg_table.T, focal_mask, trace_row, trace_col, block_count)
-    utab, vtab, smat = call(
-        table_kernel,
-        [
-            shape(2, 4, 2 * UROWS, 256, dtype=BF16),
-            shape(2, 2, 2, HALF, FHALF, dtype=BF16),
-            shape(NF, 256, dtype=BF16),
-        ],
-        0,
-        1,
-        tail=anywhere,
-    )(piece)
+    utab = call(focal_table_kernel, shape(2, 4, 2 * UROWS, 256, dtype=BF16), 0, 1, tail=anywhere)(piece)
     p1 = lax.ppermute(up, "slab", along_z(1))
     p3 = lax.ppermute(down, "slab", along_z(3))
     p2 = lax.ppermute(piece, "slab", along_z(2))
     own, wrap = call(merge_kernel, [shape(2, MROWS, 128), shape(EDGE, 128)], 0, 5, tail=anywhere)(
-        piece, p1, p2, p3, smat
-    )
+        piece, p1, p2, p3, utab
+    )
+    vtab, smat = call(
+        lens_table_kernel, [shape(2, 2, 2, HALF, FHALF, dtype=BF16), shape(NF, 256, dtype=BF16)], 0, 1, tail=anywhere
+    )(own)
     partner = lax.ppermute(own, "slab", along_y((3, 2, 1, 0)))
     beside = lax.ppermute(own, "slab", along_y((1, 0, 3, 2)))
     last = lax.ppermute(own, "slab", along_y((2, 3, 0, 1)))
     edge = lax.ppermute(
         wrap, "slab", [(4 * y, 4 * y + 4) for y in range(3)] + [(4 * y + 7, 4 * y + 3) for y in range(3)]
     )
-    scratch = [pltpu.VMEM((256, 512), BF16)] * 2
-    before = call(first_kernel, shape(4, UROWS, 512), 0, 3, scratch)(own, partner, utab)
+    scratch = [pltpu.VMEM((4, 256, 512), BF16)] * 2
+    before = call(first_kernel, shape(4, UROWS, 512), 0, 4, scratch, tail=anywhere)(own, partner, utab, smat)
     keep, give = call(second_kernel, [shape(2, UROWS, 512)] * 2, 0, 5, scratch, tail=anywhere)(
         beside, last, utab, before, edge
     )
@@ -497,29 +512,33 @@
     )
     sibling = [(i, i ^ 1) for i in range(NWAV)]
     crossed = lax.ppermute(give, "wav", sibling)
-    mine, other = call(lens_kernel, [shape(4, 24, 128)] * 2, 0, 6)(
+    mine, other = call(lens_kernel, [shape(32, 128)] * 2, 0, 6)(
         keep, crossed, vtab, weight, smat, lenses
     )
     got = lax.ppermute(other, "wav", sibling)
-    sent = call(pack_kernel, [shape(2, 24, 128)] * 4, 0, 2)(mine, got)
-    arrived = [sent[0]] + [
-        lax.ppermute(sent[k], "wav", [(i, (i + 2 * k) % NWAV) for i in range(NWAV)]) for k in (1, 2, 3)
-    ]
+    def along_x(sent, k):
+        return lax.ppermute(sent, "wav", [(i, (i + 2 * k) % NWAV) for i in range(NWAV)])
+
+    (opposite,) = call(functools.partial(pack_kernel, shifts=(2,)), [shape(16, 128)], 0, 3, tail=anywhere)(mine, got, lenses)
+    a2 = along_x(opposite, 2)
+    kept, forth, back = call(functools.partial(pack_kernel, shifts=(0, 1, 3)), [shape(16, 128)] * 3, 0, 3, tail=anywhere)(
+        mine, got, opposite
+    )
+    a1, a3 = along_x(forth, 1), along_x(back, 3)
     return call(
         detector_kernel,
         shape(256, 512),
-        1,
-        5,
+        0,
+        6,
         [
-            pltpu.VMEM((NWAV, 24, 128), F32),
-            pltpu.VMEM((5, NWAV * 24, 128), F32),
-            pltpu.VMEM((72, 640), F32),
-            pltpu.VMEM((16, 640), F32),
-            pltpu.VMEM((5, 16, 512), F32),
-            pltpu.VMEM((5, 16, 512), F32),
-            pltpu.VMEM((5, 8 * TILES, 512), F32),
+            pltpu.VMEM((WAVES, 16, 128), F32),
+            pltpu.VMEM((10, 16, 512), F32),
+            pltpu.VMEM((4, 16, 512), F32),
+            pltpu.VMEM((4, 264, 128), F32),
+            pltpu.SemaphoreType.DMA((4,)),
         ],
-    )(crosstalk, *arrived)
+        outside=True,
+    )(crosstalk, kept, a1, a2, a3, lenses)
 
 
 def solution(mesh):

time: 42.1 us -> 40.2 us (0.955)
  Pallas kernels: 15.3 us -> 11.6 us
  waiting for transfers between devices: 5.97 us -> 8.33 us
  starting transfers between devices: 19.7 us -> 19 us
    pallas_call x5 -> x7, Pallas kernels: 10.5 us -> 7.51 us  [the longest x1 2.06 us: body(): call(detector_kernel, shape(256, 512), 0, 6, [pltpu.VMEM((WAVES, 16, 128)...]
    ppermute x1, waiting for transfers between devices: 0.35 us -> 2.61 us  [body(): p2 = lax.ppermute(piece, 'slab', along_z(2))]
    ppermute x3, waiting for transfers between devices: 2.39 us -> 3.34 us  [along_x(): lax.ppermute(sent, 'wav', [(i, (i + 2 * k) % NWAV) for i in range(NWAV)])]
    pallas_call x1, Pallas kernels: 2.01 us -> 1.37 us  [body(): call(second_kernel, [shape(2, UROWS, 512)] * 2, 0, 5, scratch, tail=anywh...]
    ppermute x3, starting transfers between devices: 5.73 us -> 5.12 us  [along_x(): lax.ppermute(sent, 'wav', [(i, (i + 2 * k) % NWAV) for i in range(NWAV)])]
    ppermute x1, waiting for transfers between devices: 0.59 us -> 0.01 us  [body(): last = lax.ppermute(own, 'slab', along_y((2, 3, 0, 1)))]
  transfers between devices with their start and end apart: 12 -> 12, of which waited for: 7 -> 5; matrix products, arithmetic and copies ran while one was open for 0% -> 0% of each run, Pallas kernels for 12% -> 10%
where the time goes in v2:
time: 40.2 us; the launch traced here: 39.9 us
  starting transfers between devices  19 us (47%)
  Pallas kernels  11.6 us (29%)
  waiting for transfers between devices  8.33 us (21%)
  local copies, waits for them, and re-layouts  0.83 us (2%)
    ppermute x3, starting transfers between devices, along_x(): lax.ppermute(sent, 'wav', [(i, (i + 2 * k) % NWAV) for i in range(NWAV)])  5.12 us
    ppermute x1, starting transfers between devices, body(): lax.ppermute(wrap, 'slab', [(4 * y, 4 * y + 4) for y in range(3)] + [(4 *...  3.47 us
    ppermute x3, waiting for transfers between devices, along_x(): lax.ppermute(sent, 'wav', [(i, (i + 2 * k) % NWAV) for i in range(NWAV)])  3.34 us
    ppermute x1, starting transfers between devices, body(): partner = lax.ppermute(own, 'slab', along_y((3, 2, 1, 0)))  3.09 us
    ppermute x1, waiting for transfers between devices, body(): p2 = lax.ppermute(piece, 'slab', along_z(2))  2.61 us
    pallas_call x1, Pallas kernels, body(): call(prepare_kernel, [shape(PIECE, 128), shape(PIECE + EDGE, 128), shape(...  2.31 us
    ppermute x1, starting transfers between devices, body(): p3 = lax.ppermute(down, 'slab', along_z(3))  2.2 us
    ppermute x1, starting transfers between devices, body(): p1 = lax.ppermute(up, 'slab', along_z(1))  2.07 us
  transfers between devices with their start and end apart: 12, of which 5 were waited for; matrix products, arithmetic and copies ran while one was open for 0% of the time, Pallas kernels for 10%

profile of v2, /device:TPU:0, one launch (start us, length us, event | category | flops | bytes accessed | tf_op | source)
XLA Modules:
  0.0 39.9 jit_solution(9081366619748440309)
XLA Ops:
  0.0 2.3 %prepare_kernel.1 = (f32[80,128]{1,0:T(8,128)}, f32[152,128]{1,0:T(8,128)}, f32[152,128]{1,0:T(8,128)}, f32[8,128]{1,0:T(8,128)}) custom-call(f32[32,512]{1,0:T(8,128)} %amp_in.1, s32[32,512]{1,0:T(8,128)} %seg_in.1, s32[3,798]{1,0:T(4,128)} %bitcast.1, f32[64,1024]{1,0:T(8,128)} %mask.3, s32[8,16]{1,0:T(8,128)} %trow.1, s32[8,16]{1,0:T(8,128)} %tcol.1, ...), custom_call_target="tpu_custom_call" | custom-call | tf_op jit(solution)/shard_map/prepare_kernel/pallas_call | solution.py:473
  2.3 2.1 %collective-permute-start = (f32[152,128]{1,0:T(8,128)}, f32[152,128]{1,0:T(8,128)S(1)}, u32[]{:S(2)}, u32[]{:S(2)}) collective-permute-start(f32[152,128]{1,0:T(8,128)} %get-tuple-element.23), channel_id=1, source_target_pairs={{0,1},{1,2},{2,3},{3,0},{4,5},{5,6},{6,7},{7,4},{8,9},{9,10},{10,1... | collective-permute-start | bytes 233480 | tf_op jit(solution)/shard_map/ppermute | solution.py:490
  4.4 2.2 %collective-permute-start.2 = (f32[152,128]{1,0:T(8,128)}, f32[152,128]{1,0:T(8,128)S(1)}, u32[]{:S(2)}, u32[]{:S(2)}) collective-permute-start(f32[152,128]{1,0:T(8,128)} %get-tuple-element.24), channel_id=1, source_target_pairs={{0,3},{1,0},{2,1},{3,2},{4,7},{5,4},{6,5},{7,6},{8,11},{9,8},{10,9... | collective-permute-start | bytes 233480 | tf_op jit(solution)/shard_map/ppermute | solution.py:491
  6.6 1.8 %collective-permute-start.1 = (f32[80,128]{1,0:T(8,128)}, f32[80,128]{1,0:T(8,128)S(1)}, u32[]{:S(2)}, u32[]{:S(2)}) collective-permute-start(f32[80,128]{1,0:T(8,128)} %get-tuple-element.22.after.p0), channel_id=1, source_target_pairs={{0,2},{1,3},{2,0},{3,1},{4,6},{5,7},{6,4},{7,5},{8,10},{9,11},{10,... | collective-permute-start | bytes 122888 | tf_op jit(solution)/shard_map/ppermute | solution.py:492
  8.4 0.0 copy-start.1
  8.4 0.8 %copy-done.1 = f32[80,128]{1,0:T(8,128)S(1)} copy-done((f32[80,128]{1,0:T(8,128)S(1)}, f32[80,128]{1,0:T(8,128)}, u32[]{:S(2)}) %copy-start.1) | copy-done | bytes 40984
  9.2 0.5 %focal_table_kernel.1.after.utab = bf16[2,4,160,256]{3,2,1,0:T(8,128)(2,1)S(1)} custom-call(f32[80,128]{1,0:T(8,128)S(1)} %copy-done.1), custom_call_target="tpu_custom_call" | custom-call | tf_op jit(solution)/shard_map/focal_table_kernel/pallas_call | solution.py:489
  9.7 2.6 %collective-permute-done.1.p2 = f32[80,128]{1,0:T(8,128)S(1)} collective-permute-done((f32[80,128]{1,0:T(8,128)}, f32[80,128]{1,0:T(8,128)S(1)}, u32[]{:S(2)}, u32[]{:S(2)}) %collective-permute-start.1) | collective-permute-done | bytes 40992 | tf_op jit(solution)/shard_map/ppermute | solution.py:492
  12.3 0.0 collective-permute-done.p1
  12.3 0.0 collective-permute-done.2.p3
  12.3 0.1 merge_kernel.1
  12.4 0.0 copy-start
  12.4 0.0 copy-start.3
  12.4 3.1 %collective-permute-start.5 = (f32[2,136,128]{2,1,0:T(8,128)S(1)}, f32[2,136,128]{2,1,0:T(8,128)S(1)}, u32[]{:S(2)}, u32[]{:S(2)}) collective-permute-start(f32[2,136,128]{2,1,0:T(8,128)S(1)} %get-tuple-element.25.after.first), channel_id=1, source_target_pairs={{0,12},{1,13},{2,14},{3,15},{4,8},{5,9},{6,10},{7,11},{8,4},{9,5},... | collective-permute-start | bytes 417800 | tf_op jit(solution)/shard_map/ppermute | solution.py:499
  15.5 0.6 %collective-permute-start.4 = (f32[2,136,128]{2,1,0:T(8,128)S(1)}, f32[2,136,128]{2,1,0:T(8,128)S(1)}, u32[]{:S(2)}, u32[]{:S(2)}) collective-permute-start(f32[2,136,128]{2,1,0:T(8,128)S(1)} %get-tuple-element.25.after.first), channel_id=1, source_target_pairs={{0,8},{1,9},{2,10},{3,11},{4,12},{5,13},{6,14},{7,15},{8,0},{9,1},... | collective-permute-start | bytes 417800 | tf_op jit(solution)/shard_map/ppermute | solution.py:501
  16.2 0.5 %collective-permute-start.3 = (f32[2,136,128]{2,1,0:T(8,128)S(1)}, f32[2,136,128]{2,1,0:T(8,128)S(1)}, u32[]{:S(2)}, u32[]{:S(2)}) collective-permute-start(f32[2,136,128]{2,1,0:T(8,128)S(1)} %get-tuple-element.25.after.first), channel_id=1, source_target_pairs={{0,4},{1,5},{2,6},{3,7},{4,0},{5,1},{6,2},{7,3},{8,12},{9,13},{10,... | collective-permute-start | bytes 417800 | tf_op jit(solution)/shard_map/ppermute | solution.py:500
  16.6 3.5 %collective-permute-start.6 = (f32[72,128]{1,0:T(8,128)S(1)}, f32[72,128]{1,0:T(8,128)S(1)}, u32[]{:S(2)}, u32[]{:S(2)}) collective-permute-start(f32[72,128]{1,0:T(8,128)S(1)} %get-tuple-element.27), channel_id=1, source_target_pairs={{0,4},{4,8},{8,12},{7,3},{11,7},{15,11},{16,20},{20,24},{24,28},{2... | collective-permute-start | bytes 110600 | tf_op jit(solution)/shard_map/ppermute | solution.py:502
  20.1 1.9 %lens_table_kernel.1 = (bf16[2,2,2,256,512]{4,3,2,1,0:T(8,128)(2,1)S(1)}, bf16[1024,256]{1,0:T(8,128)(2,1)S(1)}) custom-call(f32[2,136,128]{2,1,0:T(8,128)S(1)} %get-tuple-element.25.after.first), custom_call_target="tpu_custom_call" | custom-call | tf_op jit(solution)/shard_map/lens_table_kernel/pallas_call | solution.py:496
  22.0 0.0 collective-permute-done.5.second
  22.1 1.3 %first_kernel.1.before = f32[4,80,512]{2,1,0:T(8,128)S(1)} custom-call(f32[2,136,128]{2,1,0:T(8,128)S(1)} %get-tuple-element.25.after.first, f32[2,136,128]{2,1,0:T(8,128)S(1)} %collective-permute-done.5.second, bf16[2,4,160,256]{3,2,1,0:T(8,128)(2,1)S(1)} %focal_table_kernel.1.after.utab, bf16[1024,256]{1,0:T(8,128)(2,1)S(1)} %get-tuple-element.26.after.smat), custom_call_target="tpu_custom_call" | custom-call | tf_op jit(solution)/shard_map/first_kernel/pallas_call | solution.py:506
  23.4 0.0 collective-permute-done.6.after.edge
  23.4 0.0 collective-permute-done.4.second
  23.4 0.0 collective-permute-done.3.first
  23.4 1.4 %second_kernel.1 = (f32[2,80,512]{2,1,0:T(8,128)S(1)}, f32[2,80,512]{2,1,0:T(8,128)S(1)}) custom-call(f32[2,136,128]{2,1,0:T(8,128)S(1)} %collective-permute-done.3.first, f32[2,136,128]{2,1,0:T(8,128)S(1)} %collective-permute-done.4.second, bf16[2,4,160,256]{3,2,1,0:T(8,128)(2,1)S(1)} %focal_table_kernel.1.after.utab, ...), custom_call_target="tpu_custom_call" | custom-call | tf_op jit(solution)/shard_map/second_kernel/pallas_call | solution.py:507
  24.8 0.1 collective-permute-start.7
  24.9 0.0 copy-done
  24.9 0.0 copy-done.3
  24.9 0.0 copy-start.2
  24.9 0.3 weight_kernel.1
  25.2 1.3 %collective-permute-done.7.got = f32[2,80,512]{2,1,0:T(8,128)S(1)} collective-permute-done((f32[2,80,512]{2,1,0:T(8,128)S(1)}, f32[2,80,512]{2,1,0:T(8,128)S(1)}, u32[]{:S(2)}, u32[]{:S(2)}) %collective-permute-start.7) | collective-permute-done | bytes 327712 | tf_op jit(solution)/shard_map/ppermute | solution.py:514
  26.5 1.5 %lens_kernel.1 = (f32[32,128]{1,0:T(8,128)S(1)}, f32[32,128]{1,0:T(8,128)S(1)}) custom-call(f32[2,80,512]{2,1,0:T(8,128)S(1)} %get-tuple-element.28.keep, f32[2,80,512]{2,1,0:T(8,128)S(1)} %collective-permute-done.7.got, bf16[2,2,2,256,512]{4,3,2,1,0:T(8,128)(2,1)S(1)} %get-tuple-element.30.vtab, f32[80,1024]{1,0:T(8,128)S(1)} %get-tuple-element.32.weight, ...), custom_call_target="tpu_custom_call" | custom-call | tf_op jit(solution)/shard_map/lens_kernel/pallas_call | solution.py:515
  28.0 0.1 collective-permute-start.8
  28.2 1.0 %collective-permute-done.8.got = f32[32,128]{1,0:T(8,128)S(1)} collective-permute-done((f32[32,128]{1,0:T(8,128)S(1)}, f32[32,128]{1,0:T(8,128)S(1)}, u32[]{:S(2)}, u32[]{:S(2)}) %collective-permute-start.8) | collective-permute-done | bytes 16416 | tf_op jit(solution)/shard_map/ppermute | solution.py:518
  29.2 0.1 pack_kernel.2.after
  29.3 0.1 pack_kernel.3
  29.4 1.6 %collective-permute-start.9 = (f32[16,128]{1,0:T(8,128)S(1)}, f32[16,128]{1,0:T(8,128)S(1)}, u32[]{:S(2)}, u32[]{:S(2)}) collective-permute-start(f32[16,128]{1,0:T(8,128)S(1)} %get-tuple-element.37), channel_id=1, source_target_pairs={{0,32},{16,48},{32,64},{48,80},{64,96},{80,112},{96,0},{112,16},{1... | collective-permute-start | bytes 24584 | tf_op jit(solution)/shard_map/ppermute | solution.py:520
  31.0 1.7 %collective-permute-start.11 = (f32[16,128]{1,0:T(8,128)S(1)}, f32[16,128]{1,0:T(8,128)S(1)}, u32[]{:S(2)}, u32[]{:S(2)}) collective-permute-start(f32[16,128]{1,0:T(8,128)S(1)} %get-tuple-element.38), channel_id=1, source_target_pairs={{0,96},{16,112},{32,0},{48,16},{64,32},{80,48},{96,64},{112,80},{1... | collective-permute-start | bytes 24584 | tf_op jit(solution)/shard_map/ppermute | solution.py:520
  32.7 1.8 %collective-permute-start.10 = (f32[16,128]{1,0:T(8,128)S(1)}, f32[16,128]{1,0:T(8,128)S(1)}, u32[]{:S(2)}, u32[]{:S(2)}) collective-permute-start(f32[16,128]{1,0:T(8,128)S(1)} %pack_kernel.2.after), channel_id=1, source_target_pairs={{0,64},{16,80},{32,96},{48,112},{64,0},{80,16},{96,32},{112,48},{1... | collective-permute-start | bytes 24584 | tf_op jit(solution)/shard_map/ppermute | solution.py:520
  34.5 0.0 collective-permute-done.9.a1
  34.5 0.1 collective-permute-done.11.a3
  34.6 3.2 %collective-permute-done.10.a2 = f32[16,128]{1,0:T(8,128)S(1)} collective-permute-done((f32[16,128]{1,0:T(8,128)S(1)}, f32[16,128]{1,0:T(8,128)S(1)}, u32[]{:S(2)}, u32[]{:S(2)}) %collective-permute-start.10) | collective-permute-done | bytes 8224 | tf_op jit(solution)/shard_map/ppermute | solution.py:520
  37.9 0.0 copy-done.2
  37.9 2.1 %detector_kernel.1 = f32[256,512]{1,0:T(8,128)} custom-call(f32[5,5]{1,0:T(8,128)S(1)} %copy-done.2, f32[16,128]{1,0:T(8,128)S(1)} %get-tuple-element.36.a0, f32[16,128]{1,0:T(8,128)S(1)} %collective-permute-done.9.a1, f32[16,128]{1,0:T(8,128)S(1)} %collective-permute-done.10.a2, f32[16,128]{1,0:T(8,128)S(1)} %collective-permute-done.11.a3, ...), custom_call_target="tpu_custom_call" | custom-call | tf_op jit(solution)/shard_map/detector_kernel/pallas_call | solution.py:528
Async XLA Ops:
  2.3 10.0 %collective-permute-start = (f32[152,128]{1,0:T(8,128)}, f32[152,128]{1,0:T(8,128)S(1)}, u32[]{:S(2)}, u32[]{:S(2)}) collective-permute-start(f32[152,128]{1,0:T(8,128)} %get-tuple-element.23), channel_id=1, source_target_pairs={{0,1},{1,2},{2,3},{3,0},{4,5},{5,6},{6,7},{7,4},{8,9},{9,10},{10,1... | collective-permute-start | bytes 233480 | tf_op jit(solution)/shard_map/ppermute | solution.py:490
  4.4 7.9 %collective-permute-start.2 = (f32[152,128]{1,0:T(8,128)}, f32[152,128]{1,0:T(8,128)S(1)}, u32[]{:S(2)}, u32[]{:S(2)}) collective-permute-start(f32[152,128]{1,0:T(8,128)} %get-tuple-element.24), channel_id=1, source_target_pairs={{0,3},{1,0},{2,1},{3,2},{4,7},{5,4},{6,5},{7,6},{8,11},{9,8},{10,9... | collective-permute-start | bytes 233480 | tf_op jit(solution)/shard_map/ppermute | solution.py:491
  6.6 5.7 %collective-permute-start.1 = (f32[80,128]{1,0:T(8,128)}, f32[80,128]{1,0:T(8,128)S(1)}, u32[]{:S(2)}, u32[]{:S(2)}) collective-permute-start(f32[80,128]{1,0:T(8,128)} %get-tuple-element.22.after.p0), channel_id=1, source_target_pairs={{0,2},{1,3},{2,0},{3,1},{4,6},{5,7},{6,4},{7,5},{8,10},{9,11},{10,... | collective-permute-start | bytes 122888 | tf_op jit(solution)/shard_map/ppermute | solution.py:492
  8.4 0.8 %copy-start.1 = (f32[80,128]{1,0:T(8,128)S(1)}, f32[80,128]{1,0:T(8,128)}, u32[]{:S(2)}) copy-start(f32[80,128]{1,0:T(8,128)} %get-tuple-element.22.after.p0) | copy-start | bytes 122884
  12.4 12.5 %copy-start = (f32[64,1024]{1,0:T(8,128)S(1)}, f32[64,1024]{1,0:T(8,128)}, u32[]{:S(2)}) copy-start(f32[64,1024]{1,0:T(8,128)} %mask.3) | copy-start | bytes 786436
  12.4 12.5 %copy-start.3 = (f32[8,128]{1,0:T(8,128)S(1)}, f32[8,128]{1,0:T(8,128)}, u32[]{:S(2)}) copy-start(f32[8,128]{1,0:T(8,128)} %get-tuple-element.31.trace) | copy-start | bytes 12292
  12.4 9.6 %collective-permute-start.5 = (f32[2,136,128]{2,1,0:T(8,128)S(1)}, f32[2,136,128]{2,1,0:T(8,128)S(1)}, u32[]{:S(2)}, u32[]{:S(2)}) collective-permute-start(f32[2,136,128]{2,1,0:T(8,128)S(1)} %get-tuple-element.25.after.first), channel_id=1, source_target_pairs={{0,12},{1,13},{2,14},{3,15},{4,8},{5,9},{6,10},{7,11},{8,4},{9,5},... | collective-permute-start | bytes 417800 | tf_op jit(solution)/shard_map/ppermute | solution.py:499
  15.5 7.9 %collective-permute-start.4 = (f32[2,136,128]{2,1,0:T(8,128)S(1)}, f32[2,136,128]{2,1,0:T(8,128)S(1)}, u32[]{:S(2)}, u32[]{:S(2)}) collective-permute-start(f32[2,136,128]{2,1,0:T(8,128)S(1)} %get-tuple-element.25.after.first), channel_id=1, source_target_pairs={{0,8},{1,9},{2,10},{3,11},{4,12},{5,13},{6,14},{7,15},{8,0},{9,1},... | collective-permute-start | bytes 417800 | tf_op jit(solution)/shard_map/ppermute | solution.py:501
  16.2 7.2 %collective-permute-start.3 = (f32[2,136,128]{2,1,0:T(8,128)S(1)}, f32[2,136,128]{2,1,0:T(8,128)S(1)}, u32[]{:S(2)}, u32[]{:S(2)}) collective-permute-start(f32[2,136,128]{2,1,0:T(8,128)S(1)} %get-tuple-element.25.after.first), channel_id=1, source_target_pairs={{0,4},{1,5},{2,6},{3,7},{4,0},{5,1},{6,2},{7,3},{8,12},{9,13},{10,... | collective-permute-start | bytes 417800 | tf_op jit(solution)/shard_map/ppermute | solution.py:500
  16.6 6.8 %collective-permute-start.6 = (f32[72,128]{1,0:T(8,128)S(1)}, f32[72,128]{1,0:T(8,128)S(1)}, u32[]{:S(2)}, u32[]{:S(2)}) collective-permute-start(f32[72,128]{1,0:T(8,128)S(1)} %get-tuple-element.27), channel_id=1, source_target_pairs={{0,4},{4,8},{8,12},{7,3},{11,7},{15,11},{16,20},{20,24},{24,28},{2... | collective-permute-start | bytes 110600 | tf_op jit(solution)/shard_map/ppermute | solution.py:502
  24.8 1.7 %collective-permute-start.7 = (f32[2,80,512]{2,1,0:T(8,128)S(1)}, f32[2,80,512]{2,1,0:T(8,128)S(1)}, u32[]{:S(2)}, u32[]{:S(2)}) collective-permute-start(f32[2,80,512]{2,1,0:T(8,128)S(1)} %get-tuple-element.29.after), channel_id=1, source_target_pairs={{0,16},{16,0},{32,48},{48,32},{64,80},{80,64},{96,112},{112,96},{1... | collective-permute-start | bytes 983048 | tf_op jit(solution)/shard_map/ppermute | solution.py:514
  24.9 12.9 %copy-start.2 = (f32[5,5]{1,0:T(8,128)S(1)}, f32[5,5]{1,0:T(8,128)}, u32[]{:S(2)}) copy-start(f32[5,5]{1,0:T(8,128)} %kernel.1) | copy-start | bytes 304
  28.0 1.2 %collective-permute-start.8 = (f32[32,128]{1,0:T(8,128)S(1)}, f32[32,128]{1,0:T(8,128)S(1)}, u32[]{:S(2)}, u32[]{:S(2)}) collective-permute-start(f32[32,128]{1,0:T(8,128)S(1)} %get-tuple-element.35), channel_id=1, source_target_pairs={{0,16},{16,0},{32,48},{48,32},{64,80},{80,64},{96,112},{112,96},{1... | collective-permute-start | bytes 49160 | tf_op jit(solution)/shard_map/ppermute | solution.py:518
  29.4 5.1 %collective-permute-start.9 = (f32[16,128]{1,0:T(8,128)S(1)}, f32[16,128]{1,0:T(8,128)S(1)}, u32[]{:S(2)}, u32[]{:S(2)}) collective-permute-start(f32[16,128]{1,0:T(8,128)S(1)} %get-tuple-element.37), channel_id=1, source_target_pairs={{0,32},{16,48},{32,64},{48,80},{64,96},{80,112},{96,0},{112,16},{1... | collective-permute-start | bytes 24584 | tf_op jit(solution)/shard_map/ppermute | solution.py:520
  31.0 3.7 %collective-permute-start.11 = (f32[16,128]{1,0:T(8,128)S(1)}, f32[16,128]{1,0:T(8,128)S(1)}, u32[]{:S(2)}, u32[]{:S(2)}) collective-permute-start(f32[16,128]{1,0:T(8,128)S(1)} %get-tuple-element.38), channel_id=1, source_target_pairs={{0,96},{16,112},{32,0},{48,16},{64,32},{80,48},{96,64},{112,80},{1... | collective-permute-start | bytes 24584 | tf_op jit(solution)/shard_map/ppermute | solution.py:520
  32.7 5.2 %collective-permute-start.10 = (f32[16,128]{1,0:T(8,128)S(1)}, f32[16,128]{1,0:T(8,128)S(1)}, u32[]{:S(2)}, u32[]{:S(2)}) collective-permute-start(f32[16,128]{1,0:T(8,128)S(1)} %pack_kernel.2.after), channel_id=1, source_target_pairs={{0,64},{16,80},{32,96},{48,112},{64,0},{80,16},{96,32},{112,48},{1... | collective-permute-start | bytes 24584 | tf_op jit(solution)/shard_map/ppermute | solution.py:520

commit v3 on v2

--- a/solution.py
+++ b/solution.py
@@ -65,7 +65,9 @@
 
 def focal_row(s, shape):
     a = iota(shape, 0)
-    return FROWS * s + jnp.where(a < FROWS, a, jnp.where(a < FROWS + 8, a - FROWS - 8, a - 8))
+    r = (a - FROWS) >> 1
+    own = 8 * (a & 7) + (a >> 3)
+    return FROWS * s + jnp.where(a < FROWS, own, jnp.where((a & 1) == 0, r - 8, FROWS + r))
 
 
 def reversal(n):
@@ -109,33 +111,36 @@
         trace[:, 16 * c:16 * c + 16] = table
         up[PIECE + 64:PIECE + 65, 16 * c:16 * c + 16] = table[7:8]
         down[PIECE + 64:PIECE + 65, 16 * c:16 * c + 16] = table[0:1]
-    ids = sum(dot(part, pick) for part in split2(seg[...].astype(F32)))
+    ids = dot(jnp.concatenate(split2(seg[...].astype(F32)), axis=0), pick)
+    ids = ids[0:16] + ids[16:32]
     upper_ids, lower_ids = ids[0:1], ids[8:9]
     ids = jnp.concatenate(
         [jnp.where(lower, lower_ids, upper_ids), jnp.where(lower, upper_ids, lower_ids)], axis=1
     )
     which = iota((SEGMENTS, 256), 0).astype(F32)
-    found = sum(dot(part, (which == ids).astype(BF16)) for part in split2(tab[...].astype(F32)))
+    table = jnp.concatenate([tab[...].astype(F32), jnp.zeros((5, SEGMENTS), F32)], axis=0)
+    found = dot(jnp.concatenate(split2(table), axis=0), (which == ids).astype(BF16))
+    found = found[0:3] + found[8:11]
     found = jnp.sum(jnp.where(iota((3, 256), 0) == (iota((3, 256), 1) & 127) >> 5, found, 0.0), axis=0, keepdims=True)
     for k in range(2):
         out[ROWS + k:ROWS + k + 1, :] = found[:, 128 * k:128 * k + 128]
     first = core == 0
     left = jnp.where(first, amp[:, 0:128], amp[:, 128:256])
     right = jnp.where(first, amp[:, 384:512], amp[:, 256:384])
-    out[0:ROWS, :] = sum(dot(turned, part) for part in split3(left))
-    out[ROWS + 8:2 * ROWS + 8, :] = sum(dot(turned, dot(part, rev).astype(BF16)) for part in split3(right))
+    right = dot(jnp.concatenate(split3(right), axis=0), rev).astype(BF16)
+    parts = list(split3(left)) + [right[ROWS * k:ROWS * k + ROWS] for k in range(3)]
+    found = dot(turned, jnp.concatenate(parts, axis=1))
+    for k in range(2):
+        out[(ROWS + 8) * k:(ROWS + 8) * k + ROWS, :] = sum(found[:, 128 * q:128 * q + 128] for q in range(3 * k, 3 * k + 3))
     for k, ref in enumerate((up, down)):
         ref[0:PIECE, :] = out[...]
         for q in range(8):
             ref[PIECE + 8 * q:PIECE + 8 * q + 8, :] = edges[k, :, 128 * q:128 * q + 128]
 
 
-def merge_kernel(p0, p1, p2, p3, after, out, wrap):
-    del after
-    w, s, y, z, x, core, sign, pair = place_of()
-    wrap[...] = jnp.where(z == 0, p1[PIECE:PIECE + EDGE, :], p3[PIECE:PIECE + EDGE, :])
-    out[:, GROUP:MROWS, :] = jnp.zeros((2, 8, 128), F32)
-    for k, piece in enumerate((p0, p1, p2, p3)):
+def place_pieces(out, pieces):
+    w, s, y, z, x, core, sign, pair = place_of()
+    for k, piece in pieces:
         source = lax.rem(z - k + 4, 4)
         place = jnp.where(y >= 2, 3 - source, source)
         for at in range(4):
@@ -145,8 +150,23 @@
                 for t in range(2):
                     for b in range(2):
                         r0 = (ROWS + 8) * t + 16 * b
-                        out[t, pl.ds(2 * at + b, 16, stride=8), :] = piece[r0:r0 + 16, :]
-                out[0, GROUP + 2 * at:GROUP + 2 * at + 2, :] = piece[ROWS:ROWS + 2, :]
+                        out[pl.ds(MROWS * t + 2 * at + b, 16, stride=8), :] = piece[r0:r0 + 16, :]
+                out[GROUP + 2 * at:GROUP + 2 * at + 2, :] = piece[ROWS:ROWS + 2, :]
+
+
+def opposite_kernel(p0, p2, after, out):
+    del after
+    out[GROUP:MROWS, :] = jnp.zeros((8, 128), F32)
+    out[MROWS + GROUP:2 * MROWS, :] = jnp.zeros((8, 128), F32)
+    place_pieces(out, ((0, p0), (2, p2)))
+
+
+def merge_kernel(begun, p1, p3, out, more):
+    del begun
+    w, s, y, z, x, core, sign, pair = place_of()
+    place_pieces(out, ((1, p1), (3, p3)))
+    more[0:2 * MROWS, :] = out[...]
+    more[2 * MROWS:2 * MROWS + EDGE, :] = jnp.where(z == 0, p1[PIECE:PIECE + EDGE, :], p3[PIECE:PIECE + EDGE, :])
 
 
 def wavelength(w):
@@ -172,9 +192,12 @@
     return (2 * index + 1 - count).astype(F32)
 
 
-def focal_table_kernel(after, utab):
+def table_kernel(after, utab, vtab, spot):
     del after
     w, s, y, z, x, core, sign, pair = place_of()
+    row, lane = iota((128, 768), 0), iota((128, 768), 1)
+    block = 8 * core + ((lane & 127) >> 4)
+    spot[...] = (row == 32 * (lane >> 8) + jnp.where((lane & 128) == 0, block, 31 - block)).astype(BF16)
     m = odd(focal_row(s, (UROWS, GROUP)), NF)
     rho = iota((1, GROUP), 1)
     for k in range(4):
@@ -182,15 +205,11 @@
         for p in range(2):
             g = pair if p == 0 else 1 - pair
             sin, cos = angle(m, slope(odd(128 * g + 16 * (rho & 7) + (rho >> 3), NP), wave))
-            for at, part in ((0, cos), (GROUP, sin * sign)):
+            sin = sin * sign
+            for r0, at, part in ((0, 0, cos), (0, GROUP, sin), (UROWS, 0, -sin), (UROWS, GROUP, cos)):
                 high, low = split2(part)
-                utab[p, k, 0:UROWS, at:at + GROUP] = high
-                utab[p, k, UROWS:2 * UROWS, at:at + GROUP] = low
-
-
-def lens_table_kernel(after, vtab, smat):
-    del after
-    w, s, y, z, x, core, sign, pair = place_of()
+                utab[p, k, r0:r0 + UROWS, at:at + GROUP] = high
+                utab[p, k, r0 + 2 * UROWS:r0 + 3 * UROWS, at:at + GROUP] = low
     m = odd(iota((16, 128), 1), NF)
     for k in range(2):
 
@@ -208,18 +227,16 @@
             return carry
 
         lax.fori_loop(0, HALF // 16, chunk, 0)
-    row, lane = iota((FHALF, 256), 0), iota((FHALF, 256), 1)
-    column = 2 * ((lane >> 5) & 3) + jnp.where(lane < 128, core, 1 - core)
-    lens = jnp.where((lane & 31) < 18, 16 * column - 1 + (lane & 31), -1)
-    smat[0:FHALF, :] = (lens == row >> 3).astype(BF16)
-    smat[FHALF:NF, :] = (lens == NL - 1 - (row >> 3)).astype(BF16)
-
-
-def weight_kernel(mask, p1, p3, edge, trace, after, weight, lenses):
+
+
+def weight_kernel(mask, p1, p3, partner, beside, trace, after, weight, lenses, smat, full):
     del after
     w, s, y, z, x, core, sign, pair = place_of()
-    above = jnp.where(z == 0, edge[...], p1[PIECE:PIECE + EDGE, :])
-    below = jnp.where(z == 3, edge[...], p3[PIECE:PIECE + EDGE, :])
+    rows = slice(2 * MROWS, 2 * MROWS + EDGE)
+    across = jnp.where(jnp.where(z == 0, y == 2, y == 1), partner[rows, :], beside[rows, :])
+    across = jnp.where(jnp.where(z == 0, y == 0, y == 3), 0.0, across)
+    above = jnp.where(z == 0, across, p1[PIECE:PIECE + EDGE, :])
+    below = jnp.where(z == 3, across, p3[PIECE:PIECE + EDGE, :])
     lenses[0:8, :] = trace[...]
     lenses[8:9, :] = above[64:65]
     lenses[9:10, :] = below[64:65]
@@ -229,118 +246,103 @@
     down, across = (2 * u + 1 - NF).astype(F32) * 0.5, (2 * v + 1 - NF).astype(F32) * 0.5
     fade = 1.0 - jnp.exp((down * down + across * across) * (-1.0 / 1024.0))
     rev = reversal(256)
-    above, below = (jnp.concatenate([ref[8 * q:8 * q + 8] for q in range(8)], axis=1) for ref in (above, below))
-    full = jnp.concatenate([mask[...], above, below], axis=0)
-    t = full[:, :FHALF] * fade
+    for q in range(8):
+        for a in range(8):
+            full[q, pl.ds(a, 8, stride=8), :] = mask[8 * a:8 * a + 8, 128 * q:128 * q + 128]
+        full[q, pl.ds(FROWS, 8, stride=2), :] = above[8 * q:8 * q + 8]
+        full[q, pl.ds(FROWS + 1, 8, stride=2), :] = below[8 * q:8 * q + 8]
+    t = jnp.concatenate([full[q] for q in range(4)], axis=1) * fade
     weight[:, :FHALF] = t * t * 2.0**-24
     for q in range(2):
-        flipped = sum(dot(part, rev) for part in split3(full[:, NF - 256 * (q + 1):NF - 256 * q]))
+        flipped = sum(dot(part, rev) for part in split3(jnp.concatenate([full[6 - 2 * q], full[7 - 2 * q]], axis=1)))
         t = flipped * fade[:, 256 * q:256 * (q + 1)]
         weight[:, FHALF + 256 * q:FHALF + 256 * (q + 1)] = t * t * 2.0**-24
-
-
-def pair_fields(first, second, utab, p, whi, wlo):
+    row, lane = iota((FHALF, 256), 0), iota((FHALF, 256), 1)
+    column = 2 * ((lane >> 5) & 3) + jnp.where(lane < 128, core, 1 - core)
+    lens = jnp.where((lane & 31) < 18, 16 * column - 1 + (lane & 31), -1)
+    smat[0:FHALF, :] = (lens == row >> 3).astype(BF16)
+    smat[FHALF:NF, :] = (lens == NL - 1 - (row >> 3)).astype(BF16)
+
+
+def group_kernel(ref, utab, spot, *refs, p, flipped):
+    before = refs[0] if flipped or p else None
+    outs, (whi, wlo) = refs[before is not None:-2], refs[-2:]
     w, s, y, z, x, core, sign, pair = place_of()
     g = pair if p == 0 else 1 - pair
-    coef = jnp.concatenate([first[0, GROUP:MROWS, :], second[0, GROUP:MROWS, :]], axis=0)
-    high, low = split2(coef)
-    coef = jnp.concatenate([high, low], axis=0)
-    row, lane = iota((128, 128), 0), iota((128, 128), 1)
-    place = iota((16, 128), 0)
-    down = (32 * (8 * g + (place & 7)) + 1 - NP).astype(F32) * (1.0 / 1024.0)
-    toward = jnp.where(place < 8, sign, -sign)
-    across = (2 * (128 * core + iota((16, 128), 1)) + 1 - NP).astype(F32) * (1.0 / 1024.0)
+    turned = -1.0 if flipped else 1.0
+    coef = jnp.concatenate(split2(ref[GROUP:MROWS, :]), axis=0)
+    both = dot(coef, spot[...])
+    coef = both[0:8] + both[8:16]
+    down = odd(16 * (8 * g + iota((8, 128), 0)), NP) * (1.0 / 1024.0)
+    across = odd(128 * core + iota((8, 128), 1), NP) * (1.0 / 1024.0)
     paths, steps = [], []
     for side in range(2):
-        block = 8 * core + (lane >> 4)
-        block = block if side == 0 else 31 - block
-        pqr = []
-        for c in range(3):
-            both = dot(coef, (row == 32 * c + block).astype(BF16))
-            pqr.append(both[0:16] + both[16:32])
-        slope = toward * pqr[2]
-        paths.append(pqr[0] + (across if side == 0 else -across) * pqr[1] + slope * down)
-        steps.append(slope * (1.0 / 512.0))
-    fields = []
+        piston, tip, tilt = (coef[:, 256 * c + 128 * side:256 * c + 128 * side + 128] for c in range(3))
+        tilt = (sign * turned) * tilt
+        paths.append(piston + (across if side == 0 else -across) * tip + tilt * down)
+        steps.append(tilt * (1.0 / 512.0))
     for m in range(4):
         inverse = 1.0 / wavelength(2 * (w if m < 2 else w ^ 1) + (m & 1))
-        start = [sincos(path * inverse) for path in paths]
-        turn = [sincos(step * inverse) for step in steps]
-
-        def four(values, n):
-            return [values[side][n][8 * t:8 * t + 8] for t in range(2) for side in range(2)]
-
-        step_im, step_re = four(turn, 0), four(turn, 1)
-
-        def rows(r2, carry, m=m, step_im=step_im, step_re=step_re):
-            re, im = carry
-            found = [[] for _ in range(8)]
+        im, re = zip(*(sincos(path * (turned * inverse)) for path in paths))
+        step_im, step_re = zip(*(sincos(step * (turned * inverse)) for step in steps))
+        for r2 in range(8):
+            found = [[] for _ in range(4)]
             for h in range(2):
-                r0 = pl.multiple_of(16 * r2 + 8 * h, 8)
-                qre, qim = [], []
-                for t, ref in enumerate((first, second)):
-                    for side in range(2):
-                        a = ref[side, pl.ds(r0, 8), :]
-                        qre.append(a * re[2 * t + side])
-                        qim.append(a * im[2 * t + side])
+                r0 = 16 * r2 + 8 * h
                 for side in range(2):
-                    found[2 * side].append(qre[side] + qre[2 + side])
-                    found[2 * side + 1].append(qim[side] + qim[2 + side])
-                    found[4 + 2 * side].append(qim[side] - qim[2 + side])
-                    found[5 + 2 * side].append(qre[2 + side] - qre[side])
+                    a = ref[MROWS * side + r0:MROWS * side + r0 + 8, :]
+                    found[side].append(a * re[side])
+                    found[2 + side].append(a * im[side])
                 re, im = (
-                    [x * p - y * q for x, y, p, q in zip(re, im, step_re, step_im)],
-                    [x * q + y * p for x, y, p, q in zip(re, im, step_re, step_im)],
+                    [a * p - b * q for a, b, p, q in zip(re, im, step_re, step_im)],
+                    [a * q + b * p for a, b, p, q in zip(re, im, step_re, step_im)],
                 )
-            for q, values in enumerate(found):
+            for k, values in enumerate(found):
                 high, low = split2(jnp.concatenate(values, axis=0))
-                r0 = pl.multiple_of(16 * r2 + (GROUP if q >= 4 else 0), 16)
-                c0 = 128 * (q & 3)
-                whi[m, pl.ds(r0, 16), c0:c0 + 128] = high
-                wlo[m, pl.ds(r0, 16), c0:c0 + 128] = low
-            return re, im
-
-        lax.fori_loop(0, 8, rows, (four(start, 1), four(start, 0)), unroll=True)
+                r0, c0 = GROUP * (k >> 1) + 16 * r2, 128 * (k & 1)
+                whi[m, r0:r0 + 16, c0:c0 + 128] = high
+                wlo[m, r0:r0 + 16, c0:c0 + 128] = low
+    for m in range(4):
         table = utab[p, m]
         both = dot(table, whi[m])
-        fields.append(both[:UROWS] + both[UROWS:] + dot(table[:UROWS], wlo[m]))
-    return fields
-
-
-def first_kernel(first, second, utab, after, out, whi, wlo):
-    del after
-    for m, field in enumerate(pair_fields(first, second, utab, 0, whi, wlo)):
-        out[m] = field
-
-
-def second_kernel(first, second, utab, before, after, keep, give, whi, wlo):
-    del after
-    for m, field in enumerate(pair_fields(first, second, utab, 1, whi, wlo)):
-        (keep if m < 2 else give)[m & 1] = field + before[m]
+        field = both[:2 * UROWS] + both[2 * UROWS:] + dot(table[:2 * UROWS], wlo[m])
+        out = outs[0].at[m] if len(outs) == 1 else outs[m >> 1].at[m & 1]
+        if before is None:
+            out[...] = field
+        elif flipped:
+            out[0:UROWS] = before[m, 0:UROWS] + field[:UROWS]
+            out[UROWS:2 * UROWS] = before[m, UROWS:2 * UROWS] - field[UROWS:]
+        else:
+            out[...] = before[m] + field
 
 
 def lens_kernel(keep, got, vtab, weight, smat, lenses, mine, other):
+    parts = []
     for m in range(2):
-        lre, lim, rre, rim = (
-            jnp.concatenate([ref[m, :, 128 * q:128 * q + 128] for ref in (keep, got)], axis=1) for q in range(4)
+        left, right = (
+            jnp.concatenate([ref[m, :, 128 * q:128 * q + 128] for ref in (keep, got)], axis=1) for q in range(2)
         )
-        parts = [lre + rre, lim + rim, lim - rim, rre - lre]
+        odd_part = left - right
+        sides = left + right, jnp.concatenate([odd_part[UROWS:], -odd_part[:UROWS]], axis=0)
         terms = []
-        for q in range(2):
-            side = jnp.concatenate(parts[2 * q:2 * q + 2], axis=0)
+        for q, side in enumerate(sides):
             high, low = split2(side)
             both = dot(jnp.concatenate([high, low], axis=0), vtab[m, q, 0])
             terms.append(both[:2 * UROWS] + both[2 * UROWS:] + dot(high, vtab[m, q, 1]))
-        lens = 0.0
+        summed = []
         for q, value in enumerate((terms[0] + terms[1], terms[0] - terms[1])):
             re, im = value[:UROWS], value[UROWS:]
             power = (re * re + im * im) * weight[:, FHALF * q:FHALF * (q + 1)]
-            summed = jnp.sum(power.reshape(UROWS // 8, 8, FHALF), axis=1)
-            for part in split2(summed):
-                lens = lens + dot(part, smat[FHALF * q:FHALF * (q + 1), :])
+            edges = power[FROWS:FROWS + 8] + power[FROWS + 8:]
+            edges = edges + pltpu.roll(edges, 4, 0)
+            edges = edges + pltpu.roll(edges, 2, 0)
+            summed.append(jnp.concatenate([sum(power[8 * r:8 * r + 8] for r in range(8)), edges], axis=0))
+        parts.extend(split2(jnp.concatenate(summed, axis=1)))
+    lens = dot(jnp.concatenate(parts, axis=0), smat[...])
+    for m in range(2):
         for k, out in enumerate((mine, other)):
-            out[16 * m:16 * m + 10, :] = lens[:, 128 * k:128 * k + 128]
-            out[16 * m + 10:16 * m + 16, :] = jnp.zeros((6, 128), F32)
+            at = slice(128 * k, 128 * k + 128)
+            out[16 * m:16 * m + 16, :] = lens[32 * m:32 * m + 16, at] + lens[32 * m + 16:32 * m + 32, at]
     row, lane = iota((128, 128), 0), iota((128, 128), 1) & 31
     spot = ((lane >= 18) & (lane < 21) & (row == 16 * (lane - 18) + 15)) | ((lane >= 21) & (lane < 24) & (row == 16 * (lane - 21)))
     sides = dot(lenses[...].astype(BF16), spot.astype(BF16))
@@ -362,15 +364,24 @@
         out[...] = packed
 
 
+def unpack_kernel(a0, a2, out):
+    for k, ref in enumerate((a0, a2)):
+        for c in range(4):
+            out[4 * k + c] = ref[...] if c == 0 else pltpu.roll(ref[...], 128 - 32 * c, 1)
+
+
 def order(a):
     return a - 1 if 0 < a < 9 else 8 + a // 9
 
 
-def detector_kernel(kernel, a0, a1, a2, a3, lenses, out, arrived, base, across, image, sems):
-    w, s, y, z, x, core, sign, pair = place_of()
-    for k, ref in enumerate((a0, a1, a2, a3)):
+def detector_kernel(kernel, begun, a1, a3, lenses, out, arrived, base, across, image, sems):
+    w, s, y, z, x, core, sign, pair = place_of()
+    for k, ref in ((1, a1), (3, a3)):
         for c in range(4):
             arrived[4 * ((x - k + 4) & 3) + c] = ref[...] if c == 0 else pltpu.roll(ref[...], 128 - 32 * c, 1)
+    for k in (0, 2):
+        for c in range(4):
+            arrived[4 * ((x - k + 4) & 3) + c] = begun[2 * k + c]
     spot = (iota((128, 640), 0) == (iota((128, 640), 1) >> 5)) & (iota((128, 640), 1) < 18 * DPIX)
     spot = spot.astype(BF16)
     left, own, right = arrived[jnp.maximum(2 * w - 2, 0)], lenses[...], arrived[jnp.minimum(2 * w + 2, WAVES - 1)]
@@ -384,9 +395,10 @@
                 jnp.where(lane == 17, pltpu.roll(right, 128 - 4 - c, 1), pltpu.roll(own, 129 - 16 * c if c else 1, 1)),
             )
         )
-    wide = dot(jnp.concatenate(tables, axis=0).astype(BF16), spot)
-    row, column, count = wide[0:16] * 0.25, wide[16:32], wide[32:48]
-    values = sum(dot(part, spot) for part in split2(arrived[...].reshape(WAVES * 16, 128)))
+    parts = list(split2(arrived[...].reshape(WAVES * 16, 128)))
+    wide = dot(jnp.concatenate(parts + [jnp.concatenate(tables, axis=0).astype(BF16)], axis=0), spot)
+    values, tables = wide[:16 * WAVES] + wide[16 * WAVES:32 * WAVES], wide[32 * WAVES:]
+    row, column, count = tables[0:16] * 0.25, tables[16:32], tables[32:48]
     offset = 0.5 * ((iota((16, 640), 1) & 31).astype(F32) - column)
     falling, rising = jnp.exp(-offset), jnp.exp(offset)
     spread = 0.0
@@ -439,7 +451,7 @@
         copy.wait()
 
 
-def call(kernel, outs, in_smem, n_in, scratch=(), tail=(), limit=40, outside=False):
+def call(kernel, outs, in_smem, n_in, scratch=(), tail=(), limit=40, outside=False, aliases=None):
     specs = [pl.BlockSpec(memory_space=pltpu.SMEM)] * in_smem
     specs += [pl.BlockSpec(memory_space=pltpu.VMEM)] * (n_in - in_smem)
     specs[n_in - len(tail):] = tail
@@ -451,6 +463,7 @@
         in_specs=specs,
         out_specs=pl.BlockSpec(memory_space=pl.ANY) if outside else vmem if single else [vmem] * len(outs),
         scratch_shapes=list(scratch),
+        input_output_aliases=aliases or {},
         compiler_params=pltpu.CompilerParams(vmem_limit_bytes=limit * 2**20),
         name=getattr(kernel, "func", kernel).__name__,
     )
@@ -486,30 +499,41 @@
         tail=anywhere * 7,
         limit=54,
     )(amplitude, seg_map, seg_table.T, focal_mask, trace_row, trace_col, block_count)
-    utab = call(focal_table_kernel, shape(2, 4, 2 * UROWS, 256, dtype=BF16), 0, 1, tail=anywhere)(piece)
+    utab, vtab, spot = call(
+        table_kernel,
+        [shape(2, 4, 4 * UROWS, 256, dtype=BF16), shape(2, 2, 2, HALF, FHALF, dtype=BF16), shape(128, 768, dtype=BF16)],
+        0,
+        1,
+        tail=anywhere,
+    )(piece)
     p1 = lax.ppermute(up, "slab", along_z(1))
     p3 = lax.ppermute(down, "slab", along_z(3))
     p2 = lax.ppermute(piece, "slab", along_z(2))
-    own, wrap = call(merge_kernel, [shape(2, MROWS, 128), shape(EDGE, 128)], 0, 5, tail=anywhere)(
-        piece, p1, p2, p3, utab
-    )
-    vtab, smat = call(
-        lens_table_kernel, [shape(2, 2, 2, HALF, FHALF, dtype=BF16), shape(NF, 256, dtype=BF16)], 0, 1, tail=anywhere
-    )(own)
-    partner = lax.ppermute(own, "slab", along_y((3, 2, 1, 0)))
-    beside = lax.ppermute(own, "slab", along_y((1, 0, 3, 2)))
+    begun = call(opposite_kernel, shape(2 * MROWS, 128), 0, 3, tail=anywhere)(piece, p2, utab)
+    own, more = call(
+        merge_kernel, [shape(2 * MROWS, 128), shape(2 * MROWS + EDGE, 128)], 0, 3, aliases={0: 0}
+    )(begun, p1, p3)
+    partner = lax.ppermute(more, "slab", along_y((3, 2, 1, 0)))
+    beside = lax.ppermute(more, "slab", along_y((1, 0, 3, 2)))
     last = lax.ppermute(own, "slab", along_y((2, 3, 0, 1)))
-    edge = lax.ppermute(
-        wrap, "slab", [(4 * y, 4 * y + 4) for y in range(3)] + [(4 * y + 7, 4 * y + 3) for y in range(3)]
-    )
-    scratch = [pltpu.VMEM((4, 256, 512), BF16)] * 2
-    before = call(first_kernel, shape(4, UROWS, 512), 0, 4, scratch, tail=anywhere)(own, partner, utab, smat)
-    keep, give = call(second_kernel, [shape(2, UROWS, 512)] * 2, 0, 5, scratch, tail=anywhere)(
-        beside, last, utab, before, edge
-    )
-    weight, lenses = call(weight_kernel, [shape(UROWS, NF), shape(16, 128)], 0, 6, tail=anywhere)(
-        focal_mask, p1, p3, edge, trace, give
-    )
+    scratch = [pltpu.VMEM((4, 256, 256), BF16)] * 2
+
+    def add(group, p, flipped, *before, outs=shape(4, 2 * UROWS, 256), **options):
+        kernel = functools.partial(group_kernel, p=p, flipped=flipped)
+        return call(kernel, outs, 0, 3 + len(before), scratch, **options)(group, utab, spot, *before)
+
+    field = add(own, 0, False)
+    field = add(partner, 0, True, field)
+    field = add(beside, 1, False, field)
+    keep, give = add(last, 1, True, field, outs=[shape(2, 2 * UROWS, 256)] * 2)
+    weight, lenses, smat = call(
+        weight_kernel,
+        [shape(UROWS, NF), shape(16, 128), shape(NF, 256, dtype=BF16)],
+        0,
+        7,
+        [pltpu.VMEM((8, UROWS, 128), F32)],
+        tail=anywhere,
+    )(focal_mask, p1, p3, partner, beside, trace, give)
     sibling = [(i, i ^ 1) for i in range(NWAV)]
     crossed = lax.ppermute(give, "wav", sibling)
     mine, other = call(lens_kernel, [shape(32, 128)] * 2, 0, 6)(
@@ -525,11 +549,12 @@
         mine, got, opposite
     )
     a1, a3 = along_x(forth, 1), along_x(back, 3)
+    begun = call(unpack_kernel, shape(8, 16, 128), 0, 2)(kept, a2)
     return call(
         detector_kernel,
         shape(256, 512),
         0,
-        6,
+        5,
         [
             pltpu.VMEM((WAVES, 16, 128), F32),
             pltpu.VMEM((10, 16, 512), F32),
@@ -538,7 +563,7 @@
             pltpu.SemaphoreType.DMA((4,)),
         ],
         outside=True,
-    )(crosstalk, kept, a1, a2, a3, lenses)
+    )(crosstalk, begun, a1, a3, lenses)
 
 
 def solution(mesh):

time: 40.2 us -> 38.2 us (0.950)
  starting transfers between devices: 19 us -> 17.5 us
  waiting for transfers between devices: 8.33 us -> 7.74 us
    ppermute x3 -> x2, starting transfers between devices: 7.01 us -> 3.24 us  [the longest x1 3.1 us: body(): partner = lax.ppermute(more, 'slab', along_y((3, 2, 1, 0)))]
    ppermute x3 -> x2, waiting for transfers between devices: 0.01 us -> 2.65 us  [the longest x1 2.59 us: body(): partner = lax.ppermute(more, 'slab', along_y((3, 2, 1, 0)))]
    ppermute x3, waiting for transfers between devices: 3.34 us -> 1.55 us  [along_x(): lax.ppermute(sent, 'wav', [(i, (i + 2 * k) % NWAV) for i in range(NWAV)])]
    ppermute x1, waiting for transfers between devices: 2.61 us -> 0.87 us  [body(): p2 = lax.ppermute(piece, 'slab', along_z(2))]
    ppermute x3, starting transfers between devices: 5.12 us -> 6.36 us  [along_x(): lax.ppermute(sent, 'wav', [(i, (i + 2 * k) % NWAV) for i in range(NWAV)])]
    ppermute x1, starting transfers between devices: 0.63 us -> 1.54 us  [body(): last = lax.ppermute(own, 'slab', along_y((2, 3, 0, 1)))]
    pallas_call x7 -> x10, Pallas kernels: 7.58 us -> 8.26 us  [the longest x4 3.44 us: add(): call(kernel, outs, 0, 3 + len(before), scratch, **options)]
    pallas_call x1, Pallas kernels: 1.51 us -> 0.91 us  [body(): call(lens_kernel, [shape(32, 128)] * 2, 0, 6)]
  transfers between devices with their start and end apart: 12 -> 11, of which waited for: 5 -> 7; matrix products, arithmetic and copies ran while one was open for 0% -> 0% of each run, Pallas kernels for 10% -> 14%
where the time goes in v3:
time: 38.2 us; the launch traced here: 37.6 us
  starting transfers between devices  17.5 us (46%)
  Pallas kernels  11.4 us (30%)
  waiting for transfers between devices  7.74 us (20%)
  local copies, waits for them, and re-layouts  0.83 us (2%)
    ppermute x3, starting transfers between devices, along_x(): lax.ppermute(sent, 'wav', [(i, (i + 2 * k) % NWAV) for i in range(NWAV)])  6.36 us
    pallas_call x4, Pallas kernels, add(): call(kernel, outs, 0, 3 + len(before), scratch, **options)  3.44 us
    ppermute x1, starting transfers between devices, body(): partner = lax.ppermute(more, 'slab', along_y((3, 2, 1, 0)))  3.1 us
    ppermute x1, waiting for transfers between devices, body(): partner = lax.ppermute(more, 'slab', along_y((3, 2, 1, 0)))  2.59 us
    pallas_call x1, Pallas kernels, body(): call(table_kernel, [shape(2, 4, 4 * UROWS, 256, dtype=BF16), shape(2, 2,...  2.24 us
    ppermute x1, starting transfers between devices, body(): p3 = lax.ppermute(down, 'slab', along_z(3))  2.2 us
    pallas_call x1, Pallas kernels, body(): call(prepare_kernel, [shape(PIECE, 128), shape(PIECE + EDGE, 128), shape(...  2.1 us
    ppermute x1, starting transfers between devices, body(): p1 = lax.ppermute(up, 'slab', along_z(1))  2.07 us
  transfers between devices with their start and end apart: 11, of which 7 were waited for; matrix products, arithmetic and copies ran while one was open for 0% of the time, Pallas kernels for 14%

profile of v3, /device:TPU:0, one launch (start us, length us, event | category | flops | bytes accessed | tf_op | source)
XLA Modules:
  0.0 37.6 jit_solution(14853153870881514267)
XLA Ops:
  0.0 2.1 %prepare_kernel.1 = (f32[80,128]{1,0:T(8,128)}, f32[152,128]{1,0:T(8,128)}, f32[152,128]{1,0:T(8,128)}, f32[8,128]{1,0:T(8,128)}) custom-call(f32[32,512]{1,0:T(8,128)} %amp_in.1, s32[32,512]{1,0:T(8,128)} %seg_in.1, s32[3,798]{1,0:T(4,128)} %bitcast.1, f32[64,1024]{1,0:T(8,128)} %mask.3, s32[8,16]{1,0:T(8,128)} %trow.1, s32[8,16]{1,0:T(8,128)} %tcol.1, ...), custom_call_target="tpu_custom_call" | custom-call | tf_op jit(solution)/shard_map/prepare_kernel/pallas_call | solution.py:486
  2.1 2.1 %collective-permute-start.1 = (f32[152,128]{1,0:T(8,128)}, f32[152,128]{1,0:T(8,128)S(1)}, u32[]{:S(2)}, u32[]{:S(2)}) collective-permute-start(f32[152,128]{1,0:T(8,128)} %get-tuple-element.26), channel_id=1, source_target_pairs={{0,1},{1,2},{2,3},{3,0},{4,5},{5,6},{6,7},{7,4},{8,9},{9,10},{10,1... | collective-permute-start | bytes 233480 | tf_op jit(solution)/shard_map/ppermute | solution.py:509
  4.2 2.2 %collective-permute-start.2 = (f32[152,128]{1,0:T(8,128)}, f32[152,128]{1,0:T(8,128)S(1)}, u32[]{:S(2)}, u32[]{:S(2)}) collective-permute-start(f32[152,128]{1,0:T(8,128)} %get-tuple-element.27), channel_id=1, source_target_pairs={{0,3},{1,0},{2,1},{3,2},{4,7},{5,4},{6,5},{7,6},{8,11},{9,8},{10,9... | collective-permute-start | bytes 233480 | tf_op jit(solution)/shard_map/ppermute | solution.py:510
  6.4 1.8 %collective-permute-start = (f32[80,128]{1,0:T(8,128)}, f32[80,128]{1,0:T(8,128)S(1)}, u32[]{:S(2)}, u32[]{:S(2)}) collective-permute-start(f32[80,128]{1,0:T(8,128)} %get-tuple-element.24.after.p0), channel_id=1, source_target_pairs={{0,2},{1,3},{2,0},{3,1},{4,6},{5,7},{6,4},{7,5},{8,10},{9,11},{10,... | collective-permute-start | bytes 122888 | tf_op jit(solution)/shard_map/ppermute | solution.py:511
  8.2 0.0 copy-start.1
  8.2 0.8 %copy-done.1 = f32[80,128]{1,0:T(8,128)S(1)} copy-done((f32[80,128]{1,0:T(8,128)S(1)}, f32[80,128]{1,0:T(8,128)}, u32[]{:S(2)}) %copy-start.1) | copy-done | bytes 40984
  9.0 2.2 %table_kernel.1 = (bf16[2,4,320,256]{3,2,1,0:T(8,128)(2,1)S(1)}, bf16[2,2,2,256,512]{4,3,2,1,0:T(8,128)(2,1)S(1)}, bf16[128,768]{1,0:T(8,128)(2,1)S(1)}) custom-call(f32[80,128]{1,0:T(8,128)S(1)} %copy-done.1), custom_call_target="tpu_custom_call" | custom-call | tf_op jit(solution)/shard_map/table_kernel/pallas_call | solution.py:502
  11.2 0.9 %collective-permute-done.p2 = f32[80,128]{1,0:T(8,128)S(1)} collective-permute-done((f32[80,128]{1,0:T(8,128)}, f32[80,128]{1,0:T(8,128)S(1)}, u32[]{:S(2)}, u32[]{:S(2)}) %collective-permute-start) | collective-permute-done | bytes 40992 | tf_op jit(solution)/shard_map/ppermute | solution.py:511
  12.1 0.0 collective-permute-done.1.p1
  12.1 0.0 collective-permute-done.2.p3
  12.1 0.1 merge_kernel.1
  12.2 3.1 %collective-permute-start.5 = (f32[344,128]{1,0:T(8,128)S(1)}, f32[344,128]{1,0:T(8,128)S(1)}, u32[]{:S(2)}, u32[]{:S(2)}) collective-permute-start(f32[344,128]{1,0:T(8,128)S(1)} %get-tuple-element.30), channel_id=1, source_target_pairs={{0,12},{1,13},{2,14},{3,15},{4,8},{5,9},{6,10},{7,11},{8,4},{9,5},... | collective-permute-start | bytes 528392 | tf_op jit(solution)/shard_map/ppermute | solution.py:516
  15.3 0.1 collective-permute-start.4
  15.5 1.5 %collective-permute-start.3 = (f32[272,128]{1,0:T(8,128)S(1)}, f32[272,128]{1,0:T(8,128)S(1)}, u32[]{:S(2)}, u32[]{:S(2)}) collective-permute-start(f32[272,128]{1,0:T(8,128)S(1)} %get-tuple-element.28.ref), channel_id=1, source_target_pairs={{0,8},{1,9},{2,10},{3,11},{4,12},{5,13},{6,14},{7,15},{8,0},{9,1},... | collective-permute-start | bytes 417800 | tf_op jit(solution)/shard_map/ppermute | solution.py:518
  17.0 0.9 %group_kernel.4.refs_0_ = f32[4,160,256]{2,1,0:T(8,128)S(1)} custom-call(f32[272,128]{1,0:T(8,128)S(1)} %get-tuple-element.28.ref, bf16[2,4,320,256]{3,2,1,0:T(8,128)(2,1)S(1)} %get-tuple-element.25.after.utab, bf16[128,768]{1,0:T(8,128)(2,1)S(1)} %get-tuple-element.29.spot), custom_call_target="tpu_custom_call" | custom-call | tf_op jit(solution)/shard_map/group_kernel/pallas_call | solution.py:523
  17.9 2.6 %collective-permute-done.5.ref.partner = f32[344,128]{1,0:T(8,128)S(1)} collective-permute-done((f32[344,128]{1,0:T(8,128)S(1)}, f32[344,128]{1,0:T(8,128)S(1)}, u32[]{:S(2)}, u32[]{:S(2)}) %collective-permute-start.5) | collective-permute-done | bytes 176160 | tf_op jit(solution)/shard_map/ppermute | solution.py:516
  20.5 0.9 %group_kernel.5.refs_0_ = f32[4,160,256]{2,1,0:T(8,128)S(1)} custom-call(f32[344,128]{1,0:T(8,128)S(1)} %collective-permute-done.5.ref.partner, bf16[2,4,320,256]{3,2,1,0:T(8,128)(2,1)S(1)} %get-tuple-element.25.after.utab, bf16[128,768]{1,0:T(8,128)(2,1)S(1)} %get-tuple-element.29.spot, f32[4,160,256]{2,1,0:T(8,128)S(1)} %group_kernel.4.refs_0_), custom_call_target="tpu_custom_call" | custom-call | tf_op jit(solution)/shard_map/group_kernel/pallas_call | solution.py:523
  21.3 0.0 copy-start
  21.3 0.0 copy-start.3
  21.4 0.1 collective-permute-done.4.ref.beside
  21.4 0.9 %group_kernel.6.refs_0_ = f32[4,160,256]{2,1,0:T(8,128)S(1)} custom-call(f32[344,128]{1,0:T(8,128)S(1)} %collective-permute-done.4.ref.beside, bf16[2,4,320,256]{3,2,1,0:T(8,128)(2,1)S(1)} %get-tuple-element.25.after.utab, bf16[128,768]{1,0:T(8,128)(2,1)S(1)} %get-tuple-element.29.spot, f32[4,160,256]{2,1,0:T(8,128)S(1)} %group_kernel.5.refs_0_), custom_call_target="tpu_custom_call" | custom-call | tf_op jit(solution)/shard_map/group_kernel/pallas_call | solution.py:523
  22.3 0.4 %collective-permute-done.3.ref = f32[272,128]{1,0:T(8,128)S(1)} collective-permute-done((f32[272,128]{1,0:T(8,128)S(1)}, f32[272,128]{1,0:T(8,128)S(1)}, u32[]{:S(2)}, u32[]{:S(2)}) %collective-permute-start.3) | collective-permute-done | bytes 139296 | tf_op jit(solution)/shard_map/ppermute | solution.py:518
  22.7 0.9 %group_kernel.7 = (f32[2,160,256]{2,1,0:T(8,128)S(1)}, f32[2,160,256]{2,1,0:T(8,128)S(1)}) custom-call(f32[272,128]{1,0:T(8,128)S(1)} %collective-permute-done.3.ref, bf16[2,4,320,256]{3,2,1,0:T(8,128)(2,1)S(1)} %get-tuple-element.25.after.utab, bf16[128,768]{1,0:T(8,128)(2,1)S(1)} %get-tuple-element.29.spot, f32[4,160,256]{2,1,0:T(8,128)S(1)} %group_kernel.6.refs_0_), custom_call_target="tpu_custom_call" | custom-call | tf_op jit(solution)/shard_map/group_kernel/pallas_call | solution.py:523
  23.6 0.1 collective-permute-start.6
  23.7 0.0 copy-done
  23.7 0.0 copy-done.3
  23.7 0.4 %weight_kernel.1 = (f32[80,1024]{1,0:T(8,128)S(1)}, f32[16,128]{1,0:T(8,128)S(1)}, bf16[1024,256]{1,0:T(8,128)(2,1)S(1)}) custom-call(f32[64,1024]{1,0:T(8,128)S(1)} %copy-done, f32[152,128]{1,0:T(8,128)S(1)} %collective-permute-done.1.p1, f32[152,128]{1,0:T(8,128)S(1)} %collective-permute-done.2.p3, f32[344,128]{1,0:T(8,128)S(1)} %collective-permute-done.5.ref.partner, ...), custom_call_target="tpu_custom_call" | custom-call | tf_op jit(solution)/shard_map/weight_kernel/pallas_call | solution.py:529
  24.1 0.0 copy-start.2
  24.1 1.2 %collective-permute-done.6.got = f32[2,160,256]{2,1,0:T(8,128)S(1)} collective-permute-done((f32[2,160,256]{2,1,0:T(8,128)S(1)}, f32[2,160,256]{2,1,0:T(8,128)S(1)}, u32[]{:S(2)}, u32[]{:S(2)}) %collective-permute-start.6) | collective-permute-done | bytes 327712 | tf_op jit(solution)/shard_map/ppermute | solution.py:538
  25.3 0.9 %lens_kernel.1 = (f32[32,128]{1,0:T(8,128)S(1)}, f32[32,128]{1,0:T(8,128)S(1)}) custom-call(f32[2,160,256]{2,1,0:T(8,128)S(1)} %get-tuple-element.31.keep, f32[2,160,256]{2,1,0:T(8,128)S(1)} %collective-permute-done.6.got, bf16[2,2,2,256,512]{4,3,2,1,0:T(8,128)(2,1)S(1)} %get-tuple-element.33.vtab, f32[80,1024]{1,0:T(8,128)S(1)} %get-tuple-element.35.weight, ...), custom_call_target="tpu_custom_call" | custom-call | tf_op jit(solution)/shard_map/lens_kernel/pallas_call | solution.py:539
  26.2 0.2 collective-permute-start.7
  26.4 1.0 %collective-permute-done.7.got = f32[32,128]{1,0:T(8,128)S(1)} collective-permute-done((f32[32,128]{1,0:T(8,128)S(1)}, f32[32,128]{1,0:T(8,128)S(1)}, u32[]{:S(2)}, u32[]{:S(2)}) %collective-permute-start.7) | collective-permute-done | bytes 16416 | tf_op jit(solution)/shard_map/ppermute | solution.py:542
  27.5 0.1 pack_kernel.2.after
  27.5 3.1 %collective-permute-start.8 = (f32[16,128]{1,0:T(8,128)S(1)}, f32[16,128]{1,0:T(8,128)S(1)}, u32[]{:S(2)}, u32[]{:S(2)}) collective-permute-start(f32[16,128]{1,0:T(8,128)S(1)} %pack_kernel.2.after), channel_id=1, source_target_pairs={{0,64},{16,80},{32,96},{48,112},{64,0},{80,16},{96,32},{112,48},{1... | collective-permute-start | bytes 24584 | tf_op jit(solution)/shard_map/ppermute | solution.py:544
  30.6 0.1 pack_kernel.3
  30.7 0.7 %collective-permute-start.9 = (f32[16,128]{1,0:T(8,128)S(1)}, f32[16,128]{1,0:T(8,128)S(1)}, u32[]{:S(2)}, u32[]{:S(2)}) collective-permute-start(f32[16,128]{1,0:T(8,128)S(1)} %get-tuple-element.41), channel_id=1, source_target_pairs={{0,32},{16,48},{32,64},{48,80},{64,96},{80,112},{96,0},{112,16},{1... | collective-permute-start | bytes 24584 | tf_op jit(solution)/shard_map/ppermute | solution.py:544
  31.3 2.6 %collective-permute-start.10 = (f32[16,128]{1,0:T(8,128)S(1)}, f32[16,128]{1,0:T(8,128)S(1)}, u32[]{:S(2)}, u32[]{:S(2)}) collective-permute-start(f32[16,128]{1,0:T(8,128)S(1)} %get-tuple-element.42), channel_id=1, source_target_pairs={{0,96},{16,112},{32,0},{48,16},{64,32},{80,48},{96,64},{112,80},{1... | collective-permute-start | bytes 24584 | tf_op jit(solution)/shard_map/ppermute | solution.py:544
  34.0 0.0 collective-permute-done.8.a2
  34.0 0.1 unpack_kernel.1.begun
  34.1 1.5 %collective-permute-done.9.a1 = f32[16,128]{1,0:T(8,128)S(1)} collective-permute-done((f32[16,128]{1,0:T(8,128)S(1)}, f32[16,128]{1,0:T(8,128)S(1)}, u32[]{:S(2)}, u32[]{:S(2)}) %collective-permute-start.9) | collective-permute-done | bytes 8224 | tf_op jit(solution)/shard_map/ppermute | solution.py:544
  35.6 0.0 collective-permute-done.10.a3
  35.6 0.0 copy-done.2
  35.6 2.0 %detector_kernel.1 = f32[256,512]{1,0:T(8,128)} custom-call(f32[5,5]{1,0:T(8,128)S(1)} %copy-done.2, f32[8,16,128]{2,1,0:T(8,128)S(1)} %unpack_kernel.1.begun, f32[16,128]{1,0:T(8,128)S(1)} %collective-permute-done.9.a1, f32[16,128]{1,0:T(8,128)S(1)} %collective-permute-done.10.a3, f32[16,128]{1,0:T(8,128)S(1)} %get-tuple-element.37.lenses.after), custom_call_target="tpu_custom_call" | custom-call | tf_op jit(solution)/shard_map/detector_kernel/pallas_call | solution.py:553
  (1 shorter events, 0.0 us)
Async XLA Ops:
  2.1 10.0 %collective-permute-start.1 = (f32[152,128]{1,0:T(8,128)}, f32[152,128]{1,0:T(8,128)S(1)}, u32[]{:S(2)}, u32[]{:S(2)}) collective-permute-start(f32[152,128]{1,0:T(8,128)} %get-tuple-element.26), channel_id=1, source_target_pairs={{0,1},{1,2},{2,3},{3,0},{4,5},{5,6},{6,7},{7,4},{8,9},{9,10},{10,1... | collective-permute-start | bytes 233480 | tf_op jit(solution)/shard_map/ppermute | solution.py:509
  4.2 8.0 %collective-permute-start.2 = (f32[152,128]{1,0:T(8,128)}, f32[152,128]{1,0:T(8,128)S(1)}, u32[]{:S(2)}, u32[]{:S(2)}) collective-permute-start(f32[152,128]{1,0:T(8,128)} %get-tuple-element.27), channel_id=1, source_target_pairs={{0,3},{1,0},{2,1},{3,2},{4,7},{5,4},{6,5},{7,6},{8,11},{9,8},{10,9... | collective-permute-start | bytes 233480 | tf_op jit(solution)/shard_map/ppermute | solution.py:510
  6.4 5.7 %collective-permute-start = (f32[80,128]{1,0:T(8,128)}, f32[80,128]{1,0:T(8,128)S(1)}, u32[]{:S(2)}, u32[]{:S(2)}) collective-permute-start(f32[80,128]{1,0:T(8,128)} %get-tuple-element.24.after.p0), channel_id=1, source_target_pairs={{0,2},{1,3},{2,0},{3,1},{4,6},{5,7},{6,4},{7,5},{8,10},{9,11},{10,... | collective-permute-start | bytes 122888 | tf_op jit(solution)/shard_map/ppermute | solution.py:511
  8.2 0.8 %copy-start.1 = (f32[80,128]{1,0:T(8,128)S(1)}, f32[80,128]{1,0:T(8,128)}, u32[]{:S(2)}) copy-start(f32[80,128]{1,0:T(8,128)} %get-tuple-element.24.after.p0) | copy-start | bytes 122884
  12.2 8.2 %collective-permute-start.5 = (f32[344,128]{1,0:T(8,128)S(1)}, f32[344,128]{1,0:T(8,128)S(1)}, u32[]{:S(2)}, u32[]{:S(2)}) collective-permute-start(f32[344,128]{1,0:T(8,128)S(1)} %get-tuple-element.30), channel_id=1, source_target_pairs={{0,12},{1,13},{2,14},{3,15},{4,8},{5,9},{6,10},{7,11},{8,4},{9,5},... | collective-permute-start | bytes 528392 | tf_op jit(solution)/shard_map/ppermute | solution.py:516
  15.3 6.1 %collective-permute-start.4 = (f32[344,128]{1,0:T(8,128)S(1)}, f32[344,128]{1,0:T(8,128)S(1)}, u32[]{:S(2)}, u32[]{:S(2)}) collective-permute-start(f32[344,128]{1,0:T(8,128)S(1)} %get-tuple-element.30), channel_id=1, source_target_pairs={{0,4},{1,5},{2,6},{3,7},{4,0},{5,1},{6,2},{7,3},{8,12},{9,13},{10,... | collective-permute-start | bytes 528392 | tf_op jit(solution)/shard_map/ppermute | solution.py:517
  15.5 7.2 %collective-permute-start.3 = (f32[272,128]{1,0:T(8,128)S(1)}, f32[272,128]{1,0:T(8,128)S(1)}, u32[]{:S(2)}, u32[]{:S(2)}) collective-permute-start(f32[272,128]{1,0:T(8,128)S(1)} %get-tuple-element.28.ref), channel_id=1, source_target_pairs={{0,8},{1,9},{2,10},{3,11},{4,12},{5,13},{6,14},{7,15},{8,0},{9,1},... | collective-permute-start | bytes 417800 | tf_op jit(solution)/shard_map/ppermute | solution.py:518
  21.3 2.3 %copy-start = (f32[64,1024]{1,0:T(8,128)S(1)}, f32[64,1024]{1,0:T(8,128)}, u32[]{:S(2)}) copy-start(f32[64,1024]{1,0:T(8,128)} %mask.3) | copy-start | bytes 786436
  21.3 2.3 %copy-start.3 = (f32[8,128]{1,0:T(8,128)S(1)}, f32[8,128]{1,0:T(8,128)}, u32[]{:S(2)}) copy-start(f32[8,128]{1,0:T(8,128)} %get-tuple-element.34.trace) | copy-start | bytes 12292
  23.6 1.7 %collective-permute-start.6 = (f32[2,160,256]{2,1,0:T(8,128)S(1)}, f32[2,160,256]{2,1,0:T(8,128)S(1)}, u32[]{:S(2)}, u32[]{:S(2)}) collective-permute-start(f32[2,160,256]{2,1,0:T(8,128)S(1)} %get-tuple-element.32.after), channel_id=1, source_target_pairs={{0,16},{16,0},{32,48},{48,32},{64,80},{80,64},{96,112},{112,96},{1... | collective-permute-start | bytes 983048 | tf_op jit(solution)/shard_map/ppermute | solution.py:538
  24.1 11.5 %copy-start.2 = (f32[5,5]{1,0:T(8,128)S(1)}, f32[5,5]{1,0:T(8,128)}, u32[]{:S(2)}) copy-start(f32[5,5]{1,0:T(8,128)} %kernel.1) | copy-start | bytes 304
  26.2 1.3 %collective-permute-start.7 = (f32[32,128]{1,0:T(8,128)S(1)}, f32[32,128]{1,0:T(8,128)S(1)}, u32[]{:S(2)}, u32[]{:S(2)}) collective-permute-start(f32[32,128]{1,0:T(8,128)S(1)} %get-tuple-element.39), channel_id=1, source_target_pairs={{0,16},{16,0},{32,48},{48,32},{64,80},{80,64},{96,112},{112,96},{1... | collective-permute-start | bytes 49160 | tf_op jit(solution)/shard_map/ppermute | solution.py:542
  27.5 6.5 %collective-permute-start.8 = (f32[16,128]{1,0:T(8,128)S(1)}, f32[16,128]{1,0:T(8,128)S(1)}, u32[]{:S(2)}, u32[]{:S(2)}) collective-permute-start(f32[16,128]{1,0:T(8,128)S(1)} %pack_kernel.2.after), channel_id=1, source_target_pairs={{0,64},{16,80},{32,96},{48,112},{64,0},{80,16},{96,32},{112,48},{1... | collective-permute-start | bytes 24584 | tf_op jit(solution)/shard_map/ppermute | solution.py:544
  30.7 4.9 %collective-permute-start.9 = (f32[16,128]{1,0:T(8,128)S(1)}, f32[16,128]{1,0:T(8,128)S(1)}, u32[]{:S(2)}, u32[]{:S(2)}) collective-permute-start(f32[16,128]{1,0:T(8,128)S(1)} %get-tuple-element.41), channel_id=1, source_target_pairs={{0,32},{16,48},{32,64},{48,80},{64,96},{80,112},{96,0},{112,16},{1... | collective-permute-start | bytes 24584 | tf_op jit(solution)/shard_map/ppermute | solution.py:544
  31.3 4.3 %collective-permute-start.10 = (f32[16,128]{1,0:T(8,128)S(1)}, f32[16,128]{1,0:T(8,128)S(1)}, u32[]{:S(2)}, u32[]{:S(2)}) collective-permute-start(f32[16,128]{1,0:T(8,128)S(1)} %get-tuple-element.42), channel_id=1, source_target_pairs={{0,96},{16,112},{32,0},{48,16},{64,32},{80,48},{96,64},{112,80},{1... | collective-permute-start | bytes 24584 | tf_op jit(solution)/shard_map/ppermute | solution.py:544

commit v4 on v3

--- a/solution.py
+++ b/solution.py
@@ -17,7 +17,7 @@
 FROWS = NF // NSLAB
 UROWS = FROWS + 16
 GROUP = 128
-PIECE, EDGE = 2 * (ROWS + 8), 72
+PIECE, EDGE = 2 * (ROWS + 8), 40
 MROWS = GROUP + 8
 HALF, FHALF = NP // 2, NF // 2
 
@@ -76,6 +76,7 @@
 
 def prepare_kernel(amp_in, seg_in, tab_in, mask, trow, tcol, count, out, up, down, trace, amp, seg, tab, tables, edges, sems):
     w, s, y, z, x, core, sign, pair = place_of()
+    half = pl.ds(pl.multiple_of(FHALF * core, FHALF), FHALF)
     copies = [
         pltpu.make_async_copy(a, b, sems.at[k])
         for k, (a, b) in enumerate(
@@ -87,8 +88,8 @@
                 (trow, tables.at[0]),
                 (tcol, tables.at[1]),
                 (count, tables.at[2]),
-                (mask.at[FROWS - 8:FROWS, :], edges.at[0]),
-                (mask.at[0:8, :], edges.at[1]),
+                (mask.at[FROWS - 8:FROWS, half], edges.at[0]),
+                (mask.at[0:8, half], edges.at[1]),
             )
         )
     ]
@@ -102,15 +103,15 @@
     pick = ((iota((NP, 128), 0) == 16 * (lane & 31)) & (lane < 96)).astype(BF16)
     out[...] = jnp.zeros((PIECE, 128), F32)
     for ref in (up, down):
-        ref[PIECE + 64:PIECE + EDGE, :] = jnp.zeros((8, 128), F32)
+        ref[PIECE + 32:PIECE + EDGE, :] = jnp.zeros((8, 128), F32)
     trace[...] = jnp.zeros((8, 128), F32)
     for copy in copies:
         copy.wait()
     for c in range(3):
         table = tables[c].astype(F32)
         trace[:, 16 * c:16 * c + 16] = table
-        up[PIECE + 64:PIECE + 65, 16 * c:16 * c + 16] = table[7:8]
-        down[PIECE + 64:PIECE + 65, 16 * c:16 * c + 16] = table[0:1]
+        up[PIECE + 32:PIECE + 33, 16 * c:16 * c + 16] = table[7:8]
+        down[PIECE + 32:PIECE + 33, 16 * c:16 * c + 16] = table[0:1]
     ids = dot(jnp.concatenate(split2(seg[...].astype(F32)), axis=0), pick)
     ids = ids[0:16] + ids[16:32]
     upper_ids, lower_ids = ids[0:1], ids[8:9]
@@ -134,7 +135,7 @@
         out[(ROWS + 8) * k:(ROWS + 8) * k + ROWS, :] = sum(found[:, 128 * q:128 * q + 128] for q in range(3 * k, 3 * k + 3))
     for k, ref in enumerate((up, down)):
         ref[0:PIECE, :] = out[...]
-        for q in range(8):
+        for q in range(4):
             ref[PIECE + 8 * q:PIECE + 8 * q + 8, :] = edges[k, :, 128 * q:128 * q + 128]
 
 
@@ -166,7 +167,9 @@
     w, s, y, z, x, core, sign, pair = place_of()
     place_pieces(out, ((1, p1), (3, p3)))
     more[0:2 * MROWS, :] = out[...]
-    more[2 * MROWS:2 * MROWS + EDGE, :] = jnp.where(z == 0, p1[PIECE:PIECE + EDGE, :], p3[PIECE:PIECE + EDGE, :])
+    wrap = jnp.where(z == 0, p1[PIECE:PIECE + EDGE, :], p3[PIECE:PIECE + EDGE, :])
+    more[2 * MROWS:2 * MROWS + 32, :] = wrap[0:32]
+    more[MROWS + GROUP:2 * MROWS, :] = wrap[32:EDGE]
 
 
 def wavelength(w):
@@ -229,34 +232,43 @@
         lax.fori_loop(0, HALF // 16, chunk, 0)
 
 
-def weight_kernel(mask, p1, p3, partner, beside, trace, after, weight, lenses, smat, full):
-    del after
-    w, s, y, z, x, core, sign, pair = place_of()
-    rows = slice(2 * MROWS, 2 * MROWS + EDGE)
-    across = jnp.where(jnp.where(z == 0, y == 2, y == 1), partner[rows, :], beside[rows, :])
-    across = jnp.where(jnp.where(z == 0, y == 0, y == 3), 0.0, across)
-    above = jnp.where(z == 0, across, p1[PIECE:PIECE + EDGE, :])
-    below = jnp.where(z == 3, across, p3[PIECE:PIECE + EDGE, :])
+def flipped_columns(x):
+    rev = reversal(256)
+    n = x.shape[1] // 256
+    parts = [jnp.concatenate(split3(x[:, 256 * q:256 * q + 256]), axis=0) for q in range(n)]
+    rows, found = x.shape[0], [dot(part, rev) for part in reversed(parts)]
+    return jnp.concatenate([f[:rows] + f[rows:2 * rows] + f[2 * rows:] for f in found], axis=1)
+
+
+def weight_kernel(mask, p1, p3, partner, beside, trace, weight, border, lenses, smat, full, edges):
+    w, s, y, z, x, core, sign, pair = place_of()
+    rows, row = slice(2 * MROWS, 2 * MROWS + 32), slice(MROWS + GROUP, 2 * MROWS)
+    inner, outer = jnp.where(z == 0, y == 2, y == 1), jnp.where(z == 0, y == 0, y == 3)
+    crossing = [jnp.where(outer, 0.0, jnp.where(inner, partner[r, :], beside[r, :])) for r in (rows, row)]
+    own_rows = slice(PIECE, PIECE + 32), slice(PIECE + 32, PIECE + EDGE)
+    above = [jnp.where(z == 0, c, p1[r, :]) for c, r in zip(crossing, own_rows)]
+    below = [jnp.where(z == 3, c, p3[r, :]) for c, r in zip(crossing, own_rows)]
     lenses[0:8, :] = trace[...]
-    lenses[8:9, :] = above[64:65]
-    lenses[9:10, :] = below[64:65]
+    lenses[8:9, :] = above[1][0:1]
+    lenses[9:10, :] = below[1][0:1]
     lenses[10:16, :] = jnp.zeros((6, 128), F32)
-    u = focal_row(s, (UROWS, FHALF))
     v = iota((UROWS, FHALF), 1)
-    down, across = (2 * u + 1 - NF).astype(F32) * 0.5, (2 * v + 1 - NF).astype(F32) * 0.5
+    down, across = odd(focal_row(s, (UROWS, FHALF)), NF) * 0.5, odd(v, NF) * 0.5
     fade = 1.0 - jnp.exp((down * down + across * across) * (-1.0 / 1024.0))
-    rev = reversal(256)
     for q in range(8):
         for a in range(8):
             full[q, pl.ds(a, 8, stride=8), :] = mask[8 * a:8 * a + 8, 128 * q:128 * q + 128]
-        full[q, pl.ds(FROWS, 8, stride=2), :] = above[8 * q:8 * q + 8]
-        full[q, pl.ds(FROWS + 1, 8, stride=2), :] = below[8 * q:8 * q + 8]
-    t = jnp.concatenate([full[q] for q in range(4)], axis=1) * fade
-    weight[:, :FHALF] = t * t * 2.0**-24
-    for q in range(2):
-        flipped = sum(dot(part, rev) for part in split3(jnp.concatenate([full[6 - 2 * q], full[7 - 2 * q]], axis=1)))
-        t = flipped * fade[:, 256 * q:256 * (q + 1)]
-        weight[:, FHALF + 256 * q:FHALF + 256 * (q + 1)] = t * t * 2.0**-24
+    for q in range(4):
+        edges[q, pl.ds(0, 8, stride=2), :] = above[0][8 * q:8 * q + 8]
+        edges[q, pl.ds(1, 8, stride=2), :] = below[0][8 * q:8 * q + 8]
+    half = jnp.concatenate([edges[q] for q in range(4)], axis=1)
+    half = jnp.where(core == 0, half, flipped_columns(half))
+    t = half * fade[FROWS:]
+    border[...] = t * t * 2.0**-24
+    left, right = (jnp.concatenate([full[4 * k + q] for q in range(4)], axis=1) for k in range(2))
+    for k, part in enumerate((left, flipped_columns(right))):
+        t = part * fade[:FROWS]
+        weight[:, FHALF * k:FHALF * (k + 1)] = t * t * 2.0**-24
     row, lane = iota((FHALF, 256), 0), iota((FHALF, 256), 1)
     column = 2 * ((lane >> 5) & 3) + jnp.where(lane < 128, core, 1 - core)
     lens = jnp.where((lane & 31) < 18, 16 * column - 1 + (lane & 31), -1)
@@ -264,9 +276,17 @@
     smat[FHALF:NF, :] = (lens == NL - 1 - (row >> 3)).astype(BF16)
 
 
-def group_kernel(ref, utab, spot, *refs, p, flipped):
+def group_kernel(ref, utab, spot, *refs, p, flipped, waves=range(4)):
     before = refs[0] if flipped or p else None
     outs, (whi, wlo) = refs[before is not None:-2], refs[-2:]
+    if len(waves) == 4:
+        outs = [outs[0].at[m] for m in range(4)]
+    else:
+        *rest, out = outs
+        outs = {m: out.at[2 * UROWS * (m & 1):2 * UROWS * ((m & 1) + 1), :] for m in waves}
+        if 2 in waves:
+            for k in range(2):
+                out[4 * UROWS + 16 * k:4 * UROWS + 16 * k + 16, :] = rest[0][:, 256 * k:256 * k + 256]
     w, s, y, z, x, core, sign, pair = place_of()
     g = pair if p == 0 else 1 - pair
     turned = -1.0 if flipped else 1.0
@@ -281,7 +301,7 @@
         tilt = (sign * turned) * tilt
         paths.append(piston + (across if side == 0 else -across) * tip + tilt * down)
         steps.append(tilt * (1.0 / 512.0))
-    for m in range(4):
+    for m in waves:
         inverse = 1.0 / wavelength(2 * (w if m < 2 else w ^ 1) + (m & 1))
         im, re = zip(*(sincos(path * (turned * inverse)) for path in paths))
         step_im, step_re = zip(*(sincos(step * (turned * inverse)) for step in steps))
@@ -302,11 +322,11 @@
                 r0, c0 = GROUP * (k >> 1) + 16 * r2, 128 * (k & 1)
                 whi[m, r0:r0 + 16, c0:c0 + 128] = high
                 wlo[m, r0:r0 + 16, c0:c0 + 128] = low
-    for m in range(4):
+    for m in waves:
         table = utab[p, m]
         both = dot(table, whi[m])
         field = both[:2 * UROWS] + both[2 * UROWS:] + dot(table[:2 * UROWS], wlo[m])
-        out = outs[0].at[m] if len(outs) == 1 else outs[m >> 1].at[m & 1]
+        out = outs[m]
         if before is None:
             out[...] = field
         elif flipped:
@@ -316,11 +336,16 @@
             out[...] = before[m] + field
 
 
-def lens_kernel(keep, got, vtab, weight, smat, lenses, mine, other):
+def lens_kernel(keep, got, vtab, weight, border, smat, lenses, mine, other):
     parts = []
+    w, s, y, z, x, core, sign, pair = place_of()
+    theirs = jnp.concatenate([got[4 * UROWS + 16 * k:4 * UROWS + 16 * k + 16, :] for k in range(2)], axis=1)
+    first = core == 0
+    borders = jnp.where(first, border[...], theirs), jnp.where(first, theirs, border[...])
     for m in range(2):
+        rows = slice(2 * UROWS * m, 2 * UROWS * (m + 1))
         left, right = (
-            jnp.concatenate([ref[m, :, 128 * q:128 * q + 128] for ref in (keep, got)], axis=1) for q in range(2)
+            jnp.concatenate([ref[rows, 128 * q:128 * q + 128] for ref in (keep, got)], axis=1) for q in range(2)
         )
         odd_part = left - right
         sides = left + right, jnp.concatenate([odd_part[UROWS:], -odd_part[:UROWS]], axis=0)
@@ -332,8 +357,10 @@
         summed = []
         for q, value in enumerate((terms[0] + terms[1], terms[0] - terms[1])):
             re, im = value[:UROWS], value[UROWS:]
-            power = (re * re + im * im) * weight[:, FHALF * q:FHALF * (q + 1)]
-            edges = power[FROWS:FROWS + 8] + power[FROWS + 8:]
+            power = re * re + im * im
+            edges = power[FROWS:] * borders[q]
+            power = power[:FROWS] * weight[:, FHALF * q:FHALF * (q + 1)]
+            edges = edges[:8] + edges[8:]
             edges = edges + pltpu.roll(edges, 4, 0)
             edges = edges + pltpu.roll(edges, 2, 0)
             summed.append(jnp.concatenate([sum(power[8 * r:8 * r + 8] for r in range(8)), edges], axis=0))
@@ -493,12 +520,11 @@
             pltpu.VMEM((16, NP), I32),
             pltpu.VMEM((3, SEGMENTS), I32),
             pltpu.VMEM((3, 8, 16), I32),
-            pltpu.VMEM((2, 8, NF), F32),
+            pltpu.VMEM((2, 8, FHALF), F32),
             pltpu.SemaphoreType.DMA((9,)),
         ],
-        tail=anywhere * 7,
-        limit=54,
-    )(amplitude, seg_map, seg_table.T, focal_mask, trace_row, trace_col, block_count)
+        tail=[pl.BlockSpec(memory_space=pltpu.HBM)] * 7,
+    )(*(pltpu.with_memory_space_constraint(v, pltpu.HBM) for v in (amplitude, seg_map, seg_table.T, focal_mask, trace_row, trace_col, block_count)))
     utab, vtab, spot = call(
         table_kernel,
         [shape(2, 4, 4 * UROWS, 256, dtype=BF16), shape(2, 2, 2, HALF, FHALF, dtype=BF16), shape(128, 768, dtype=BF16)],
@@ -511,33 +537,33 @@
     p2 = lax.ppermute(piece, "slab", along_z(2))
     begun = call(opposite_kernel, shape(2 * MROWS, 128), 0, 3, tail=anywhere)(piece, p2, utab)
     own, more = call(
-        merge_kernel, [shape(2 * MROWS, 128), shape(2 * MROWS + EDGE, 128)], 0, 3, aliases={0: 0}
+        merge_kernel, [shape(2 * MROWS, 128), shape(2 * MROWS + 32, 128)], 0, 3, aliases={0: 0}
     )(begun, p1, p3)
     partner = lax.ppermute(more, "slab", along_y((3, 2, 1, 0)))
     beside = lax.ppermute(more, "slab", along_y((1, 0, 3, 2)))
     last = lax.ppermute(own, "slab", along_y((2, 3, 0, 1)))
     scratch = [pltpu.VMEM((4, 256, 256), BF16)] * 2
 
-    def add(group, p, flipped, *before, outs=shape(4, 2 * UROWS, 256), **options):
-        kernel = functools.partial(group_kernel, p=p, flipped=flipped)
-        return call(kernel, outs, 0, 3 + len(before), scratch, **options)(group, utab, spot, *before)
+    def add(group, p, flipped, *before, outs=shape(4, 2 * UROWS, 256), tail=(), **options):
+        kernel = functools.partial(group_kernel, p=p, flipped=flipped, **options)
+        return call(kernel, outs, 0, 3 + len(before), scratch, tail=tail)(group, utab, spot, *before)
 
     field = add(own, 0, False)
     field = add(partner, 0, True, field)
     field = add(beside, 1, False, field)
-    keep, give = add(last, 1, True, field, outs=[shape(2, 2 * UROWS, 256)] * 2)
-    weight, lenses, smat = call(
+    weight, border, lenses, smat = call(
         weight_kernel,
-        [shape(UROWS, NF), shape(16, 128), shape(NF, 256, dtype=BF16)],
+        [shape(FROWS, NF), shape(16, FHALF), shape(16, 128), shape(NF, 256, dtype=BF16)],
         0,
-        7,
-        [pltpu.VMEM((8, UROWS, 128), F32)],
-        tail=anywhere,
-    )(focal_mask, p1, p3, partner, beside, trace, give)
+        6,
+        [pltpu.VMEM((8, FROWS, 128), F32), pltpu.VMEM((4, 16, 128), F32)],
+    )(focal_mask, p1, p3, partner, beside, trace)
+    give = add(last, 1, True, field, border, outs=shape(4 * UROWS + 32, 256), waves=(2, 3))
+    keep = add(last, 1, True, field, give, outs=shape(4 * UROWS, 256), waves=(0, 1), tail=anywhere)
     sibling = [(i, i ^ 1) for i in range(NWAV)]
     crossed = lax.ppermute(give, "wav", sibling)
-    mine, other = call(lens_kernel, [shape(32, 128)] * 2, 0, 6)(
-        keep, crossed, vtab, weight, smat, lenses
+    mine, other = call(lens_kernel, [shape(32, 128)] * 2, 0, 7)(
+        keep, crossed, vtab, weight, border, smat, lenses
     )
     got = lax.ppermute(other, "wav", sibling)
     def along_x(sent, k):

time: 38.2 us -> 36.9 us (0.966)
  local copies, waits for them, and re-layouts: 0.83 us -> 0.07 us
    unnamed x8 -> x4, local copies, waits for them, and re-layouts: 0.83 us -> 0.07 us
    pallas_call x1, Pallas kernels: 2.1 us -> 1.42 us  [body(): call(prepare_kernel, [shape(PIECE, 128), shape(PIECE + EDGE, 128), shape(...]
    ppermute x1, waiting for transfers between devices: 0.87 us -> 1.48 us  [body(): p2 = lax.ppermute(piece, 'slab', along_z(2))]
    ppermute x1, waiting for transfers between devices: 0.43 us -> 0.01 us  [body(): last = lax.ppermute(own, 'slab', along_y((2, 3, 0, 1)))]
    pallas_call x7 -> x8, Pallas kernels: 4.81 us -> 5.11 us  [the longest x5 3.79 us: add(): call(kernel, outs, 0, 3 + len(before), scratch, tail=tail)]
  transfers between devices with their start and end apart: 11 -> 11, of which waited for: 7 -> 5; matrix products, arithmetic and copies ran while one was open for 0% -> 0% of each run, Pallas kernels for 14% -> 17%
where the time goes in v4:
time: 36.9 us; the launch traced here: 36.2 us
  starting transfers between devices  17.5 us (47%)
  Pallas kernels  11.1 us (30%)
  waiting for transfers between devices  7.49 us (20%)
    ppermute x3, starting transfers between devices, along_x(): lax.ppermute(sent, 'wav', [(i, (i + 2 * k) % NWAV) for i in range(NWAV)])  6.36 us
    pallas_call x5, Pallas kernels, add(): call(kernel, outs, 0, 3 + len(before), scratch, tail=tail)  3.79 us
    ppermute x1, starting transfers between devices, body(): partner = lax.ppermute(more, 'slab', along_y((3, 2, 1, 0)))  3.1 us
    ppermute x1, waiting for transfers between devices, body(): partner = lax.ppermute(more, 'slab', along_y((3, 2, 1, 0)))  2.37 us
    pallas_call x1, Pallas kernels, body(): call(table_kernel, [shape(2, 4, 4 * UROWS, 256, dtype=BF16), shape(2, 2,...  2.24 us
    ppermute x1, starting transfers between devices, body(): p3 = lax.ppermute(down, 'slab', along_z(3))  2.2 us
    ppermute x1, starting transfers between devices, body(): p1 = lax.ppermute(up, 'slab', along_z(1))  2.07 us
    pallas_call x1, Pallas kernels, body(): call(detector_kernel, shape(256, 512), 0, 5, [pltpu.VMEM((WAVES, 16, 128)...  2.03 us
  transfers between devices with their start and end apart: 11, of which 5 were waited for; matrix products, arithmetic and copies ran while one was open for 0% of the time, Pallas kernels for 17%

profile of v4, /device:TPU:0, one launch (start us, length us, event | category | flops | bytes accessed | tf_op | source)
XLA Modules:
  0.0 36.2 jit_solution(5005970541890336294)
XLA Ops:
  0.0 1.4 %prepare_kernel.1 = (f32[80,128]{1,0:T(8,128)S(1)}, f32[120,128]{1,0:T(8,128)S(1)}, f32[120,128]{1,0:T(8,128)S(1)}, f32[8,128]{1,0:T(8,128)S(1)}) custom-call(f32[32,512]{1,0:T(8,128)} %amp_in.1, s32[32,512]{1,0:T(8,128)} %seg_in.1, s32[3,798]{1,0:T(4,128)} %bitcast.1, f32[64,1024]{1,0:T(8,128)} %mask.3, s32[8,16]{1,0:T(8,128)} %trow.1, s32[8,16]{1,0:T(8,128)} %tcol.1, ...), custom_call_target="tpu_custom_call" | custom-call | tf_op jit(solution)/shard_map/prepare_kernel/pallas_call | solution.py:513
  1.4 2.1 %collective-permute-start.1 = (f32[120,128]{1,0:T(8,128)S(1)}, f32[120,128]{1,0:T(8,128)S(1)}, u32[]{:S(2)}, u32[]{:S(2)}) collective-permute-start(f32[120,128]{1,0:T(8,128)S(1)} %get-tuple-element.25), channel_id=1, source_target_pairs={{0,1},{1,2},{2,3},{3,0},{4,5},{5,6},{6,7},{7,4},{8,9},{9,10},{10,1... | collective-permute-start | bytes 184328 | tf_op jit(solution)/shard_map/ppermute | solution.py:535
  3.5 2.2 %collective-permute-start.2 = (f32[120,128]{1,0:T(8,128)S(1)}, f32[120,128]{1,0:T(8,128)S(1)}, u32[]{:S(2)}, u32[]{:S(2)}) collective-permute-start(f32[120,128]{1,0:T(8,128)S(1)} %get-tuple-element.26), channel_id=1, source_target_pairs={{0,3},{1,0},{2,1},{3,2},{4,7},{5,4},{6,5},{7,6},{8,11},{9,8},{10,9... | collective-permute-start | bytes 184328 | tf_op jit(solution)/shard_map/ppermute | solution.py:536
  5.7 1.8 %collective-permute-start = (f32[80,128]{1,0:T(8,128)S(1)}, f32[80,128]{1,0:T(8,128)S(1)}, u32[]{:S(2)}, u32[]{:S(2)}) collective-permute-start(f32[80,128]{1,0:T(8,128)S(1)} %get-tuple-element.23.after.p0), channel_id=1, source_target_pairs={{0,2},{1,3},{2,0},{3,1},{4,6},{5,7},{6,4},{7,5},{8,10},{9,11},{10,... | collective-permute-start | bytes 122888 | tf_op jit(solution)/shard_map/ppermute | solution.py:537
  7.5 2.2 %table_kernel.1 = (bf16[2,4,320,256]{3,2,1,0:T(8,128)(2,1)S(1)}, bf16[2,2,2,256,512]{4,3,2,1,0:T(8,128)(2,1)S(1)}, bf16[128,768]{1,0:T(8,128)(2,1)S(1)}) custom-call(f32[80,128]{1,0:T(8,128)S(1)} %get-tuple-element.23.after.p0), custom_call_target="tpu_custom_call" | custom-call | tf_op jit(solution)/shard_map/table_kernel/pallas_call | solution.py:528
  9.7 1.5 %collective-permute-done.p2 = f32[80,128]{1,0:T(8,128)S(1)} collective-permute-done((f32[80,128]{1,0:T(8,128)S(1)}, f32[80,128]{1,0:T(8,128)S(1)}, u32[]{:S(2)}, u32[]{:S(2)}) %collective-permute-start) | collective-permute-done | bytes 40992 | tf_op jit(solution)/shard_map/ppermute | solution.py:537
  11.2 0.0 collective-permute-done.1.p1
  11.2 0.0 collective-permute-done.2.p3
  11.3 0.1 merge_kernel.1
  11.3 3.1 %collective-permute-start.5 = (f32[304,128]{1,0:T(8,128)S(1)}, f32[304,128]{1,0:T(8,128)S(1)}, u32[]{:S(2)}, u32[]{:S(2)}) collective-permute-start(f32[304,128]{1,0:T(8,128)S(1)} %get-tuple-element.29), channel_id=1, source_target_pairs={{0,12},{1,13},{2,14},{3,15},{4,8},{5,9},{6,10},{7,11},{8,4},{9,5},... | collective-permute-start | bytes 466952 | tf_op jit(solution)/shard_map/ppermute | solution.py:542
  14.4 0.1 collective-permute-start.4
  14.6 1.5 %collective-permute-start.3 = (f32[272,128]{1,0:T(8,128)S(1)}, f32[272,128]{1,0:T(8,128)S(1)}, u32[]{:S(2)}, u32[]{:S(2)}) collective-permute-start(f32[272,128]{1,0:T(8,128)S(1)} %get-tuple-element.27.ref), channel_id=1, source_target_pairs={{0,8},{1,9},{2,10},{3,11},{4,12},{5,13},{6,14},{7,15},{8,0},{9,1},... | collective-permute-start | bytes 417800 | tf_op jit(solution)/shard_map/ppermute | solution.py:544
  16.1 0.9 %group_kernel.5.refs_0_ = f32[4,160,256]{2,1,0:T(8,128)S(1)} custom-call(f32[272,128]{1,0:T(8,128)S(1)} %get-tuple-element.27.ref, bf16[2,4,320,256]{3,2,1,0:T(8,128)(2,1)S(1)} %get-tuple-element.24.after.utab, bf16[128,768]{1,0:T(8,128)(2,1)S(1)} %get-tuple-element.28.spot), custom_call_target="tpu_custom_call" | custom-call | tf_op jit(solution)/shard_map/group_kernel/pallas_call | solution.py:549
  17.0 2.4 %collective-permute-done.5.ref.partner = f32[304,128]{1,0:T(8,128)S(1)} collective-permute-done((f32[304,128]{1,0:T(8,128)S(1)}, f32[304,128]{1,0:T(8,128)S(1)}, u32[]{:S(2)}, u32[]{:S(2)}) %collective-permute-start.5) | collective-permute-done | bytes 155680 | tf_op jit(solution)/shard_map/ppermute | solution.py:542
  19.3 0.9 %group_kernel.6.refs_0_ = f32[4,160,256]{2,1,0:T(8,128)S(1)} custom-call(f32[304,128]{1,0:T(8,128)S(1)} %collective-permute-done.5.ref.partner, bf16[2,4,320,256]{3,2,1,0:T(8,128)(2,1)S(1)} %get-tuple-element.24.after.utab, bf16[128,768]{1,0:T(8,128)(2,1)S(1)} %get-tuple-element.28.spot, f32[4,160,256]{2,1,0:T(8,128)S(1)} %group_kernel.5.refs_0_), custom_call_target="tpu_custom_call" | custom-call | tf_op jit(solution)/shard_map/group_kernel/pallas_call | solution.py:549
  20.2 0.0 copy-start
  20.2 0.0 collective-permute-done.4.ref.beside
  20.2 0.9 %group_kernel.7.refs_0_ = f32[4,160,256]{2,1,0:T(8,128)S(1)} custom-call(f32[304,128]{1,0:T(8,128)S(1)} %collective-permute-done.4.ref.beside, bf16[2,4,320,256]{3,2,1,0:T(8,128)(2,1)S(1)} %get-tuple-element.24.after.utab, bf16[128,768]{1,0:T(8,128)(2,1)S(1)} %get-tuple-element.28.spot, f32[4,160,256]{2,1,0:T(8,128)S(1)} %group_kernel.6.refs_0_), custom_call_target="tpu_custom_call" | custom-call | tf_op jit(solution)/shard_map/group_kernel/pallas_call | solution.py:549
  21.1 0.1 copy-done
  21.2 0.4 %weight_kernel.1 = (f32[64,1024]{1,0:T(8,128)S(1)}, f32[16,512]{1,0:T(8,128)S(1)}, f32[16,128]{1,0:T(8,128)S(1)}, bf16[1024,256]{1,0:T(8,128)(2,1)S(1)}) custom-call(f32[64,1024]{1,0:T(8,128)S(1)} %copy-done, f32[120,128]{1,0:T(8,128)S(1)} %collective-permute-done.1.p1, f32[120,128]{1,0:T(8,128)S(1)} %collective-permute-done.2.p3, ...), custom_call_target="tpu_custom_call" | custom-call | tf_op jit(solution)/shard_map/weight_kernel/pallas_call | solution.py:554
  21.5 0.0 collective-permute-done.3.ref
  21.6 0.6 %group_kernel.8.refs_1_ = f32[352,256]{1,0:T(8,128)S(1)} custom-call(f32[272,128]{1,0:T(8,128)S(1)} %collective-permute-done.3.ref, bf16[2,4,320,256]{3,2,1,0:T(8,128)(2,1)S(1)} %get-tuple-element.24.after.utab, bf16[128,768]{1,0:T(8,128)(2,1)S(1)} %get-tuple-element.28.spot, f32[4,160,256]{2,1,0:T(8,128)S(1)} %group_kernel.7.refs_0_, ...), custom_call_target="tpu_custom_call" | custom-call | tf_op jit(solution)/shard_map/group_kernel/pallas_call | solution.py:549
  22.2 0.1 collective-permute-start.6
  22.3 0.6 %group_kernel.9.keep = f32[320,256]{1,0:T(8,128)S(1)} custom-call(f32[272,128]{1,0:T(8,128)S(1)} %collective-permute-done.3.ref, bf16[2,4,320,256]{3,2,1,0:T(8,128)(2,1)S(1)} %get-tuple-element.24.after.utab, bf16[128,768]{1,0:T(8,128)(2,1)S(1)} %get-tuple-element.28.spot, f32[4,160,256]{2,1,0:T(8,128)S(1)} %group_kernel.7.refs_0_, ...), custom_call_target="tpu_custom_call" | custom-call | tf_op jit(solution)/shard_map/group_kernel/pallas_call | solution.py:549
  22.9 0.0 copy-start.1
  22.9 1.0 %collective-permute-done.6.got = f32[352,256]{1,0:T(8,128)S(1)} collective-permute-done((f32[352,256]{1,0:T(8,128)S(1)}, f32[352,256]{1,0:T(8,128)S(1)}, u32[]{:S(2)}, u32[]{:S(2)}) %collective-permute-start.6) | collective-permute-done | bytes 360480 | tf_op jit(solution)/shard_map/ppermute | solution.py:564
  23.9 0.9 %lens_kernel.1 = (f32[32,128]{1,0:T(8,128)S(1)}, f32[32,128]{1,0:T(8,128)S(1)}) custom-call(f32[320,256]{1,0:T(8,128)S(1)} %group_kernel.9.keep, f32[352,256]{1,0:T(8,128)S(1)} %collective-permute-done.6.got, bf16[2,2,2,256,512]{4,3,2,1,0:T(8,128)(2,1)S(1)} %get-tuple-element.32.vtab, f32[64,1024]{1,0:T(8,128)S(1)} %get-tuple-element.33.weight, ...), custom_call_target="tpu_custom_call" | custom-call | tf_op jit(solution)/shard_map/lens_kernel/pallas_call | solution.py:565
  24.8 0.2 collective-permute-start.7
  25.0 1.0 %collective-permute-done.7.got = f32[32,128]{1,0:T(8,128)S(1)} collective-permute-done((f32[32,128]{1,0:T(8,128)S(1)}, f32[32,128]{1,0:T(8,128)S(1)}, u32[]{:S(2)}, u32[]{:S(2)}) %collective-permute-start.7) | collective-permute-done | bytes 16416 | tf_op jit(solution)/shard_map/ppermute | solution.py:568
  26.1 0.1 pack_kernel.2.after
  26.1 3.1 %collective-permute-start.8 = (f32[16,128]{1,0:T(8,128)S(1)}, f32[16,128]{1,0:T(8,128)S(1)}, u32[]{:S(2)}, u32[]{:S(2)}) collective-permute-start(f32[16,128]{1,0:T(8,128)S(1)} %pack_kernel.2.after), channel_id=1, source_target_pairs={{0,64},{16,80},{32,96},{48,112},{64,0},{80,16},{96,32},{112,48},{1... | collective-permute-start | bytes 24584 | tf_op jit(solution)/shard_map/ppermute | solution.py:570
  29.2 0.1 pack_kernel.3
  29.3 0.7 %collective-permute-start.9 = (f32[16,128]{1,0:T(8,128)S(1)}, f32[16,128]{1,0:T(8,128)S(1)}, u32[]{:S(2)}, u32[]{:S(2)}) collective-permute-start(f32[16,128]{1,0:T(8,128)S(1)} %get-tuple-element.39), channel_id=1, source_target_pairs={{0,32},{16,48},{32,64},{48,80},{64,96},{80,112},{96,0},{112,16},{1... | collective-permute-start | bytes 24584 | tf_op jit(solution)/shard_map/ppermute | solution.py:570
  29.9 2.6 %collective-permute-start.10 = (f32[16,128]{1,0:T(8,128)S(1)}, f32[16,128]{1,0:T(8,128)S(1)}, u32[]{:S(2)}, u32[]{:S(2)}) collective-permute-start(f32[16,128]{1,0:T(8,128)S(1)} %get-tuple-element.40), channel_id=1, source_target_pairs={{0,96},{16,112},{32,0},{48,16},{64,32},{80,48},{96,64},{112,80},{1... | collective-permute-start | bytes 24584 | tf_op jit(solution)/shard_map/ppermute | solution.py:570
  32.6 0.0 collective-permute-done.8.a2
  32.6 0.1 unpack_kernel.1.begun
  32.7 1.5 %collective-permute-done.9.a1 = f32[16,128]{1,0:T(8,128)S(1)} collective-permute-done((f32[16,128]{1,0:T(8,128)S(1)}, f32[16,128]{1,0:T(8,128)S(1)}, u32[]{:S(2)}, u32[]{:S(2)}) %collective-permute-start.9) | collective-permute-done | bytes 8224 | tf_op jit(solution)/shard_map/ppermute | solution.py:570
  34.2 0.0 collective-permute-done.10.a3
  34.2 0.0 copy-done.1
  34.2 2.0 %detector_kernel.1 = f32[256,512]{1,0:T(8,128)} custom-call(f32[5,5]{1,0:T(8,128)S(1)} %copy-done.1, f32[8,16,128]{2,1,0:T(8,128)S(1)} %unpack_kernel.1.begun, f32[16,128]{1,0:T(8,128)S(1)} %collective-permute-done.9.a1, f32[16,128]{1,0:T(8,128)S(1)} %collective-permute-done.10.a3, f32[16,128]{1,0:T(8,128)S(1)} %get-tuple-element.35.lenses.after), custom_call_target="tpu_custom_call" | custom-call | tf_op jit(solution)/shard_map/detector_kernel/pallas_call | solution.py:579
  (1 shorter events, 0.0 us)
Async XLA Ops:
  1.4 9.8 %collective-permute-start.1 = (f32[120,128]{1,0:T(8,128)S(1)}, f32[120,128]{1,0:T(8,128)S(1)}, u32[]{:S(2)}, u32[]{:S(2)}) collective-permute-start(f32[120,128]{1,0:T(8,128)S(1)} %get-tuple-element.25), channel_id=1, source_target_pairs={{0,1},{1,2},{2,3},{3,0},{4,5},{5,6},{6,7},{7,4},{8,9},{9,10},{10,1... | collective-permute-start | bytes 184328 | tf_op jit(solution)/shard_map/ppermute | solution.py:535
  3.5 7.7 %collective-permute-start.2 = (f32[120,128]{1,0:T(8,128)S(1)}, f32[120,128]{1,0:T(8,128)S(1)}, u32[]{:S(2)}, u32[]{:S(2)}) collective-permute-start(f32[120,128]{1,0:T(8,128)S(1)} %get-tuple-element.26), channel_id=1, source_target_pairs={{0,3},{1,0},{2,1},{3,2},{4,7},{5,4},{6,5},{7,6},{8,11},{9,8},{10,9... | collective-permute-start | bytes 184328 | tf_op jit(solution)/shard_map/ppermute | solution.py:536
  5.7 5.5 %collective-permute-start = (f32[80,128]{1,0:T(8,128)S(1)}, f32[80,128]{1,0:T(8,128)S(1)}, u32[]{:S(2)}, u32[]{:S(2)}) collective-permute-start(f32[80,128]{1,0:T(8,128)S(1)} %get-tuple-element.23.after.p0), channel_id=1, source_target_pairs={{0,2},{1,3},{2,0},{3,1},{4,6},{5,7},{6,4},{7,5},{8,10},{9,11},{10,... | collective-permute-start | bytes 122888 | tf_op jit(solution)/shard_map/ppermute | solution.py:537
  11.3 8.0 %collective-permute-start.5 = (f32[304,128]{1,0:T(8,128)S(1)}, f32[304,128]{1,0:T(8,128)S(1)}, u32[]{:S(2)}, u32[]{:S(2)}) collective-permute-start(f32[304,128]{1,0:T(8,128)S(1)} %get-tuple-element.29), channel_id=1, source_target_pairs={{0,12},{1,13},{2,14},{3,15},{4,8},{5,9},{6,10},{7,11},{8,4},{9,5},... | collective-permute-start | bytes 466952 | tf_op jit(solution)/shard_map/ppermute | solution.py:542
  14.4 5.8 %collective-permute-start.4 = (f32[304,128]{1,0:T(8,128)S(1)}, f32[304,128]{1,0:T(8,128)S(1)}, u32[]{:S(2)}, u32[]{:S(2)}) collective-permute-start(f32[304,128]{1,0:T(8,128)S(1)} %get-tuple-element.29), channel_id=1, source_target_pairs={{0,4},{1,5},{2,6},{3,7},{4,0},{5,1},{6,2},{7,3},{8,12},{9,13},{10,... | collective-permute-start | bytes 466952 | tf_op jit(solution)/shard_map/ppermute | solution.py:543
  14.6 7.0 %collective-permute-start.3 = (f32[272,128]{1,0:T(8,128)S(1)}, f32[272,128]{1,0:T(8,128)S(1)}, u32[]{:S(2)}, u32[]{:S(2)}) collective-permute-start(f32[272,128]{1,0:T(8,128)S(1)} %get-tuple-element.27.ref), channel_id=1, source_target_pairs={{0,8},{1,9},{2,10},{3,11},{4,12},{5,13},{6,14},{7,15},{8,0},{9,1},... | collective-permute-start | bytes 417800 | tf_op jit(solution)/shard_map/ppermute | solution.py:544
  20.2 1.0 %copy-start = (f32[64,1024]{1,0:T(8,128)S(1)}, f32[64,1024]{1,0:T(8,128)}, u32[]{:S(2)}) copy-start(f32[64,1024]{1,0:T(8,128)} %mask.3) | copy-start | bytes 786436
  22.2 1.8 %collective-permute-start.6 = (f32[352,256]{1,0:T(8,128)S(1)}, f32[352,256]{1,0:T(8,128)S(1)}, u32[]{:S(2)}, u32[]{:S(2)}) collective-permute-start(f32[352,256]{1,0:T(8,128)S(1)} %group_kernel.8.refs_1_), channel_id=1, source_target_pairs={{0,16},{16,0},{32,48},{48,32},{64,80},{80,64},{96,112},{112,96},{1... | collective-permute-start | bytes 1081352 | tf_op jit(solution)/shard_map/ppermute | solution.py:564
  22.9 11.3 %copy-start.1 = (f32[5,5]{1,0:T(8,128)S(1)}, f32[5,5]{1,0:T(8,128)}, u32[]{:S(2)}) copy-start(f32[5,5]{1,0:T(8,128)} %kernel.1) | copy-start | bytes 304
  24.8 1.2 %collective-permute-start.7 = (f32[32,128]{1,0:T(8,128)S(1)}, f32[32,128]{1,0:T(8,128)S(1)}, u32[]{:S(2)}, u32[]{:S(2)}) collective-permute-start(f32[32,128]{1,0:T(8,128)S(1)} %get-tuple-element.37), channel_id=1, source_target_pairs={{0,16},{16,0},{32,48},{48,32},{64,80},{80,64},{96,112},{112,96},{1... | collective-permute-start | bytes 49160 | tf_op jit(solution)/shard_map/ppermute | solution.py:568
  26.1 6.5 %collective-permute-start.8 = (f32[16,128]{1,0:T(8,128)S(1)}, f32[16,128]{1,0:T(8,128)S(1)}, u32[]{:S(2)}, u32[]{:S(2)}) collective-permute-start(f32[16,128]{1,0:T(8,128)S(1)} %pack_kernel.2.after), channel_id=1, source_target_pairs={{0,64},{16,80},{32,96},{48,112},{64,0},{80,16},{96,32},{112,48},{1... | collective-permute-start | bytes 24584 | tf_op jit(solution)/shard_map/ppermute | solution.py:570
  29.3 4.9 %collective-permute-start.9 = (f32[16,128]{1,0:T(8,128)S(1)}, f32[16,128]{1,0:T(8,128)S(1)}, u32[]{:S(2)}, u32[]{:S(2)}) collective-permute-start(f32[16,128]{1,0:T(8,128)S(1)} %get-tuple-element.39), channel_id=1, source_target_pairs={{0,32},{16,48},{32,64},{48,80},{64,96},{80,112},{96,0},{112,16},{1... | collective-permute-start | bytes 24584 | tf_op jit(solution)/shard_map/ppermute | solution.py:570
  29.9 4.3 %collective-permute-start.10 = (f32[16,128]{1,0:T(8,128)S(1)}, f32[16,128]{1,0:T(8,128)S(1)}, u32[]{:S(2)}, u32[]{:S(2)}) collective-permute-start(f32[16,128]{1,0:T(8,128)S(1)} %get-tuple-element.40), channel_id=1, source_target_pairs={{0,96},{16,112},{32,0},{48,16},{64,32},{80,48},{96,64},{112,80},{1... | collective-permute-start | bytes 24584 | tf_op jit(solution)/shard_map/ppermute | solution.py:570

commit v5 on v4

--- a/solution.py
+++ b/solution.py
@@ -261,11 +261,11 @@
     for q in range(4):
         edges[q, pl.ds(0, 8, stride=2), :] = above[0][8 * q:8 * q + 8]
         edges[q, pl.ds(1, 8, stride=2), :] = below[0][8 * q:8 * q + 8]
-    half = jnp.concatenate([edges[q] for q in range(4)], axis=1)
+    half = jnp.concatenate([edges[q, 0:16, :] for q in range(4)], axis=1)
     half = jnp.where(core == 0, half, flipped_columns(half))
     t = half * fade[FROWS:]
     border[...] = t * t * 2.0**-24
-    left, right = (jnp.concatenate([full[4 * k + q] for q in range(4)], axis=1) for k in range(2))
+    left, right = (jnp.concatenate([full[4 * k + q, 0:FROWS, :] for q in range(4)], axis=1) for k in range(2))
     for k, part in enumerate((left, flipped_columns(right))):
         t = part * fade[:FROWS]
         weight[:, FHALF * k:FHALF * (k + 1)] = t * t * 2.0**-24
@@ -377,10 +377,10 @@
         out[0:16, :] += sides
 
 
-def pack_kernel(mine, got, after, *outs, shifts):
+def pack_kernel(mine, got, *outs):
     w, s, y, z, x, core, sign, pair = place_of()
     lane = iota((16, 128), 1) >> 5
-    for out, k in zip(outs, shifts):
+    for k, out in enumerate(outs):
         at = (x + k) & 3
         packed = 0.0
         for c in range(2):
@@ -391,24 +391,15 @@
         out[...] = packed
 
 
-def unpack_kernel(a0, a2, out):
-    for k, ref in enumerate((a0, a2)):
-        for c in range(4):
-            out[4 * k + c] = ref[...] if c == 0 else pltpu.roll(ref[...], 128 - 32 * c, 1)
-
-
 def order(a):
     return a - 1 if 0 < a < 9 else 8 + a // 9
 
 
-def detector_kernel(kernel, begun, a1, a3, lenses, out, arrived, base, across, image, sems):
-    w, s, y, z, x, core, sign, pair = place_of()
-    for k, ref in ((1, a1), (3, a3)):
+def detector_kernel(kernel, a0, a1, a2, a3, lenses, out, arrived, base, across, image, sems):
+    w, s, y, z, x, core, sign, pair = place_of()
+    for k, ref in enumerate((a0, a1, a2, a3)):
         for c in range(4):
             arrived[4 * ((x - k + 4) & 3) + c] = ref[...] if c == 0 else pltpu.roll(ref[...], 128 - 32 * c, 1)
-    for k in (0, 2):
-        for c in range(4):
-            arrived[4 * ((x - k + 4) & 3) + c] = begun[2 * k + c]
     spot = (iota((128, 640), 0) == (iota((128, 640), 1) >> 5)) & (iota((128, 640), 1) < 18 * DPIX)
     spot = spot.astype(BF16)
     left, own, right = arrived[jnp.maximum(2 * w - 2, 0)], lenses[...], arrived[jnp.minimum(2 * w + 2, WAVES - 1)]
@@ -556,7 +547,7 @@
         [shape(FROWS, NF), shape(16, FHALF), shape(16, 128), shape(NF, 256, dtype=BF16)],
         0,
         6,
-        [pltpu.VMEM((8, FROWS, 128), F32), pltpu.VMEM((4, 16, 128), F32)],
+        [pltpu.VMEM((8, FROWS + 8, 128), F32), pltpu.VMEM((4, 24, 128), F32)],
     )(focal_mask, p1, p3, partner, beside, trace)
     give = add(last, 1, True, field, border, outs=shape(4 * UROWS + 32, 256), waves=(2, 3))
     keep = add(last, 1, True, field, give, outs=shape(4 * UROWS, 256), waves=(0, 1), tail=anywhere)
@@ -569,18 +560,13 @@
     def along_x(sent, k):
         return lax.ppermute(sent, "wav", [(i, (i + 2 * k) % NWAV) for i in range(NWAV)])
 
-    (opposite,) = call(functools.partial(pack_kernel, shifts=(2,)), [shape(16, 128)], 0, 3, tail=anywhere)(mine, got, lenses)
-    a2 = along_x(opposite, 2)
-    kept, forth, back = call(functools.partial(pack_kernel, shifts=(0, 1, 3)), [shape(16, 128)] * 3, 0, 3, tail=anywhere)(
-        mine, got, opposite
-    )
-    a1, a3 = along_x(forth, 1), along_x(back, 3)
-    begun = call(unpack_kernel, shape(8, 16, 128), 0, 2)(kept, a2)
+    kept, *sent = call(pack_kernel, [shape(16, 128)] * 4, 0, 2)(mine, got)
+    arrived = [along_x(sent[k - 1], k) for k in (1, 2, 3)]
     return call(
         detector_kernel,
         shape(256, 512),
         0,
-        5,
+        6,
         [
             pltpu.VMEM((WAVES, 16, 128), F32),
             pltpu.VMEM((10, 16, 512), F32),
@@ -589,7 +575,7 @@
             pltpu.SemaphoreType.DMA((4,)),
         ],
         outside=True,
-    )(crosstalk, begun, a1, a3, lenses)
+    )(crosstalk, kept, *arrived, lenses)
 
 
 def solution(mesh):

time: 36.9 us -> 36.4 us (0.986); the launches traced: 36.2 us -> 36.1 us
  starting transfers between devices: 17.5 us -> 16.8 us
  waiting for transfers between devices: 7.49 us -> 8.15 us
    ppermute x3, waiting for transfers between devices: 1.55 us -> 2.21 us  [along_x(): lax.ppermute(sent, 'wav', [(i, (i + 2 * k) % NWAV) for i in range(NWAV)])]
    ppermute x3, starting transfers between devices: 6.36 us -> 5.73 us  [along_x(): lax.ppermute(sent, 'wav', [(i, (i + 2 * k) % NWAV) for i in range(NWAV)])]
    pallas_call x4 -> x2, Pallas kernels: 2.27 us -> 2.13 us  [the longest x1 2.03 us: body(): call(detector_kernel, shape(256, 512), 0, 6, [pltpu.VMEM((WAVES, 16, 128)...]
  transfers between devices with their start and end apart: 11 -> 11, of which waited for: 5 -> 6; matrix products, arithmetic and copies ran while one was open for 0% -> 0% of each run, Pallas kernels for 17% -> 16%
where the time goes in v5:
time: 36.4 us; the launch traced here: 36.1 us
  starting transfers between devices  16.8 us (46%)
  Pallas kernels  10.9 us (30%)
  waiting for transfers between devices  8.15 us (22%)
    ppermute x3, starting transfers between devices, along_x(): lax.ppermute(sent, 'wav', [(i, (i + 2 * k) % NWAV) for i in range(NWAV)])  5.73 us
    pallas_call x5, Pallas kernels, add(): call(kernel, outs, 0, 3 + len(before), scratch, tail=tail)  3.79 us
    ppermute x1, starting transfers between devices, body(): partner = lax.ppermute(more, 'slab', along_y((3, 2, 1, 0)))  3.1 us
    ppermute x1, waiting for transfers between devices, body(): partner = lax.ppermute(more, 'slab', along_y((3, 2, 1, 0)))  2.37 us
    pallas_call x1, Pallas kernels, body(): call(table_kernel, [shape(2, 4, 4 * UROWS, 256, dtype=BF16), shape(2, 2,...  2.24 us
    ppermute x3, waiting for transfers between devices, along_x(): lax.ppermute(sent, 'wav', [(i, (i + 2 * k) % NWAV) for i in range(NWAV)])  2.21 us
    ppermute x1, starting transfers between devices, body(): p3 = lax.ppermute(down, 'slab', along_z(3))  2.2 us
    ppermute x1, starting transfers between devices, body(): p1 = lax.ppermute(up, 'slab', along_z(1))  2.07 us
  transfers between devices with their start and end apart: 11, of which 6 were waited for; matrix products, arithmetic and copies ran while one was open for 0% of the time, Pallas kernels for 16%

profile of v5, /device:TPU:0, one launch (start us, length us, event | category | flops | bytes accessed | tf_op | source)
XLA Modules:
  0.0 36.1 jit_solution(2110573501244300278)
XLA Ops:
  0.0 1.4 %prepare_kernel.1 = (f32[80,128]{1,0:T(8,128)S(1)}, f32[120,128]{1,0:T(8,128)S(1)}, f32[120,128]{1,0:T(8,128)S(1)}, f32[8,128]{1,0:T(8,128)S(1)}) custom-call(f32[32,512]{1,0:T(8,128)} %amp_in.1, s32[32,512]{1,0:T(8,128)} %seg_in.1, s32[3,798]{1,0:T(4,128)} %bitcast.1, f32[64,1024]{1,0:T(8,128)} %mask.3, s32[8,16]{1,0:T(8,128)} %trow.1, s32[8,16]{1,0:T(8,128)} %tcol.1, ...), custom_call_target="tpu_custom_call" | custom-call | tf_op jit(solution)/shard_map/prepare_kernel/pallas_call | solution.py:504
  1.4 2.1 %collective-permute-start.1 = (f32[120,128]{1,0:T(8,128)S(1)}, f32[120,128]{1,0:T(8,128)S(1)}, u32[]{:S(2)}, u32[]{:S(2)}) collective-permute-start(f32[120,128]{1,0:T(8,128)S(1)} %get-tuple-element.26), channel_id=1, source_target_pairs={{0,1},{1,2},{2,3},{3,0},{4,5},{5,6},{6,7},{7,4},{8,9},{9,10},{10,1... | collective-permute-start | bytes 184328 | tf_op jit(solution)/shard_map/ppermute | solution.py:526
  3.5 2.2 %collective-permute-start.2 = (f32[120,128]{1,0:T(8,128)S(1)}, f32[120,128]{1,0:T(8,128)S(1)}, u32[]{:S(2)}, u32[]{:S(2)}) collective-permute-start(f32[120,128]{1,0:T(8,128)S(1)} %get-tuple-element.27), channel_id=1, source_target_pairs={{0,3},{1,0},{2,1},{3,2},{4,7},{5,4},{6,5},{7,6},{8,11},{9,8},{10,9... | collective-permute-start | bytes 184328 | tf_op jit(solution)/shard_map/ppermute | solution.py:527
  5.7 1.8 %collective-permute-start = (f32[80,128]{1,0:T(8,128)S(1)}, f32[80,128]{1,0:T(8,128)S(1)}, u32[]{:S(2)}, u32[]{:S(2)}) collective-permute-start(f32[80,128]{1,0:T(8,128)S(1)} %get-tuple-element.24.after.p0), channel_id=1, source_target_pairs={{0,2},{1,3},{2,0},{3,1},{4,6},{5,7},{6,4},{7,5},{8,10},{9,11},{10,... | collective-permute-start | bytes 122888 | tf_op jit(solution)/shard_map/ppermute | solution.py:528
  7.5 2.2 %table_kernel.1 = (bf16[2,4,320,256]{3,2,1,0:T(8,128)(2,1)S(1)}, bf16[2,2,2,256,512]{4,3,2,1,0:T(8,128)(2,1)S(1)}, bf16[128,768]{1,0:T(8,128)(2,1)S(1)}) custom-call(f32[80,128]{1,0:T(8,128)S(1)} %get-tuple-element.24.after.p0), custom_call_target="tpu_custom_call" | custom-call | tf_op jit(solution)/shard_map/table_kernel/pallas_call | solution.py:519
  9.7 1.5 %collective-permute-done.p2 = f32[80,128]{1,0:T(8,128)S(1)} collective-permute-done((f32[80,128]{1,0:T(8,128)S(1)}, f32[80,128]{1,0:T(8,128)S(1)}, u32[]{:S(2)}, u32[]{:S(2)}) %collective-permute-start) | collective-permute-done | bytes 40992 | tf_op jit(solution)/shard_map/ppermute | solution.py:528
  11.2 0.0 collective-permute-done.1.p1
  11.2 0.0 collective-permute-done.2.p3
  11.3 0.1 merge_kernel.1
  11.3 3.1 %collective-permute-start.5 = (f32[304,128]{1,0:T(8,128)S(1)}, f32[304,128]{1,0:T(8,128)S(1)}, u32[]{:S(2)}, u32[]{:S(2)}) collective-permute-start(f32[304,128]{1,0:T(8,128)S(1)} %get-tuple-element.30), channel_id=1, source_target_pairs={{0,12},{1,13},{2,14},{3,15},{4,8},{5,9},{6,10},{7,11},{8,4},{9,5},... | collective-permute-start | bytes 466952 | tf_op jit(solution)/shard_map/ppermute | solution.py:533
  14.4 0.1 collective-permute-start.4
  14.6 1.5 %collective-permute-start.3 = (f32[272,128]{1,0:T(8,128)S(1)}, f32[272,128]{1,0:T(8,128)S(1)}, u32[]{:S(2)}, u32[]{:S(2)}) collective-permute-start(f32[272,128]{1,0:T(8,128)S(1)} %get-tuple-element.28.ref), channel_id=1, source_target_pairs={{0,8},{1,9},{2,10},{3,11},{4,12},{5,13},{6,14},{7,15},{8,0},{9,1},... | collective-permute-start | bytes 417800 | tf_op jit(solution)/shard_map/ppermute | solution.py:535
  16.1 0.9 %group_kernel.5.refs_0_ = f32[4,160,256]{2,1,0:T(8,128)S(1)} custom-call(f32[272,128]{1,0:T(8,128)S(1)} %get-tuple-element.28.ref, bf16[2,4,320,256]{3,2,1,0:T(8,128)(2,1)S(1)} %get-tuple-element.25.after.utab, bf16[128,768]{1,0:T(8,128)(2,1)S(1)} %get-tuple-element.29.spot), custom_call_target="tpu_custom_call" | custom-call | tf_op jit(solution)/shard_map/group_kernel/pallas_call | solution.py:540
  17.0 2.4 %collective-permute-done.5.ref.partner = f32[304,128]{1,0:T(8,128)S(1)} collective-permute-done((f32[304,128]{1,0:T(8,128)S(1)}, f32[304,128]{1,0:T(8,128)S(1)}, u32[]{:S(2)}, u32[]{:S(2)}) %collective-permute-start.5) | collective-permute-done | bytes 155680 | tf_op jit(solution)/shard_map/ppermute | solution.py:533
  19.3 0.9 %group_kernel.6.refs_0_ = f32[4,160,256]{2,1,0:T(8,128)S(1)} custom-call(f32[304,128]{1,0:T(8,128)S(1)} %collective-permute-done.5.ref.partner, bf16[2,4,320,256]{3,2,1,0:T(8,128)(2,1)S(1)} %get-tuple-element.25.after.utab, bf16[128,768]{1,0:T(8,128)(2,1)S(1)} %get-tuple-element.29.spot, f32[4,160,256]{2,1,0:T(8,128)S(1)} %group_kernel.5.refs_0_), custom_call_target="tpu_custom_call" | custom-call | tf_op jit(solution)/shard_map/group_kernel/pallas_call | solution.py:540
  20.2 0.0 copy-start
  20.2 0.0 collective-permute-done.4.ref.beside
  20.2 0.9 %group_kernel.7.refs_0_ = f32[4,160,256]{2,1,0:T(8,128)S(1)} custom-call(f32[304,128]{1,0:T(8,128)S(1)} %collective-permute-done.4.ref.beside, bf16[2,4,320,256]{3,2,1,0:T(8,128)(2,1)S(1)} %get-tuple-element.25.after.utab, bf16[128,768]{1,0:T(8,128)(2,1)S(1)} %get-tuple-element.29.spot, f32[4,160,256]{2,1,0:T(8,128)S(1)} %group_kernel.6.refs_0_), custom_call_target="tpu_custom_call" | custom-call | tf_op jit(solution)/shard_map/group_kernel/pallas_call | solution.py:540
  21.1 0.1 copy-done
  21.2 0.4 %weight_kernel.1 = (f32[64,1024]{1,0:T(8,128)S(1)}, f32[16,512]{1,0:T(8,128)S(1)}, f32[16,128]{1,0:T(8,128)S(1)}, bf16[1024,256]{1,0:T(8,128)(2,1)S(1)}) custom-call(f32[64,1024]{1,0:T(8,128)S(1)} %copy-done, f32[120,128]{1,0:T(8,128)S(1)} %collective-permute-done.1.p1, f32[120,128]{1,0:T(8,128)S(1)} %collective-permute-done.2.p3, ...), custom_call_target="tpu_custom_call" | custom-call | tf_op jit(solution)/shard_map/weight_kernel/pallas_call | solution.py:545
  21.5 0.0 collective-permute-done.3.ref
  21.6 0.6 %group_kernel.8.refs_1_ = f32[352,256]{1,0:T(8,128)S(1)} custom-call(f32[272,128]{1,0:T(8,128)S(1)} %collective-permute-done.3.ref, bf16[2,4,320,256]{3,2,1,0:T(8,128)(2,1)S(1)} %get-tuple-element.25.after.utab, bf16[128,768]{1,0:T(8,128)(2,1)S(1)} %get-tuple-element.29.spot, f32[4,160,256]{2,1,0:T(8,128)S(1)} %group_kernel.7.refs_0_, ...), custom_call_target="tpu_custom_call" | custom-call | tf_op jit(solution)/shard_map/group_kernel/pallas_call | solution.py:540
  22.2 0.1 collective-permute-start.6
  22.3 0.6 %group_kernel.9.keep = f32[320,256]{1,0:T(8,128)S(1)} custom-call(f32[272,128]{1,0:T(8,128)S(1)} %collective-permute-done.3.ref, bf16[2,4,320,256]{3,2,1,0:T(8,128)(2,1)S(1)} %get-tuple-element.25.after.utab, bf16[128,768]{1,0:T(8,128)(2,1)S(1)} %get-tuple-element.29.spot, f32[4,160,256]{2,1,0:T(8,128)S(1)} %group_kernel.7.refs_0_, ...), custom_call_target="tpu_custom_call" | custom-call | tf_op jit(solution)/shard_map/group_kernel/pallas_call | solution.py:540
  22.9 0.0 copy-start.1
  22.9 1.0 %collective-permute-done.6.got = f32[352,256]{1,0:T(8,128)S(1)} collective-permute-done((f32[352,256]{1,0:T(8,128)S(1)}, f32[352,256]{1,0:T(8,128)S(1)}, u32[]{:S(2)}, u32[]{:S(2)}) %collective-permute-start.6) | collective-permute-done | bytes 360480 | tf_op jit(solution)/shard_map/ppermute | solution.py:555
  23.9 0.9 %lens_kernel.1 = (f32[32,128]{1,0:T(8,128)S(1)}, f32[32,128]{1,0:T(8,128)S(1)}) custom-call(f32[320,256]{1,0:T(8,128)S(1)} %group_kernel.9.keep, f32[352,256]{1,0:T(8,128)S(1)} %collective-permute-done.6.got, bf16[2,2,2,256,512]{4,3,2,1,0:T(8,128)(2,1)S(1)} %get-tuple-element.33.vtab, f32[64,1024]{1,0:T(8,128)S(1)} %get-tuple-element.34.weight, ...), custom_call_target="tpu_custom_call" | custom-call | tf_op jit(solution)/shard_map/lens_kernel/pallas_call | solution.py:556
  24.8 0.2 collective-permute-start.7
  25.0 1.0 %collective-permute-done.7.got = f32[32,128]{1,0:T(8,128)S(1)} collective-permute-done((f32[32,128]{1,0:T(8,128)S(1)}, f32[32,128]{1,0:T(8,128)S(1)}, u32[]{:S(2)}, u32[]{:S(2)}) %collective-permute-start.7) | collective-permute-done | bytes 16416 | tf_op jit(solution)/shard_map/ppermute | solution.py:559
  26.1 0.1 pack_kernel.1
  26.2 1.6 %collective-permute-start.8 = (f32[16,128]{1,0:T(8,128)S(1)}, f32[16,128]{1,0:T(8,128)S(1)}, u32[]{:S(2)}, u32[]{:S(2)}) collective-permute-start(f32[16,128]{1,0:T(8,128)S(1)} %get-tuple-element.40), channel_id=1, source_target_pairs={{0,32},{16,48},{32,64},{48,80},{64,96},{80,112},{96,0},{112,16},{1... | collective-permute-start | bytes 24584 | tf_op jit(solution)/shard_map/ppermute | solution.py:561
  27.7 2.7 %collective-permute-start.9 = (f32[16,128]{1,0:T(8,128)S(1)}, f32[16,128]{1,0:T(8,128)S(1)}, u32[]{:S(2)}, u32[]{:S(2)}) collective-permute-start(f32[16,128]{1,0:T(8,128)S(1)} %get-tuple-element.41), channel_id=1, source_target_pairs={{0,64},{16,80},{32,96},{48,112},{64,0},{80,16},{96,32},{112,48},{1... | collective-permute-start | bytes 24584 | tf_op jit(solution)/shard_map/ppermute | solution.py:561
  30.4 1.4 %collective-permute-start.10 = (f32[16,128]{1,0:T(8,128)S(1)}, f32[16,128]{1,0:T(8,128)S(1)}, u32[]{:S(2)}, u32[]{:S(2)}) collective-permute-start(f32[16,128]{1,0:T(8,128)S(1)} %get-tuple-element.42), channel_id=1, source_target_pairs={{0,96},{16,112},{32,0},{48,16},{64,32},{80,48},{96,64},{112,80},{1... | collective-permute-start | bytes 24584 | tf_op jit(solution)/shard_map/ppermute | solution.py:561
  31.9 0.0 collective-permute-done.8.a1
  31.9 1.0 %collective-permute-done.9.a2 = f32[16,128]{1,0:T(8,128)S(1)} collective-permute-done((f32[16,128]{1,0:T(8,128)S(1)}, f32[16,128]{1,0:T(8,128)S(1)}, u32[]{:S(2)}, u32[]{:S(2)}) %collective-permute-start.9) | collective-permute-done | bytes 8224 | tf_op jit(solution)/shard_map/ppermute | solution.py:561
  32.9 1.2 %collective-permute-done.10.a3 = f32[16,128]{1,0:T(8,128)S(1)} collective-permute-done((f32[16,128]{1,0:T(8,128)S(1)}, f32[16,128]{1,0:T(8,128)S(1)}, u32[]{:S(2)}, u32[]{:S(2)}) %collective-permute-start.10) | collective-permute-done | bytes 8224 | tf_op jit(solution)/shard_map/ppermute | solution.py:561
  34.1 0.0 copy-done.1
  34.1 2.0 %detector_kernel.1 = f32[256,512]{1,0:T(8,128)} custom-call(f32[5,5]{1,0:T(8,128)S(1)} %copy-done.1, f32[16,128]{1,0:T(8,128)S(1)} %get-tuple-element.39.a0, f32[16,128]{1,0:T(8,128)S(1)} %collective-permute-done.8.a1, f32[16,128]{1,0:T(8,128)S(1)} %collective-permute-done.9.a2, f32[16,128]{1,0:T(8,128)S(1)} %collective-permute-done.10.a3, ...), custom_call_target="tpu_custom_call" | custom-call | tf_op jit(solution)/shard_map/detector_kernel/pallas_call | solution.py:565
  (1 shorter events, 0.0 us)
Async XLA Ops:
  1.4 9.8 %collective-permute-start.1 = (f32[120,128]{1,0:T(8,128)S(1)}, f32[120,128]{1,0:T(8,128)S(1)}, u32[]{:S(2)}, u32[]{:S(2)}) collective-permute-start(f32[120,128]{1,0:T(8,128)S(1)} %get-tuple-element.26), channel_id=1, source_target_pairs={{0,1},{1,2},{2,3},{3,0},{4,5},{5,6},{6,7},{7,4},{8,9},{9,10},{10,1... | collective-permute-start | bytes 184328 | tf_op jit(solution)/shard_map/ppermute | solution.py:526
  3.5 7.7 %collective-permute-start.2 = (f32[120,128]{1,0:T(8,128)S(1)}, f32[120,128]{1,0:T(8,128)S(1)}, u32[]{:S(2)}, u32[]{:S(2)}) collective-permute-start(f32[120,128]{1,0:T(8,128)S(1)} %get-tuple-element.27), channel_id=1, source_target_pairs={{0,3},{1,0},{2,1},{3,2},{4,7},{5,4},{6,5},{7,6},{8,11},{9,8},{10,9... | collective-permute-start | bytes 184328 | tf_op jit(solution)/shard_map/ppermute | solution.py:527
  5.7 5.5 %collective-permute-start = (f32[80,128]{1,0:T(8,128)S(1)}, f32[80,128]{1,0:T(8,128)S(1)}, u32[]{:S(2)}, u32[]{:S(2)}) collective-permute-start(f32[80,128]{1,0:T(8,128)S(1)} %get-tuple-element.24.after.p0), channel_id=1, source_target_pairs={{0,2},{1,3},{2,0},{3,1},{4,6},{5,7},{6,4},{7,5},{8,10},{9,11},{10,... | collective-permute-start | bytes 122888 | tf_op jit(solution)/shard_map/ppermute | solution.py:528
  11.3 8.0 %collective-permute-start.5 = (f32[304,128]{1,0:T(8,128)S(1)}, f32[304,128]{1,0:T(8,128)S(1)}, u32[]{:S(2)}, u32[]{:S(2)}) collective-permute-start(f32[304,128]{1,0:T(8,128)S(1)} %get-tuple-element.30), channel_id=1, source_target_pairs={{0,12},{1,13},{2,14},{3,15},{4,8},{5,9},{6,10},{7,11},{8,4},{9,5},... | collective-permute-start | bytes 466952 | tf_op jit(solution)/shard_map/ppermute | solution.py:533
  14.4 5.8 %collective-permute-start.4 = (f32[304,128]{1,0:T(8,128)S(1)}, f32[304,128]{1,0:T(8,128)S(1)}, u32[]{:S(2)}, u32[]{:S(2)}) collective-permute-start(f32[304,128]{1,0:T(8,128)S(1)} %get-tuple-element.30), channel_id=1, source_target_pairs={{0,4},{1,5},{2,6},{3,7},{4,0},{5,1},{6,2},{7,3},{8,12},{9,13},{10,... | collective-permute-start | bytes 466952 | tf_op jit(solution)/shard_map/ppermute | solution.py:534
  14.6 7.0 %collective-permute-start.3 = (f32[272,128]{1,0:T(8,128)S(1)}, f32[272,128]{1,0:T(8,128)S(1)}, u32[]{:S(2)}, u32[]{:S(2)}) collective-permute-start(f32[272,128]{1,0:T(8,128)S(1)} %get-tuple-element.28.ref), channel_id=1, source_target_pairs={{0,8},{1,9},{2,10},{3,11},{4,12},{5,13},{6,14},{7,15},{8,0},{9,1},... | collective-permute-start | bytes 417800 | tf_op jit(solution)/shard_map/ppermute | solution.py:535
  20.2 1.0 %copy-start = (f32[64,1024]{1,0:T(8,128)S(1)}, f32[64,1024]{1,0:T(8,128)}, u32[]{:S(2)}) copy-start(f32[64,1024]{1,0:T(8,128)} %mask.3) | copy-start | bytes 786436
  22.2 1.8 %collective-permute-start.6 = (f32[352,256]{1,0:T(8,128)S(1)}, f32[352,256]{1,0:T(8,128)S(1)}, u32[]{:S(2)}, u32[]{:S(2)}) collective-permute-start(f32[352,256]{1,0:T(8,128)S(1)} %group_kernel.8.refs_1_), channel_id=1, source_target_pairs={{0,16},{16,0},{32,48},{48,32},{64,80},{80,64},{96,112},{112,96},{1... | collective-permute-start | bytes 1081352 | tf_op jit(solution)/shard_map/ppermute | solution.py:555
  22.9 11.2 %copy-start.1 = (f32[5,5]{1,0:T(8,128)S(1)}, f32[5,5]{1,0:T(8,128)}, u32[]{:S(2)}) copy-start(f32[5,5]{1,0:T(8,128)} %kernel.1) | copy-start | bytes 304
  24.8 1.2 %collective-permute-start.7 = (f32[32,128]{1,0:T(8,128)S(1)}, f32[32,128]{1,0:T(8,128)S(1)}, u32[]{:S(2)}, u32[]{:S(2)}) collective-permute-start(f32[32,128]{1,0:T(8,128)S(1)} %get-tuple-element.38), channel_id=1, source_target_pairs={{0,16},{16,0},{32,48},{48,32},{64,80},{80,64},{96,112},{112,96},{1... | collective-permute-start | bytes 49160 | tf_op jit(solution)/shard_map/ppermute | solution.py:559
  26.2 5.7 %collective-permute-start.8 = (f32[16,128]{1,0:T(8,128)S(1)}, f32[16,128]{1,0:T(8,128)S(1)}, u32[]{:S(2)}, u32[]{:S(2)}) collective-permute-start(f32[16,128]{1,0:T(8,128)S(1)} %get-tuple-element.40), channel_id=1, source_target_pairs={{0,32},{16,48},{32,64},{48,80},{64,96},{80,112},{96,0},{112,16},{1... | collective-permute-start | bytes 24584 | tf_op jit(solution)/shard_map/ppermute | solution.py:561
  27.7 5.2 %collective-permute-start.9 = (f32[16,128]{1,0:T(8,128)S(1)}, f32[16,128]{1,0:T(8,128)S(1)}, u32[]{:S(2)}, u32[]{:S(2)}) collective-permute-start(f32[16,128]{1,0:T(8,128)S(1)} %get-tuple-element.41), channel_id=1, source_target_pairs={{0,64},{16,80},{32,96},{48,112},{64,0},{80,16},{96,32},{112,48},{1... | collective-permute-start | bytes 24584 | tf_op jit(solution)/shard_map/ppermute | solution.py:561
  30.4 3.7 %collective-permute-start.10 = (f32[16,128]{1,0:T(8,128)S(1)}, f32[16,128]{1,0:T(8,128)S(1)}, u32[]{:S(2)}, u32[]{:S(2)}) collective-permute-start(f32[16,128]{1,0:T(8,128)S(1)} %get-tuple-element.42), channel_id=1, source_target_pairs={{0,96},{16,112},{32,0},{48,16},{64,32},{80,48},{96,64},{112,80},{1... | collective-permute-start | bytes 24584 | tf_op jit(solution)/shard_map/ppermute | solution.py:561

commit v6 on v5

--- a/solution.py
+++ b/solution.py
@@ -155,17 +155,12 @@
                 out[GROUP + 2 * at:GROUP + 2 * at + 2, :] = piece[ROWS:ROWS + 2, :]
 
 
-def opposite_kernel(p0, p2, after, out):
+def merge_kernel(p0, p1, p2, p3, after, out, more):
     del after
     out[GROUP:MROWS, :] = jnp.zeros((8, 128), F32)
     out[MROWS + GROUP:2 * MROWS, :] = jnp.zeros((8, 128), F32)
-    place_pieces(out, ((0, p0), (2, p2)))
-
-
-def merge_kernel(begun, p1, p3, out, more):
-    del begun
-    w, s, y, z, x, core, sign, pair = place_of()
-    place_pieces(out, ((1, p1), (3, p3)))
+    w, s, y, z, x, core, sign, pair = place_of()
+    place_pieces(out, enumerate((p0, p1, p2, p3)))
     more[0:2 * MROWS, :] = out[...]
     wrap = jnp.where(z == 0, p1[PIECE:PIECE + EDGE, :], p3[PIECE:PIECE + EDGE, :])
     more[2 * MROWS:2 * MROWS + 32, :] = wrap[0:32]
@@ -240,7 +235,30 @@
     return jnp.concatenate([f[:rows] + f[rows:2 * rows] + f[2 * rows:] for f in found], axis=1)
 
 
-def weight_kernel(mask, p1, p3, partner, beside, trace, weight, border, lenses, smat, full, edges):
+def fading(s):
+    down, across = odd(focal_row(s, (UROWS, FHALF)), NF) * 0.5, odd(iota((UROWS, FHALF), 1), NF) * 0.5
+    return 1.0 - jnp.exp((down * down + across * across) * (-1.0 / 1024.0))
+
+
+def weight_kernel(mask, after, weight, smat, full):
+    del after
+    w, s, y, z, x, core, sign, pair = place_of()
+    fade = fading(s)
+    for q in range(8):
+        for a in range(8):
+            full[q, pl.ds(a, 8, stride=8), :] = mask[8 * a:8 * a + 8, 128 * q:128 * q + 128]
+    left, right = (jnp.concatenate([full[4 * k + q, 0:FROWS, :] for q in range(4)], axis=1) for k in range(2))
+    for k, part in enumerate((left, flipped_columns(right))):
+        t = part * fade[:FROWS]
+        weight[:, FHALF * k:FHALF * (k + 1)] = t * t * 2.0**-24
+    row, lane = iota((FHALF, 256), 0), iota((FHALF, 256), 1)
+    column = 2 * ((lane >> 5) & 3) + jnp.where(lane < 128, core, 1 - core)
+    lens = jnp.where((lane & 31) < 18, 16 * column - 1 + (lane & 31), -1)
+    smat[0:FHALF, :] = (lens == row >> 3).astype(BF16)
+    smat[FHALF:NF, :] = (lens == NL - 1 - (row >> 3)).astype(BF16)
+
+
+def border_kernel(p1, p3, beside, partner, trace, border, lenses, edges):
     w, s, y, z, x, core, sign, pair = place_of()
     rows, row = slice(2 * MROWS, 2 * MROWS + 32), slice(MROWS + GROUP, 2 * MROWS)
     inner, outer = jnp.where(z == 0, y == 2, y == 1), jnp.where(z == 0, y == 0, y == 3)
@@ -252,41 +270,16 @@
     lenses[8:9, :] = above[1][0:1]
     lenses[9:10, :] = below[1][0:1]
     lenses[10:16, :] = jnp.zeros((6, 128), F32)
-    v = iota((UROWS, FHALF), 1)
-    down, across = odd(focal_row(s, (UROWS, FHALF)), NF) * 0.5, odd(v, NF) * 0.5
-    fade = 1.0 - jnp.exp((down * down + across * across) * (-1.0 / 1024.0))
-    for q in range(8):
-        for a in range(8):
-            full[q, pl.ds(a, 8, stride=8), :] = mask[8 * a:8 * a + 8, 128 * q:128 * q + 128]
     for q in range(4):
         edges[q, pl.ds(0, 8, stride=2), :] = above[0][8 * q:8 * q + 8]
         edges[q, pl.ds(1, 8, stride=2), :] = below[0][8 * q:8 * q + 8]
     half = jnp.concatenate([edges[q, 0:16, :] for q in range(4)], axis=1)
     half = jnp.where(core == 0, half, flipped_columns(half))
-    t = half * fade[FROWS:]
+    t = half * fading(s)[FROWS:]
     border[...] = t * t * 2.0**-24
-    left, right = (jnp.concatenate([full[4 * k + q, 0:FROWS, :] for q in range(4)], axis=1) for k in range(2))
-    for k, part in enumerate((left, flipped_columns(right))):
-        t = part * fade[:FROWS]
-        weight[:, FHALF * k:FHALF * (k + 1)] = t * t * 2.0**-24
-    row, lane = iota((FHALF, 256), 0), iota((FHALF, 256), 1)
-    column = 2 * ((lane >> 5) & 3) + jnp.where(lane < 128, core, 1 - core)
-    lens = jnp.where((lane & 31) < 18, 16 * column - 1 + (lane & 31), -1)
-    smat[0:FHALF, :] = (lens == row >> 3).astype(BF16)
-    smat[FHALF:NF, :] = (lens == NL - 1 - (row >> 3)).astype(BF16)
-
-
-def group_kernel(ref, utab, spot, *refs, p, flipped, waves=range(4)):
-    before = refs[0] if flipped or p else None
-    outs, (whi, wlo) = refs[before is not None:-2], refs[-2:]
-    if len(waves) == 4:
-        outs = [outs[0].at[m] for m in range(4)]
-    else:
-        *rest, out = outs
-        outs = {m: out.at[2 * UROWS * (m & 1):2 * UROWS * ((m & 1) + 1), :] for m in waves}
-        if 2 in waves:
-            for k in range(2):
-                out[4 * UROWS + 16 * k:4 * UROWS + 16 * k + 16, :] = rest[0][:, 256 * k:256 * k + 256]
+
+
+def group_fields(ref, utab, spot, whi, wlo, p, flipped, waves=range(4)):
     w, s, y, z, x, core, sign, pair = place_of()
     g = pair if p == 0 else 1 - pair
     turned = -1.0 if flipped else 1.0
@@ -322,18 +315,32 @@
                 r0, c0 = GROUP * (k >> 1) + 16 * r2, 128 * (k & 1)
                 whi[m, r0:r0 + 16, c0:c0 + 128] = high
                 wlo[m, r0:r0 + 16, c0:c0 + 128] = low
+    fields = {}
     for m in waves:
         table = utab[p, m]
         both = dot(table, whi[m])
         field = both[:2 * UROWS] + both[2 * UROWS:] + dot(table[:2 * UROWS], wlo[m])
-        out = outs[m]
-        if before is None:
-            out[...] = field
-        elif flipped:
-            out[0:UROWS] = before[m, 0:UROWS] + field[:UROWS]
-            out[UROWS:2 * UROWS] = before[m, UROWS:2 * UROWS] - field[UROWS:]
-        else:
-            out[...] = before[m] + field
+        fields[m] = jnp.concatenate([field[:UROWS], -field[UROWS:]], axis=0) if flipped else field
+    return fields
+
+
+def own_kernel(ref, utab, spot, out, whi, wlo):
+    for m, field in group_fields(ref, utab, spot, whi, wlo, 0, False).items():
+        out[m] = field
+
+
+def neighbour_kernel(ref, utab, spot, before, after, out, whi, wlo, *, p, flipped):
+    del after
+    for m, field in group_fields(ref, utab, spot, whi, wlo, p, flipped).items():
+        out[m] = before[m] + field
+
+
+def last_kernel(ref, utab, spot, before, border, out, whi, wlo, *, waves):
+    for m, field in group_fields(ref, utab, spot, whi, wlo, 1, True, waves).items():
+        out[2 * UROWS * (m & 1):2 * UROWS * ((m & 1) + 1), :] = before[m] + field
+    if 2 in waves:
+        for k in range(2):
+            out[4 * UROWS + 16 * k:4 * UROWS + 16 * k + 16, :] = border[:, 256 * k:256 * k + 256]
 
 
 def lens_kernel(keep, got, vtab, weight, border, smat, lenses, mine, other):
@@ -526,31 +533,34 @@
     p1 = lax.ppermute(up, "slab", along_z(1))
     p3 = lax.ppermute(down, "slab", along_z(3))
     p2 = lax.ppermute(piece, "slab", along_z(2))
-    begun = call(opposite_kernel, shape(2 * MROWS, 128), 0, 3, tail=anywhere)(piece, p2, utab)
     own, more = call(
-        merge_kernel, [shape(2 * MROWS, 128), shape(2 * MROWS + 32, 128)], 0, 3, aliases={0: 0}
-    )(begun, p1, p3)
+        merge_kernel, [shape(2 * MROWS, 128), shape(2 * MROWS + 32, 128)], 0, 5, tail=anywhere
+    )(piece, p1, p2, p3, utab)
     partner = lax.ppermute(more, "slab", along_y((3, 2, 1, 0)))
     beside = lax.ppermute(more, "slab", along_y((1, 0, 3, 2)))
     last = lax.ppermute(own, "slab", along_y((2, 3, 0, 1)))
     scratch = [pltpu.VMEM((4, 256, 256), BF16)] * 2
-
-    def add(group, p, flipped, *before, outs=shape(4, 2 * UROWS, 256), tail=(), **options):
-        kernel = functools.partial(group_kernel, p=p, flipped=flipped, **options)
-        return call(kernel, outs, 0, 3 + len(before), scratch, tail=tail)(group, utab, spot, *before)
-
-    field = add(own, 0, False)
-    field = add(partner, 0, True, field)
-    field = add(beside, 1, False, field)
-    weight, border, lenses, smat = call(
+    field = call(own_kernel, shape(4, 2 * UROWS, 256), 0, 3, scratch)(own, utab, spot)
+    weight, smat = call(
         weight_kernel,
-        [shape(FROWS, NF), shape(16, FHALF), shape(16, 128), shape(NF, 256, dtype=BF16)],
+        [shape(FROWS, NF), shape(NF, 256, dtype=BF16)],
         0,
-        6,
-        [pltpu.VMEM((8, FROWS + 8, 128), F32), pltpu.VMEM((4, 24, 128), F32)],
-    )(focal_mask, p1, p3, partner, beside, trace)
-    give = add(last, 1, True, field, border, outs=shape(4 * UROWS + 32, 256), waves=(2, 3))
-    keep = add(last, 1, True, field, give, outs=shape(4 * UROWS, 256), waves=(0, 1), tail=anywhere)
+        2,
+        [pltpu.VMEM((8, FROWS + 8, 128), F32)],
+        tail=anywhere,
+    )(focal_mask, field)
+    for group, p, flipped in ((partner, 0, True), (beside, 1, False)):
+        kernel = functools.partial(neighbour_kernel, p=p, flipped=flipped)
+        field = call(kernel, shape(4, 2 * UROWS, 256), 0, 5, scratch, tail=anywhere)(group, utab, spot, field, smat)
+    border, lenses = call(
+        border_kernel, [shape(16, FHALF), shape(16, 128)], 0, 5, [pltpu.VMEM((4, 24, 128), F32)]
+    )(p1, p3, beside, partner, trace)
+    give = call(functools.partial(last_kernel, waves=(2, 3)), shape(4 * UROWS + 32, 256), 0, 5, scratch)(
+        last, utab, spot, field, border
+    )
+    keep = call(functools.partial(last_kernel, waves=(0, 1)), shape(4 * UROWS, 256), 0, 5, scratch, tail=anywhere)(
+        last, utab, spot, field, give
+    )
     sibling = [(i, i ^ 1) for i in range(NWAV)]
     crossed = lax.ppermute(give, "wav", sibling)
     mine, other = call(lens_kernel, [shape(32, 128)] * 2, 0, 7)(

time: 36.4 us -> 36.1 us (level)
  transfers between devices with their start and end apart: 11 -> 11, of which waited for: 6 -> 7; matrix products, arithmetic and copies ran while one was open for 0% -> 0% of each run, Pallas kernels for 16% -> 16%
where the time goes in v6:
time: 36.1 us; the launch traced here: 36 us
  starting transfers between devices  16.8 us (47%)
  Pallas kernels  11.1 us (31%)
  waiting for transfers between devices  7.89 us (22%)
    ppermute x3, starting transfers between devices, along_x(): lax.ppermute(sent, 'wav', [(i, (i + 2 * k) % NWAV) for i in range(NWAV)])  5.72 us
    ppermute x1, starting transfers between devices, body(): partner = lax.ppermute(more, 'slab', along_y((3, 2, 1, 0)))  3.09 us
    pallas_call x1, Pallas kernels, body(): call(table_kernel, [shape(2, 4, 4 * UROWS, 256, dtype=BF16), shape(2, 2,...  2.24 us
    ppermute x3, waiting for transfers between devices, along_x(): lax.ppermute(sent, 'wav', [(i, (i + 2 * k) % NWAV) for i in range(NWAV)])  2.22 us
    ppermute x1, starting transfers between devices, body(): p3 = lax.ppermute(down, 'slab', along_z(3))  2.2 us
    ppermute x1, starting transfers between devices, body(): p1 = lax.ppermute(up, 'slab', along_z(1))  2.07 us
    ppermute x1, waiting for transfers between devices, body(): partner = lax.ppermute(more, 'slab', along_y((3, 2, 1, 0)))  2.04 us
    pallas_call x1, Pallas kernels, body(): call(detector_kernel, shape(256, 512), 0, 6, [pltpu.VMEM((WAVES, 16, 128)...  2.02 us
  transfers between devices with their start and end apart: 11, of which 7 were waited for; matrix products, arithmetic and copies ran while one was open for 0% of the time, Pallas kernels for 16%

profile of v6, /device:TPU:0, one launch (start us, length us, event | category | flops | bytes accessed | tf_op | source)
XLA Modules:
  0.0 36.0 jit_solution(5934604831246519955)
XLA Ops:
  0.0 0.0 copy-start
  0.0 1.5 %prepare_kernel.1 = (f32[80,128]{1,0:T(8,128)S(1)}, f32[120,128]{1,0:T(8,128)S(1)}, f32[120,128]{1,0:T(8,128)S(1)}, f32[8,128]{1,0:T(8,128)S(1)}) custom-call(f32[32,512]{1,0:T(8,128)} %amp_in.1, s32[32,512]{1,0:T(8,128)} %seg_in.1, s32[3,798]{1,0:T(4,128)} %bitcast.1, f32[64,1024]{1,0:T(8,128)} %mask.3, s32[8,16]{1,0:T(8,128)} %trow.1, s32[8,16]{1,0:T(8,128)} %tcol.1, ...), custom_call_target="tpu_custom_call" | custom-call | tf_op jit(solution)/shard_map/prepare_kernel/pallas_call | solution.py:511
  1.5 2.1 %collective-permute-start = (f32[120,128]{1,0:T(8,128)S(1)}, f32[120,128]{1,0:T(8,128)S(1)}, u32[]{:S(2)}, u32[]{:S(2)}) collective-permute-start(f32[120,128]{1,0:T(8,128)S(1)} %get-tuple-element.25), channel_id=1, source_target_pairs={{0,1},{1,2},{2,3},{3,0},{4,5},{5,6},{6,7},{7,4},{8,9},{9,10},{10,1... | collective-permute-start | bytes 184328 | tf_op jit(solution)/shard_map/ppermute | solution.py:533
  3.5 2.2 %collective-permute-start.2 = (f32[120,128]{1,0:T(8,128)S(1)}, f32[120,128]{1,0:T(8,128)S(1)}, u32[]{:S(2)}, u32[]{:S(2)}) collective-permute-start(f32[120,128]{1,0:T(8,128)S(1)} %get-tuple-element.26), channel_id=1, source_target_pairs={{0,3},{1,0},{2,1},{3,2},{4,7},{5,4},{6,5},{7,6},{8,11},{9,8},{10,9... | collective-permute-start | bytes 184328 | tf_op jit(solution)/shard_map/ppermute | solution.py:534
  5.7 1.8 %collective-permute-start.1 = (f32[80,128]{1,0:T(8,128)S(1)}, f32[80,128]{1,0:T(8,128)S(1)}, u32[]{:S(2)}, u32[]{:S(2)}) collective-permute-start(f32[80,128]{1,0:T(8,128)S(1)} %get-tuple-element.24.after.p0), channel_id=1, source_target_pairs={{0,2},{1,3},{2,0},{3,1},{4,6},{5,7},{6,4},{7,5},{8,10},{9,11},{10,... | collective-permute-start | bytes 122888 | tf_op jit(solution)/shard_map/ppermute | solution.py:535
  7.5 2.2 %table_kernel.1 = (bf16[2,4,320,256]{3,2,1,0:T(8,128)(2,1)S(1)}, bf16[2,2,2,256,512]{4,3,2,1,0:T(8,128)(2,1)S(1)}, bf16[128,768]{1,0:T(8,128)(2,1)S(1)}) custom-call(f32[80,128]{1,0:T(8,128)S(1)} %get-tuple-element.24.after.p0), custom_call_target="tpu_custom_call" | custom-call | tf_op jit(solution)/shard_map/table_kernel/pallas_call | solution.py:526
  9.8 1.5 %collective-permute-done.1.p2 = f32[80,128]{1,0:T(8,128)S(1)} collective-permute-done((f32[80,128]{1,0:T(8,128)S(1)}, f32[80,128]{1,0:T(8,128)S(1)}, u32[]{:S(2)}, u32[]{:S(2)}) %collective-permute-start.1) | collective-permute-done | bytes 40992 | tf_op jit(solution)/shard_map/ppermute | solution.py:535
  11.3 0.0 collective-permute-done.p1
  11.3 0.0 collective-permute-done.2.p3
  11.3 0.1 merge_kernel.1
  11.4 3.1 %collective-permute-start.5 = (f32[304,128]{1,0:T(8,128)S(1)}, f32[304,128]{1,0:T(8,128)S(1)}, u32[]{:S(2)}, u32[]{:S(2)}) collective-permute-start(f32[304,128]{1,0:T(8,128)S(1)} %get-tuple-element.30), channel_id=1, source_target_pairs={{0,12},{1,13},{2,14},{3,15},{4,8},{5,9},{6,10},{7,11},{8,4},{9,5},... | collective-permute-start | bytes 466952 | tf_op jit(solution)/shard_map/ppermute | solution.py:539
  14.5 0.1 collective-permute-start.4
  14.6 1.5 %collective-permute-start.3 = (f32[272,128]{1,0:T(8,128)S(1)}, f32[272,128]{1,0:T(8,128)S(1)}, u32[]{:S(2)}, u32[]{:S(2)}) collective-permute-start(f32[272,128]{1,0:T(8,128)S(1)} %get-tuple-element.28.ref), channel_id=1, source_target_pairs={{0,8},{1,9},{2,10},{3,11},{4,12},{5,13},{6,14},{7,15},{8,0},{9,1},... | collective-permute-start | bytes 417800 | tf_op jit(solution)/shard_map/ppermute | solution.py:541
  16.2 0.9 %own_kernel.1.after.before = f32[4,160,256]{2,1,0:T(8,128)S(1)} custom-call(f32[272,128]{1,0:T(8,128)S(1)} %get-tuple-element.28.ref, bf16[2,4,320,256]{3,2,1,0:T(8,128)(2,1)S(1)} %get-tuple-element.27.after.utab, bf16[128,768]{1,0:T(8,128)(2,1)S(1)} %get-tuple-element.29.spot), custom_call_target="tpu_custom_call" | custom-call | tf_op jit(solution)/shard_map/own_kernel/pallas_call | solution.py:543
  17.0 0.0 copy-done
  17.0 0.3 weight_kernel.1
  17.4 2.0 %collective-permute-done.5.ref.partner = f32[304,128]{1,0:T(8,128)S(1)} collective-permute-done((f32[304,128]{1,0:T(8,128)S(1)}, f32[304,128]{1,0:T(8,128)S(1)}, u32[]{:S(2)}, u32[]{:S(2)}) %collective-permute-start.5) | collective-permute-done | bytes 155680 | tf_op jit(solution)/shard_map/ppermute | solution.py:539
  19.4 0.9 %neighbour_kernel.2.before = f32[4,160,256]{2,1,0:T(8,128)S(1)} custom-call(f32[304,128]{1,0:T(8,128)S(1)} %collective-permute-done.5.ref.partner, bf16[2,4,320,256]{3,2,1,0:T(8,128)(2,1)S(1)} %get-tuple-element.27.after.utab, bf16[128,768]{1,0:T(8,128)(2,1)S(1)} %get-tuple-element.29.spot, f32[4,160,256]{2,1,0:T(8,128)S(1)} %own_kernel.1.after.before, ...), custom_call_target="tpu_custom_call" | custom-call | tf_op jit(solution)/shard_map/neighbour_kernel/pallas_call | solution.py:554
  20.3 0.0 collective-permute-done.4.ref.beside
  20.3 0.2 border_kernel.1
  20.4 0.9 %neighbour_kernel.3.before = f32[4,160,256]{2,1,0:T(8,128)S(1)} custom-call(f32[304,128]{1,0:T(8,128)S(1)} %collective-permute-done.4.ref.beside, bf16[2,4,320,256]{3,2,1,0:T(8,128)(2,1)S(1)} %get-tuple-element.27.after.utab, bf16[128,768]{1,0:T(8,128)(2,1)S(1)} %get-tuple-element.29.spot, f32[4,160,256]{2,1,0:T(8,128)S(1)} %neighbour_kernel.2.before, ...), custom_call_target="tpu_custom_call" | custom-call | tf_op jit(solution)/shard_map/neighbour_kernel/pallas_call | solution.py:554
  21.3 0.1 collective-permute-done.3.ref
  21.4 0.6 %last_kernel.2.border = f32[352,256]{1,0:T(8,128)S(1)} custom-call(f32[272,128]{1,0:T(8,128)S(1)} %collective-permute-done.3.ref, bf16[2,4,320,256]{3,2,1,0:T(8,128)(2,1)S(1)} %get-tuple-element.27.after.utab, bf16[128,768]{1,0:T(8,128)(2,1)S(1)} %get-tuple-element.29.spot, f32[4,160,256]{2,1,0:T(8,128)S(1)} %neighbour_kernel.3.before, ...), custom_call_target="tpu_custom_call" | custom-call | tf_op jit(solution)/shard_map/last_kernel/pallas_call | solution.py:558
  22.0 0.1 collective-permute-start.6
  22.1 0.6 %last_kernel.3.keep = f32[320,256]{1,0:T(8,128)S(1)} custom-call(f32[272,128]{1,0:T(8,128)S(1)} %collective-permute-done.3.ref, bf16[2,4,320,256]{3,2,1,0:T(8,128)(2,1)S(1)} %get-tuple-element.27.after.utab, bf16[128,768]{1,0:T(8,128)(2,1)S(1)} %get-tuple-element.29.spot, f32[4,160,256]{2,1,0:T(8,128)S(1)} %neighbour_kernel.3.before, ...), custom_call_target="tpu_custom_call" | custom-call | tf_op jit(solution)/shard_map/last_kernel/pallas_call | solution.py:561
  22.7 0.0 copy-start.1
  22.7 1.0 %collective-permute-done.6.got = f32[352,256]{1,0:T(8,128)S(1)} collective-permute-done((f32[352,256]{1,0:T(8,128)S(1)}, f32[352,256]{1,0:T(8,128)S(1)}, u32[]{:S(2)}, u32[]{:S(2)}) %collective-permute-start.6) | collective-permute-done | bytes 360480 | tf_op jit(solution)/shard_map/ppermute | solution.py:565
  23.8 0.9 %lens_kernel.1 = (f32[32,128]{1,0:T(8,128)S(1)}, f32[32,128]{1,0:T(8,128)S(1)}) custom-call(f32[320,256]{1,0:T(8,128)S(1)} %last_kernel.3.keep, f32[352,256]{1,0:T(8,128)S(1)} %collective-permute-done.6.got, bf16[2,2,2,256,512]{4,3,2,1,0:T(8,128)(2,1)S(1)} %get-tuple-element.34.vtab, f32[64,1024]{1,0:T(8,128)S(1)} %get-tuple-element.35.weight, ...), custom_call_target="tpu_custom_call" | custom-call | tf_op jit(solution)/shard_map/lens_kernel/pallas_call | solution.py:566
  24.6 0.2 collective-permute-start.7
  24.8 1.1 %collective-permute-done.7.got = f32[32,128]{1,0:T(8,128)S(1)} collective-permute-done((f32[32,128]{1,0:T(8,128)S(1)}, f32[32,128]{1,0:T(8,128)S(1)}, u32[]{:S(2)}, u32[]{:S(2)}) %collective-permute-start.7) | collective-permute-done | bytes 16416 | tf_op jit(solution)/shard_map/ppermute | solution.py:569
  25.9 0.1 pack_kernel.1
  26.0 1.6 %collective-permute-start.8 = (f32[16,128]{1,0:T(8,128)S(1)}, f32[16,128]{1,0:T(8,128)S(1)}, u32[]{:S(2)}, u32[]{:S(2)}) collective-permute-start(f32[16,128]{1,0:T(8,128)S(1)} %get-tuple-element.40), channel_id=1, source_target_pairs={{0,32},{16,48},{32,64},{48,80},{64,96},{80,112},{96,0},{112,16},{1... | collective-permute-start | bytes 24584 | tf_op jit(solution)/shard_map/ppermute | solution.py:571
  27.6 2.7 %collective-permute-start.9 = (f32[16,128]{1,0:T(8,128)S(1)}, f32[16,128]{1,0:T(8,128)S(1)}, u32[]{:S(2)}, u32[]{:S(2)}) collective-permute-start(f32[16,128]{1,0:T(8,128)S(1)} %get-tuple-element.41), channel_id=1, source_target_pairs={{0,64},{16,80},{32,96},{48,112},{64,0},{80,16},{96,32},{112,48},{1... | collective-permute-start | bytes 24584 | tf_op jit(solution)/shard_map/ppermute | solution.py:571
  30.3 1.4 %collective-permute-start.10 = (f32[16,128]{1,0:T(8,128)S(1)}, f32[16,128]{1,0:T(8,128)S(1)}, u32[]{:S(2)}, u32[]{:S(2)}) collective-permute-start(f32[16,128]{1,0:T(8,128)S(1)} %get-tuple-element.42), channel_id=1, source_target_pairs={{0,96},{16,112},{32,0},{48,16},{64,32},{80,48},{96,64},{112,80},{1... | collective-permute-start | bytes 24584 | tf_op jit(solution)/shard_map/ppermute | solution.py:571
  31.7 0.0 collective-permute-done.8.a1
  31.7 1.0 %collective-permute-done.9.a2 = f32[16,128]{1,0:T(8,128)S(1)} collective-permute-done((f32[16,128]{1,0:T(8,128)S(1)}, f32[16,128]{1,0:T(8,128)S(1)}, u32[]{:S(2)}, u32[]{:S(2)}) %collective-permute-start.9) | collective-permute-done | bytes 8224 | tf_op jit(solution)/shard_map/ppermute | solution.py:571
  32.7 1.2 %collective-permute-done.10.a3 = f32[16,128]{1,0:T(8,128)S(1)} collective-permute-done((f32[16,128]{1,0:T(8,128)S(1)}, f32[16,128]{1,0:T(8,128)S(1)}, u32[]{:S(2)}, u32[]{:S(2)}) %collective-permute-start.10) | collective-permute-done | bytes 8224 | tf_op jit(solution)/shard_map/ppermute | solution.py:571
  33.9 0.0 copy-done.1
  34.0 2.0 %detector_kernel.1 = f32[256,512]{1,0:T(8,128)} custom-call(f32[5,5]{1,0:T(8,128)S(1)} %copy-done.1, f32[16,128]{1,0:T(8,128)S(1)} %get-tuple-element.39.a0, f32[16,128]{1,0:T(8,128)S(1)} %collective-permute-done.8.a1, f32[16,128]{1,0:T(8,128)S(1)} %collective-permute-done.9.a2, f32[16,128]{1,0:T(8,128)S(1)} %collective-permute-done.10.a3, ...), custom_call_target="tpu_custom_call" | custom-call | tf_op jit(solution)/shard_map/detector_kernel/pallas_call | solution.py:575
Async XLA Ops:
  0.0 17.0 %copy-start = (f32[64,1024]{1,0:T(8,128)S(1)}, f32[64,1024]{1,0:T(8,128)}, u32[]{:S(2)}) copy-start(f32[64,1024]{1,0:T(8,128)} %mask.3) | copy-start | bytes 786436
  1.5 9.8 %collective-permute-start = (f32[120,128]{1,0:T(8,128)S(1)}, f32[120,128]{1,0:T(8,128)S(1)}, u32[]{:S(2)}, u32[]{:S(2)}) collective-permute-start(f32[120,128]{1,0:T(8,128)S(1)} %get-tuple-element.25), channel_id=1, source_target_pairs={{0,1},{1,2},{2,3},{3,0},{4,5},{5,6},{6,7},{7,4},{8,9},{9,10},{10,1... | collective-permute-start | bytes 184328 | tf_op jit(solution)/shard_map/ppermute | solution.py:533
  3.5 7.7 %collective-permute-start.2 = (f32[120,128]{1,0:T(8,128)S(1)}, f32[120,128]{1,0:T(8,128)S(1)}, u32[]{:S(2)}, u32[]{:S(2)}) collective-permute-start(f32[120,128]{1,0:T(8,128)S(1)} %get-tuple-element.26), channel_id=1, source_target_pairs={{0,3},{1,0},{2,1},{3,2},{4,7},{5,4},{6,5},{7,6},{8,11},{9,8},{10,9... | collective-permute-start | bytes 184328 | tf_op jit(solution)/shard_map/ppermute | solution.py:534
  5.7 5.5 %collective-permute-start.1 = (f32[80,128]{1,0:T(8,128)S(1)}, f32[80,128]{1,0:T(8,128)S(1)}, u32[]{:S(2)}, u32[]{:S(2)}) collective-permute-start(f32[80,128]{1,0:T(8,128)S(1)} %get-tuple-element.24.after.p0), channel_id=1, source_target_pairs={{0,2},{1,3},{2,0},{3,1},{4,6},{5,7},{6,4},{7,5},{8,10},{9,11},{10,... | collective-permute-start | bytes 122888 | tf_op jit(solution)/shard_map/ppermute | solution.py:535
  11.4 8.0 %collective-permute-start.5 = (f32[304,128]{1,0:T(8,128)S(1)}, f32[304,128]{1,0:T(8,128)S(1)}, u32[]{:S(2)}, u32[]{:S(2)}) collective-permute-start(f32[304,128]{1,0:T(8,128)S(1)} %get-tuple-element.30), channel_id=1, source_target_pairs={{0,12},{1,13},{2,14},{3,15},{4,8},{5,9},{6,10},{7,11},{8,4},{9,5},... | collective-permute-start | bytes 466952 | tf_op jit(solution)/shard_map/ppermute | solution.py:539
  14.5 5.8 %collective-permute-start.4 = (f32[304,128]{1,0:T(8,128)S(1)}, f32[304,128]{1,0:T(8,128)S(1)}, u32[]{:S(2)}, u32[]{:S(2)}) collective-permute-start(f32[304,128]{1,0:T(8,128)S(1)} %get-tuple-element.30), channel_id=1, source_target_pairs={{0,4},{1,5},{2,6},{3,7},{4,0},{5,1},{6,2},{7,3},{8,12},{9,13},{10,... | collective-permute-start | bytes 466952 | tf_op jit(solution)/shard_map/ppermute | solution.py:540
  14.6 6.8 %collective-permute-start.3 = (f32[272,128]{1,0:T(8,128)S(1)}, f32[272,128]{1,0:T(8,128)S(1)}, u32[]{:S(2)}, u32[]{:S(2)}) collective-permute-start(f32[272,128]{1,0:T(8,128)S(1)} %get-tuple-element.28.ref), channel_id=1, source_target_pairs={{0,8},{1,9},{2,10},{3,11},{4,12},{5,13},{6,14},{7,15},{8,0},{9,1},... | collective-permute-start | bytes 417800 | tf_op jit(solution)/shard_map/ppermute | solution.py:541
  22.0 1.8 %collective-permute-start.6 = (f32[352,256]{1,0:T(8,128)S(1)}, f32[352,256]{1,0:T(8,128)S(1)}, u32[]{:S(2)}, u32[]{:S(2)}) collective-permute-start(f32[352,256]{1,0:T(8,128)S(1)} %last_kernel.2.border), channel_id=1, source_target_pairs={{0,16},{16,0},{32,48},{48,32},{64,80},{80,64},{96,112},{112,96},{1... | collective-permute-start | bytes 1081352 | tf_op jit(solution)/shard_map/ppermute | solution.py:565
  22.7 11.2 %copy-start.1 = (f32[5,5]{1,0:T(8,128)S(1)}, f32[5,5]{1,0:T(8,128)}, u32[]{:S(2)}) copy-start(f32[5,5]{1,0:T(8,128)} %kernel.1) | copy-start | bytes 304
  24.6 1.3 %collective-permute-start.7 = (f32[32,128]{1,0:T(8,128)S(1)}, f32[32,128]{1,0:T(8,128)S(1)}, u32[]{:S(2)}, u32[]{:S(2)}) collective-permute-start(f32[32,128]{1,0:T(8,128)S(1)} %get-tuple-element.38), channel_id=1, source_target_pairs={{0,16},{16,0},{32,48},{48,32},{64,80},{80,64},{96,112},{112,96},{1... | collective-permute-start | bytes 49160 | tf_op jit(solution)/shard_map/ppermute | solution.py:569
  26.0 5.7 %collective-permute-start.8 = (f32[16,128]{1,0:T(8,128)S(1)}, f32[16,128]{1,0:T(8,128)S(1)}, u32[]{:S(2)}, u32[]{:S(2)}) collective-permute-start(f32[16,128]{1,0:T(8,128)S(1)} %get-tuple-element.40), channel_id=1, source_target_pairs={{0,32},{16,48},{32,64},{48,80},{64,96},{80,112},{96,0},{112,16},{1... | collective-permute-start | bytes 24584 | tf_op jit(solution)/shard_map/ppermute | solution.py:571
  27.6 5.2 %collective-permute-start.9 = (f32[16,128]{1,0:T(8,128)S(1)}, f32[16,128]{1,0:T(8,128)S(1)}, u32[]{:S(2)}, u32[]{:S(2)}) collective-permute-start(f32[16,128]{1,0:T(8,128)S(1)} %get-tuple-element.41), channel_id=1, source_target_pairs={{0,64},{16,80},{32,96},{48,112},{64,0},{80,16},{96,32},{112,48},{1... | collective-permute-start | bytes 24584 | tf_op jit(solution)/shard_map/ppermute | solution.py:571
  30.3 3.7 %collective-permute-start.10 = (f32[16,128]{1,0:T(8,128)S(1)}, f32[16,128]{1,0:T(8,128)S(1)}, u32[]{:S(2)}, u32[]{:S(2)}) collective-permute-start(f32[16,128]{1,0:T(8,128)S(1)} %get-tuple-element.42), channel_id=1, source_target_pairs={{0,96},{16,112},{32,0},{48,16},{64,32},{80,48},{96,64},{112,80},{1... | collective-permute-start | bytes 24584 | tf_op jit(solution)/shard_map/ppermute | solution.py:571

commit v7 on v6

--- a/solution.py
+++ b/solution.py
@@ -470,8 +470,11 @@
                 else:
                     part = h[2]
                 state = part, h[0], h[1], h[3], h[4]
-        copies.append(pltpu.make_async_copy(image.at[lt, 8:264, :], out.at[:, at], sems.at[lt]))
-        copies[-1].start()
+            if a in (5, 9):
+                rows = (0, 152) if a == 5 else (152, 256)
+                source, place = image.at[lt, rows[0] + 8:rows[1] + 8, :], out.at[rows[0]:rows[1], at]
+                copies.append(pltpu.make_async_copy(source, place, sems.at[len(copies)]))
+                copies[-1].start()
     for copy in copies:
         copy.wait()
 
@@ -582,7 +585,7 @@
             pltpu.VMEM((10, 16, 512), F32),
             pltpu.VMEM((4, 16, 512), F32),
             pltpu.VMEM((4, 264, 128), F32),
-            pltpu.SemaphoreType.DMA((4,)),
+            pltpu.SemaphoreType.DMA((8,)),
         ],
         outside=True,
     )(crosstalk, kept, *arrived, lenses)

time: 36.1 us -> 36.1 us (level)
  no operation moved by 1% of the time
where the time goes in v7:
time: 36.1 us; the launch traced here: 36 us
  starting transfers between devices  16.8 us (47%)
  Pallas kernels  11.1 us (31%)
  waiting for transfers between devices  7.89 us (22%)
    ppermute x3, starting transfers between devices, along_x(): lax.ppermute(sent, 'wav', [(i, (i + 2 * k) % NWAV) for i in range(NWAV)])  5.72 us
    ppermute x1, starting transfers between devices, body(): partner = lax.ppermute(more, 'slab', along_y((3, 2, 1, 0)))  3.09 us
    pallas_call x1, Pallas kernels, body(): call(table_kernel, [shape(2, 4, 4 * UROWS, 256, dtype=BF16), shape(2, 2,...  2.24 us
    ppermute x3, waiting for transfers between devices, along_x(): lax.ppermute(sent, 'wav', [(i, (i + 2 * k) % NWAV) for i in range(NWAV)])  2.22 us
    ppermute x1, starting transfers between devices, body(): p3 = lax.ppermute(down, 'slab', along_z(3))  2.2 us
    ppermute x1, starting transfers between devices, body(): p1 = lax.ppermute(up, 'slab', along_z(1))  2.07 us
    ppermute x1, waiting for transfers between devices, body(): partner = lax.ppermute(more, 'slab', along_y((3, 2, 1, 0)))  2.04 us
    pallas_call x1, Pallas kernels, body(): call(detector_kernel, shape(256, 512), 0, 6, [pltpu.VMEM((WAVES, 16, 128)...  2.03 us
  transfers between devices with their start and end apart: 11, of which 7 were waited for; matrix products, arithmetic and copies ran while one was open for 0% of the time, Pallas kernels for 16%

profile of v7, /device:TPU:0, one launch (start us, length us, event | category | flops | bytes accessed | tf_op | source)
XLA Modules:
  0.0 36.0 jit_solution(12599870805851833613)
XLA Ops:
  0.0 0.0 copy-start
  0.0 1.5 %prepare_kernel.1 = (f32[80,128]{1,0:T(8,128)S(1)}, f32[120,128]{1,0:T(8,128)S(1)}, f32[120,128]{1,0:T(8,128)S(1)}, f32[8,128]{1,0:T(8,128)S(1)}) custom-call(f32[32,512]{1,0:T(8,128)} %amp_in.1, s32[32,512]{1,0:T(8,128)} %seg_in.1, s32[3,798]{1,0:T(4,128)} %bitcast.1, f32[64,1024]{1,0:T(8,128)} %mask.3, s32[8,16]{1,0:T(8,128)} %trow.1, s32[8,16]{1,0:T(8,128)} %tcol.1, ...), custom_call_target="tpu_custom_call" | custom-call | tf_op jit(solution)/shard_map/prepare_kernel/pallas_call | solution.py:514
  1.5 2.1 %collective-permute-start = (f32[120,128]{1,0:T(8,128)S(1)}, f32[120,128]{1,0:T(8,128)S(1)}, u32[]{:S(2)}, u32[]{:S(2)}) collective-permute-start(f32[120,128]{1,0:T(8,128)S(1)} %get-tuple-element.25), channel_id=1, source_target_pairs={{0,1},{1,2},{2,3},{3,0},{4,5},{5,6},{6,7},{7,4},{8,9},{9,10},{10,1... | collective-permute-start | bytes 184328 | tf_op jit(solution)/shard_map/ppermute | solution.py:536
  3.5 2.2 %collective-permute-start.2 = (f32[120,128]{1,0:T(8,128)S(1)}, f32[120,128]{1,0:T(8,128)S(1)}, u32[]{:S(2)}, u32[]{:S(2)}) collective-permute-start(f32[120,128]{1,0:T(8,128)S(1)} %get-tuple-element.26), channel_id=1, source_target_pairs={{0,3},{1,0},{2,1},{3,2},{4,7},{5,4},{6,5},{7,6},{8,11},{9,8},{10,9... | collective-permute-start | bytes 184328 | tf_op jit(solution)/shard_map/ppermute | solution.py:537
  5.7 1.8 %collective-permute-start.1 = (f32[80,128]{1,0:T(8,128)S(1)}, f32[80,128]{1,0:T(8,128)S(1)}, u32[]{:S(2)}, u32[]{:S(2)}) collective-permute-start(f32[80,128]{1,0:T(8,128)S(1)} %get-tuple-element.24.after.p0), channel_id=1, source_target_pairs={{0,2},{1,3},{2,0},{3,1},{4,6},{5,7},{6,4},{7,5},{8,10},{9,11},{10,... | collective-permute-start | bytes 122888 | tf_op jit(solution)/shard_map/ppermute | solution.py:538
  7.5 2.2 %table_kernel.1 = (bf16[2,4,320,256]{3,2,1,0:T(8,128)(2,1)S(1)}, bf16[2,2,2,256,512]{4,3,2,1,0:T(8,128)(2,1)S(1)}, bf16[128,768]{1,0:T(8,128)(2,1)S(1)}) custom-call(f32[80,128]{1,0:T(8,128)S(1)} %get-tuple-element.24.after.p0), custom_call_target="tpu_custom_call" | custom-call | tf_op jit(solution)/shard_map/table_kernel/pallas_call | solution.py:529
  9.8 1.5 %collective-permute-done.1.p2 = f32[80,128]{1,0:T(8,128)S(1)} collective-permute-done((f32[80,128]{1,0:T(8,128)S(1)}, f32[80,128]{1,0:T(8,128)S(1)}, u32[]{:S(2)}, u32[]{:S(2)}) %collective-permute-start.1) | collective-permute-done | bytes 40992 | tf_op jit(solution)/shard_map/ppermute | solution.py:538
  11.3 0.0 collective-permute-done.p1
  11.3 0.0 collective-permute-done.2.p3
  11.3 0.1 merge_kernel.1
  11.4 3.1 %collective-permute-start.5 = (f32[304,128]{1,0:T(8,128)S(1)}, f32[304,128]{1,0:T(8,128)S(1)}, u32[]{:S(2)}, u32[]{:S(2)}) collective-permute-start(f32[304,128]{1,0:T(8,128)S(1)} %get-tuple-element.30), channel_id=1, source_target_pairs={{0,12},{1,13},{2,14},{3,15},{4,8},{5,9},{6,10},{7,11},{8,4},{9,5},... | collective-permute-start | bytes 466952 | tf_op jit(solution)/shard_map/ppermute | solution.py:542
  14.5 0.1 collective-permute-start.4
  14.6 1.5 %collective-permute-start.3 = (f32[272,128]{1,0:T(8,128)S(1)}, f32[272,128]{1,0:T(8,128)S(1)}, u32[]{:S(2)}, u32[]{:S(2)}) collective-permute-start(f32[272,128]{1,0:T(8,128)S(1)} %get-tuple-element.28.ref), channel_id=1, source_target_pairs={{0,8},{1,9},{2,10},{3,11},{4,12},{5,13},{6,14},{7,15},{8,0},{9,1},... | collective-permute-start | bytes 417800 | tf_op jit(solution)/shard_map/ppermute | solution.py:544
  16.2 0.9 %own_kernel.1.after.before = f32[4,160,256]{2,1,0:T(8,128)S(1)} custom-call(f32[272,128]{1,0:T(8,128)S(1)} %get-tuple-element.28.ref, bf16[2,4,320,256]{3,2,1,0:T(8,128)(2,1)S(1)} %get-tuple-element.27.after.utab, bf16[128,768]{1,0:T(8,128)(2,1)S(1)} %get-tuple-element.29.spot), custom_call_target="tpu_custom_call" | custom-call | tf_op jit(solution)/shard_map/own_kernel/pallas_call | solution.py:546
  17.0 0.0 copy-done
  17.0 0.3 weight_kernel.1
  17.4 2.0 %collective-permute-done.5.ref.partner = f32[304,128]{1,0:T(8,128)S(1)} collective-permute-done((f32[304,128]{1,0:T(8,128)S(1)}, f32[304,128]{1,0:T(8,128)S(1)}, u32[]{:S(2)}, u32[]{:S(2)}) %collective-permute-start.5) | collective-permute-done | bytes 155680 | tf_op jit(solution)/shard_map/ppermute | solution.py:542
  19.4 0.9 %neighbour_kernel.2.before = f32[4,160,256]{2,1,0:T(8,128)S(1)} custom-call(f32[304,128]{1,0:T(8,128)S(1)} %collective-permute-done.5.ref.partner, bf16[2,4,320,256]{3,2,1,0:T(8,128)(2,1)S(1)} %get-tuple-element.27.after.utab, bf16[128,768]{1,0:T(8,128)(2,1)S(1)} %get-tuple-element.29.spot, f32[4,160,256]{2,1,0:T(8,128)S(1)} %own_kernel.1.after.before, ...), custom_call_target="tpu_custom_call" | custom-call | tf_op jit(solution)/shard_map/neighbour_kernel/pallas_call | solution.py:557
  20.3 0.0 collective-permute-done.4.ref.beside
  20.3 0.2 border_kernel.1
  20.4 0.9 %neighbour_kernel.3.before = f32[4,160,256]{2,1,0:T(8,128)S(1)} custom-call(f32[304,128]{1,0:T(8,128)S(1)} %collective-permute-done.4.ref.beside, bf16[2,4,320,256]{3,2,1,0:T(8,128)(2,1)S(1)} %get-tuple-element.27.after.utab, bf16[128,768]{1,0:T(8,128)(2,1)S(1)} %get-tuple-element.29.spot, f32[4,160,256]{2,1,0:T(8,128)S(1)} %neighbour_kernel.2.before, ...), custom_call_target="tpu_custom_call" | custom-call | tf_op jit(solution)/shard_map/neighbour_kernel/pallas_call | solution.py:557
  21.3 0.1 collective-permute-done.3.ref
  21.4 0.6 %last_kernel.2.border = f32[352,256]{1,0:T(8,128)S(1)} custom-call(f32[272,128]{1,0:T(8,128)S(1)} %collective-permute-done.3.ref, bf16[2,4,320,256]{3,2,1,0:T(8,128)(2,1)S(1)} %get-tuple-element.27.after.utab, bf16[128,768]{1,0:T(8,128)(2,1)S(1)} %get-tuple-element.29.spot, f32[4,160,256]{2,1,0:T(8,128)S(1)} %neighbour_kernel.3.before, ...), custom_call_target="tpu_custom_call" | custom-call | tf_op jit(solution)/shard_map/last_kernel/pallas_call | solution.py:561
  22.0 0.1 collective-permute-start.6
  22.1 0.6 %last_kernel.3.keep = f32[320,256]{1,0:T(8,128)S(1)} custom-call(f32[272,128]{1,0:T(8,128)S(1)} %collective-permute-done.3.ref, bf16[2,4,320,256]{3,2,1,0:T(8,128)(2,1)S(1)} %get-tuple-element.27.after.utab, bf16[128,768]{1,0:T(8,128)(2,1)S(1)} %get-tuple-element.29.spot, f32[4,160,256]{2,1,0:T(8,128)S(1)} %neighbour_kernel.3.before, ...), custom_call_target="tpu_custom_call" | custom-call | tf_op jit(solution)/shard_map/last_kernel/pallas_call | solution.py:564
  22.7 0.0 copy-start.1
  22.7 1.0 %collective-permute-done.6.got = f32[352,256]{1,0:T(8,128)S(1)} collective-permute-done((f32[352,256]{1,0:T(8,128)S(1)}, f32[352,256]{1,0:T(8,128)S(1)}, u32[]{:S(2)}, u32[]{:S(2)}) %collective-permute-start.6) | collective-permute-done | bytes 360480 | tf_op jit(solution)/shard_map/ppermute | solution.py:568
  23.8 0.9 %lens_kernel.1 = (f32[32,128]{1,0:T(8,128)S(1)}, f32[32,128]{1,0:T(8,128)S(1)}) custom-call(f32[320,256]{1,0:T(8,128)S(1)} %last_kernel.3.keep, f32[352,256]{1,0:T(8,128)S(1)} %collective-permute-done.6.got, bf16[2,2,2,256,512]{4,3,2,1,0:T(8,128)(2,1)S(1)} %get-tuple-element.34.vtab, f32[64,1024]{1,0:T(8,128)S(1)} %get-tuple-element.35.weight, ...), custom_call_target="tpu_custom_call" | custom-call | tf_op jit(solution)/shard_map/lens_kernel/pallas_call | solution.py:569
  24.6 0.2 collective-permute-start.7
  24.8 1.1 %collective-permute-done.7.got = f32[32,128]{1,0:T(8,128)S(1)} collective-permute-done((f32[32,128]{1,0:T(8,128)S(1)}, f32[32,128]{1,0:T(8,128)S(1)}, u32[]{:S(2)}, u32[]{:S(2)}) %collective-permute-start.7) | collective-permute-done | bytes 16416 | tf_op jit(solution)/shard_map/ppermute | solution.py:572
  25.9 0.1 pack_kernel.1
  26.0 1.6 %collective-permute-start.8 = (f32[16,128]{1,0:T(8,128)S(1)}, f32[16,128]{1,0:T(8,128)S(1)}, u32[]{:S(2)}, u32[]{:S(2)}) collective-permute-start(f32[16,128]{1,0:T(8,128)S(1)} %get-tuple-element.40), channel_id=1, source_target_pairs={{0,32},{16,48},{32,64},{48,80},{64,96},{80,112},{96,0},{112,16},{1... | collective-permute-start | bytes 24584 | tf_op jit(solution)/shard_map/ppermute | solution.py:574
  27.6 2.7 %collective-permute-start.9 = (f32[16,128]{1,0:T(8,128)S(1)}, f32[16,128]{1,0:T(8,128)S(1)}, u32[]{:S(2)}, u32[]{:S(2)}) collective-permute-start(f32[16,128]{1,0:T(8,128)S(1)} %get-tuple-element.41), channel_id=1, source_target_pairs={{0,64},{16,80},{32,96},{48,112},{64,0},{80,16},{96,32},{112,48},{1... | collective-permute-start | bytes 24584 | tf_op jit(solution)/shard_map/ppermute | solution.py:574
  30.3 1.4 %collective-permute-start.10 = (f32[16,128]{1,0:T(8,128)S(1)}, f32[16,128]{1,0:T(8,128)S(1)}, u32[]{:S(2)}, u32[]{:S(2)}) collective-permute-start(f32[16,128]{1,0:T(8,128)S(1)} %get-tuple-element.42), channel_id=1, source_target_pairs={{0,96},{16,112},{32,0},{48,16},{64,32},{80,48},{96,64},{112,80},{1... | collective-permute-start | bytes 24584 | tf_op jit(solution)/shard_map/ppermute | solution.py:574
  31.7 0.0 collective-permute-done.8.a1
  31.7 1.0 %collective-permute-done.9.a2 = f32[16,128]{1,0:T(8,128)S(1)} collective-permute-done((f32[16,128]{1,0:T(8,128)S(1)}, f32[16,128]{1,0:T(8,128)S(1)}, u32[]{:S(2)}, u32[]{:S(2)}) %collective-permute-start.9) | collective-permute-done | bytes 8224 | tf_op jit(solution)/shard_map/ppermute | solution.py:574
  32.7 1.2 %collective-permute-done.10.a3 = f32[16,128]{1,0:T(8,128)S(1)} collective-permute-done((f32[16,128]{1,0:T(8,128)S(1)}, f32[16,128]{1,0:T(8,128)S(1)}, u32[]{:S(2)}, u32[]{:S(2)}) %collective-permute-start.10) | collective-permute-done | bytes 8224 | tf_op jit(solution)/shard_map/ppermute | solution.py:574
  33.9 0.0 copy-done.1
  34.0 2.0 %detector_kernel.1 = f32[256,512]{1,0:T(8,128)} custom-call(f32[5,5]{1,0:T(8,128)S(1)} %copy-done.1, f32[16,128]{1,0:T(8,128)S(1)} %get-tuple-element.39.a0, f32[16,128]{1,0:T(8,128)S(1)} %collective-permute-done.8.a1, f32[16,128]{1,0:T(8,128)S(1)} %collective-permute-done.9.a2, f32[16,128]{1,0:T(8,128)S(1)} %collective-permute-done.10.a3, ...), custom_call_target="tpu_custom_call" | custom-call | tf_op jit(solution)/shard_map/detector_kernel/pallas_call | solution.py:578
Async XLA Ops:
  0.0 17.0 %copy-start = (f32[64,1024]{1,0:T(8,128)S(1)}, f32[64,1024]{1,0:T(8,128)}, u32[]{:S(2)}) copy-start(f32[64,1024]{1,0:T(8,128)} %mask.3) | copy-start | bytes 786436
  1.5 9.8 %collective-permute-start = (f32[120,128]{1,0:T(8,128)S(1)}, f32[120,128]{1,0:T(8,128)S(1)}, u32[]{:S(2)}, u32[]{:S(2)}) collective-permute-start(f32[120,128]{1,0:T(8,128)S(1)} %get-tuple-element.25), channel_id=1, source_target_pairs={{0,1},{1,2},{2,3},{3,0},{4,5},{5,6},{6,7},{7,4},{8,9},{9,10},{10,1... | collective-permute-start | bytes 184328 | tf_op jit(solution)/shard_map/ppermute | solution.py:536
  3.5 7.7 %collective-permute-start.2 = (f32[120,128]{1,0:T(8,128)S(1)}, f32[120,128]{1,0:T(8,128)S(1)}, u32[]{:S(2)}, u32[]{:S(2)}) collective-permute-start(f32[120,128]{1,0:T(8,128)S(1)} %get-tuple-element.26), channel_id=1, source_target_pairs={{0,3},{1,0},{2,1},{3,2},{4,7},{5,4},{6,5},{7,6},{8,11},{9,8},{10,9... | collective-permute-start | bytes 184328 | tf_op jit(solution)/shard_map/ppermute | solution.py:537
  5.7 5.5 %collective-permute-start.1 = (f32[80,128]{1,0:T(8,128)S(1)}, f32[80,128]{1,0:T(8,128)S(1)}, u32[]{:S(2)}, u32[]{:S(2)}) collective-permute-start(f32[80,128]{1,0:T(8,128)S(1)} %get-tuple-element.24.after.p0), channel_id=1, source_target_pairs={{0,2},{1,3},{2,0},{3,1},{4,6},{5,7},{6,4},{7,5},{8,10},{9,11},{10,... | collective-permute-start | bytes 122888 | tf_op jit(solution)/shard_map/ppermute | solution.py:538
  11.4 8.0 %collective-permute-start.5 = (f32[304,128]{1,0:T(8,128)S(1)}, f32[304,128]{1,0:T(8,128)S(1)}, u32[]{:S(2)}, u32[]{:S(2)}) collective-permute-start(f32[304,128]{1,0:T(8,128)S(1)} %get-tuple-element.30), channel_id=1, source_target_pairs={{0,12},{1,13},{2,14},{3,15},{4,8},{5,9},{6,10},{7,11},{8,4},{9,5},... | collective-permute-start | bytes 466952 | tf_op jit(solution)/shard_map/ppermute | solution.py:542
  14.5 5.8 %collective-permute-start.4 = (f32[304,128]{1,0:T(8,128)S(1)}, f32[304,128]{1,0:T(8,128)S(1)}, u32[]{:S(2)}, u32[]{:S(2)}) collective-permute-start(f32[304,128]{1,0:T(8,128)S(1)} %get-tuple-element.30), channel_id=1, source_target_pairs={{0,4},{1,5},{2,6},{3,7},{4,0},{5,1},{6,2},{7,3},{8,12},{9,13},{10,... | collective-permute-start | bytes 466952 | tf_op jit(solution)/shard_map/ppermute | solution.py:543
  14.6 6.8 %collective-permute-start.3 = (f32[272,128]{1,0:T(8,128)S(1)}, f32[272,128]{1,0:T(8,128)S(1)}, u32[]{:S(2)}, u32[]{:S(2)}) collective-permute-start(f32[272,128]{1,0:T(8,128)S(1)} %get-tuple-element.28.ref), channel_id=1, source_target_pairs={{0,8},{1,9},{2,10},{3,11},{4,12},{5,13},{6,14},{7,15},{8,0},{9,1},... | collective-permute-start | bytes 417800 | tf_op jit(solution)/shard_map/ppermute | solution.py:544
  22.0 1.8 %collective-permute-start.6 = (f32[352,256]{1,0:T(8,128)S(1)}, f32[352,256]{1,0:T(8,128)S(1)}, u32[]{:S(2)}, u32[]{:S(2)}) collective-permute-start(f32[352,256]{1,0:T(8,128)S(1)} %last_kernel.2.border), channel_id=1, source_target_pairs={{0,16},{16,0},{32,48},{48,32},{64,80},{80,64},{96,112},{112,96},{1... | collective-permute-start | bytes 1081352 | tf_op jit(solution)/shard_map/ppermute | solution.py:568
  22.7 11.2 %copy-start.1 = (f32[5,5]{1,0:T(8,128)S(1)}, f32[5,5]{1,0:T(8,128)}, u32[]{:S(2)}) copy-start(f32[5,5]{1,0:T(8,128)} %kernel.1) | copy-start | bytes 304
  24.6 1.3 %collective-permute-start.7 = (f32[32,128]{1,0:T(8,128)S(1)}, f32[32,128]{1,0:T(8,128)S(1)}, u32[]{:S(2)}, u32[]{:S(2)}) collective-permute-start(f32[32,128]{1,0:T(8,128)S(1)} %get-tuple-element.38), channel_id=1, source_target_pairs={{0,16},{16,0},{32,48},{48,32},{64,80},{80,64},{96,112},{112,96},{1... | collective-permute-start | bytes 49160 | tf_op jit(solution)/shard_map/ppermute | solution.py:572
  26.0 5.7 %collective-permute-start.8 = (f32[16,128]{1,0:T(8,128)S(1)}, f32[16,128]{1,0:T(8,128)S(1)}, u32[]{:S(2)}, u32[]{:S(2)}) collective-permute-start(f32[16,128]{1,0:T(8,128)S(1)} %get-tuple-element.40), channel_id=1, source_target_pairs={{0,32},{16,48},{32,64},{48,80},{64,96},{80,112},{96,0},{112,16},{1... | collective-permute-start | bytes 24584 | tf_op jit(solution)/shard_map/ppermute | solution.py:574
  27.6 5.2 %collective-permute-start.9 = (f32[16,128]{1,0:T(8,128)S(1)}, f32[16,128]{1,0:T(8,128)S(1)}, u32[]{:S(2)}, u32[]{:S(2)}) collective-permute-start(f32[16,128]{1,0:T(8,128)S(1)} %get-tuple-element.41), channel_id=1, source_target_pairs={{0,64},{16,80},{32,96},{48,112},{64,0},{80,16},{96,32},{112,48},{1... | collective-permute-start | bytes 24584 | tf_op jit(solution)/shard_map/ppermute | solution.py:574
  30.3 3.7 %collective-permute-start.10 = (f32[16,128]{1,0:T(8,128)S(1)}, f32[16,128]{1,0:T(8,128)S(1)}, u32[]{:S(2)}, u32[]{:S(2)}) collective-permute-start(f32[16,128]{1,0:T(8,128)S(1)} %get-tuple-element.42), channel_id=1, source_target_pairs={{0,96},{16,112},{32,0},{48,16},{64,32},{80,48},{96,64},{112,80},{1... | collective-permute-start | bytes 24584 | tf_op jit(solution)/shard_map/ppermute | solution.py:574
